TPU v7x, 32 devices: a whole 2x2x4 slice. The times are simulated.
32 devices in a mesh: row: 8 (over y, x, core), col: 4 (over z).
Axes of the slice: x: 2, y: 2, z: 4, core: 2. Of those that a mesh axis runs over, the one named last changes fastest.
Arguments:
- out_grad: bfloat16 [512, 16384], P('col', 'row'), may hold values from -6 to 6
- gate_saved: bfloat16 [512, 26624], P('row', 'col'), may hold values from -8 to 8
- up_saved: bfloat16 [512, 26624], P('row', 'col'), may hold values from -6 to 6
- gate_weight: bfloat16 [16384, 26624], P('row', 'col'), may hold values from -0.046875 to 0.046875
- up_weight: bfloat16 [16384, 26624], P('row', 'col'), may hold values from -0.046875 to 0.046875
- down_weight: bfloat16 [26624, 16384], P('col', 'row'), may hold values from -0.0390625 to 0.0390625
Outputs:
- input_grad: bfloat16 [512, 16384], P('col', 'row')
All inputs are finite; a program needn't handle non-finite values.
Results may differ from a plain program's by a relative error of at most 0.0049.
Values may be sent and summed in bfloat16 or wider, within the bound.
No kernel may reach another device: no remote copies, remote signals or barrier semaphores. Data moves between devices by JAX's collectives and lax.ppermute only.
A program may use at most 192 MiB of HBM per device.

v0:
```python
import jax
import jax.numpy as jnp
from jax import lax
from jax.sharding import PartitionSpec as P


def contract_last(left, right):
    return lax.dot_general(
        left, right, (((1,), (1,)), ((), ())), preferred_element_type=jnp.float32
    )


def swiglu_back(hidden_grad, gate_saved, up_saved):
    gate_float = gate_saved.astype(jnp.float32)
    up_float = up_saved.astype(jnp.float32)
    sigmoid_gate = jax.nn.sigmoid(gate_float)
    up_grad = (hidden_grad * gate_float * sigmoid_gate).astype(jnp.bfloat16)
    gate_grad = (
        hidden_grad * up_float * sigmoid_gate * (1.0 + gate_float * (1.0 - sigmoid_gate))
    ).astype(jnp.bfloat16)
    return (gate_grad, up_grad)


def per_device(out_grad, gate_saved, up_saved, gate_weight, up_weight, down_weight):
    partial_hidden = contract_last(lax.all_gather(out_grad, "col", axis=0, tiled=True), down_weight)
    hidden_grad = lax.psum_scatter(partial_hidden, "row", scatter_dimension=0, tiled=True)
    gate_grad, up_grad = swiglu_back(hidden_grad, gate_saved, up_saved)
    block_pair = lax.all_gather((gate_grad, up_grad), "row", axis=0, tiled=True)
    partial_input = contract_last(block_pair[0], gate_weight) + contract_last(
        block_pair[1], up_weight
    )
    return lax.psum_scatter(partial_input, "col", scatter_dimension=0, tiled=True).astype(
        jnp.bfloat16
    )


def solution(mesh):
    placed = (
        P("col", "row"),
        P("row", "col"),
        P("row", "col"),
        P("row", "col"),
        P("row", "col"),
        P("col", "row"),
    )
    return jax.shard_map(
        per_device, mesh=mesh, in_specs=placed, out_specs=P("col", "row"), check_vma=False
    )
```

profile of v0, /device:TPU:0, one launch (start us, length us, event | category | flops | bytes accessed | tf_op | source)
XLA Modules:
  0.0 383.6 jit_solution(7440917550633901060)
XLA Ops:
  6.5 0.0 all-gather.4.cloned.1.call-start
  6.5 0.7 all-gather.4.cloned.1.call-update
  7.3 0.0 reduce-scatter.3.cloned.1.call-start
  7.3 50.3 %all-gather.4.cloned.1.call-done = bf16[512,2048]{1,0:T(8,128)(2,1)} async-done(((bf16[128,2048]{1,0:T(8,128)(2,1)}), bf16[512,2048]{1,0:T(8,128)(2,1)}) %all-gather.4.cloned.1.call-update) | async-done | bytes 2097168 | tf_op jit(solution)/shard_map/all_gather | solution.py:25
  57.6 21.6 %fusion.8 = f32[512,6656]{1,0:T(8,128)} fusion(bf16[512,2048]{1,0:T(8,128)(2,1)} %all-gather.4.cloned.1.call-done, bf16[6656,2048]{1,0:T(8,128)(2,1)} %param.11), kind=kOutput, calls=%fused_computation.12 | convolution fusion | flops 13958643712 | bytes 42991616 | tf_op jit(solution)/shard_map/dot_general | solution.py:8
  79.2 0.0 copy-start
  79.2 0.0 copy-start.1
  79.2 0.0 reduce-scatter.3.cloned.1.call-update
  79.2 0.0 all-gather.6.cloned.1.call-start
  79.2 96.8 %reduce-scatter.3.cloned.1.call-done = f32[64,6656]{1,0:T(8,128)} async-done(((f32[512,6656]{1,0:T(8,128)}), f32[64,6656]{1,0:T(8,128)}) %reduce-scatter.3.cloned.1.call-update) | async-done | bytes 1703952 | tf_op jit(solution)/shard_map/reduce_scatter | solution.py:26
  176.1 0.0 copy-done
  176.1 0.0 copy-done.1
  176.1 3.5 fusion.7
  179.5 0.0 all-gather.6.cloned.1.call-update
  179.6 0.0 all-gather.8.cloned.1.call-start
  179.6 0.5 all-gather.8.cloned.1.call-update
  180.1 0.0 reduce-scatter.5.cloned.1.call-start
  180.2 47.2 %all-gather.6.cloned.1.call-done = bf16[512,6656]{1,0:T(8,128)(2,1)} async-done(((bf16[64,6656]{1,0:T(8,128)(2,1)}), bf16[512,6656]{1,0:T(8,128)(2,1)}) %all-gather.6.cloned.1.call-update) | async-done | bytes 6815760 | tf_op jit(solution)/shard_map/all_gather | solution.py:28
  227.4 21.6 %fusion.9 = f32[512,2048]{1,0:T(8,128)} fusion(bf16[512,6656]{1,0:T(8,128)(2,1)} %all-gather.6.cloned.1.call-done, bf16[2048,6656]{1,0:T(8,128)(2,1)} %param.9), kind=kOutput, calls=%fused_computation.13 | convolution fusion | flops 13958643712 | bytes 38273024 | tf_op jit(solution)/shard_map/dot_general | solution.py:8
  249.0 27.9 %all-gather.8.cloned.1.call-done = bf16[512,6656]{1,0:T(8,128)(2,1)} async-done(((bf16[64,6656]{1,0:T(8,128)(2,1)}), bf16[512,6656]{1,0:T(8,128)(2,1)}) %all-gather.8.cloned.1.call-update) | async-done | bytes 6815760 | tf_op jit(solution)/shard_map/all_gather | solution.py:28
  276.9 21.1 %convolution_add_fusion = f32[512,2048]{1,0:T(8,128)} fusion(f32[512,2048]{1,0:T(8,128)} %fusion.9, bf16[512,6656]{1,0:T(8,128)(2,1)} %all-gather.8.cloned.1.call-done, bf16[2048,6656]{1,0:T(8,128)(2,1)} %param.10), kind=kOutput, calls=%fused_computation | convolution fusion | flops 13959692288 | bytes 42467328 | tf_op jit(solution)/shard_map/dot_general | solution.py:8
  298.0 0.0 reduce-scatter.5.cloned.1.call-update
  298.0 76.9 %reduce-scatter.5.cloned.1.call-done = f32[128,2048]{1,0:T(8,128)} async-done(((f32[512,2048]{1,0:T(8,128)}), f32[128,2048]{1,0:T(8,128)}) %reduce-scatter.5.cloned.1.call-update) | async-done | bytes 1048592 | tf_op jit(solution)/shard_map/reduce_scatter | solution.py:32
  375.0 2.1 convert_element_type.19
Async XLA Ops:
  6.5 51.1 %all-gather.4.cloned.1.call-start = ((), (), s32[]{:S(2)}) async-start(), calls=%async_computation.2 | async-start | bytes 2621440 | tf_op jit(solution)/shard_map/all_gather | solution.py:25
  7.3 168.8 %reduce-scatter.3.cloned.1.call-start = ((), (), s32[]{:S(2)}) async-start(), calls=%async_computation.3 | async-start | bytes 15335424 | tf_op jit(solution)/shard_map/reduce_scatter | solution.py:26
  79.2 96.9 %copy-start = (bf16[64,6656]{1,0:T(8,128)(2,1)S(1)}, bf16[64,6656]{1,0:T(8,128)(2,1)}, u32[]{:S(2)}) copy-start(bf16[64,6656]{1,0:T(8,128)(2,1)} %param.7) | copy-start | bytes 2555908
  79.2 96.9 %copy-start.1 = (bf16[64,6656]{1,0:T(8,128)(2,1)S(1)}, bf16[64,6656]{1,0:T(8,128)(2,1)}, u32[]{:S(2)}) copy-start(bf16[64,6656]{1,0:T(8,128)(2,1)} %param.8) | copy-start | bytes 2555908
  79.2 148.2 %all-gather.6.cloned.1.call-start = ((), (), s32[]{:S(2)}) async-start(), calls=%async_computation.4 | async-start | bytes 7667712 | tf_op jit(solution)/shard_map/all_gather | solution.py:28
  179.6 97.4 %all-gather.8.cloned.1.call-start = ((), (), s32[]{:S(2)}) async-start(), calls=%async_computation.5 | async-start | bytes 7667712 | tf_op jit(solution)/shard_map/all_gather | solution.py:28
  180.1 194.8 %reduce-scatter.5.cloned.1.call-start = ((), (), s32[]{:S(2)}) async-start(), calls=%async_computation.6 | async-start | bytes 5242880 | tf_op jit(solution)/shard_map/reduce_scatter | solution.py:32
Sparse Core Ops, SparseCore 0:
  8.9 48.6 all-gather.3
  79.3 96.7 reduce-scatter.2
  179.7 47.6 all-gather.5
  229.2 47.7 all-gather.7
  298.2 76.7 reduce-scatter.4
where the time goes:
time: 384 us
  waiting for transfers between devices  300 us (78%)
  matrix products  64.2 us (17%)
  between operations  13.1 us (3%)
  other arithmetic  5.56 us (1%)
    reduce_scatter x1, waiting for transfers between devices, per_device(): lax.psum_scatter(partial_hidden, 'row', scatter_dimension=0, tiled=True)  96.8 us
    reduce_scatter x1, waiting for transfers between devices, per_device(): lax.psum_scatter(partial_input, 'col', scatter_dimension=0, tiled=True)  76.9 us
    all_gather x2, waiting for transfers between devices, per_device(): block_pair = lax.all_gather((gate_grad, up_grad), 'row', axis=0, tiled=True)  75.2 us
    dot_general x3, matrix products, contract_last(): lax.dot_general(left, right, (((1,), (1,)), ((), ())), preferred_element_...  64.2 us
    all_gather x1, waiting for transfers between devices, per_device(): lax.all_gather(out_grad, 'col', axis=0, tiled=True)  50.3 us
  transfers between devices with their start and end apart: 5, of which 5 were waited for; matrix products, arithmetic and copies ran while one was open for 6% of the time, Pallas kernels for 0%

commit v1 on v0

v1 whole, which is shorter than its diff:
```python
import jax
import jax.numpy as jnp
from jax import lax
from jax.sharding import PartitionSpec as P

TOKEN_CHUNKS = 2
HIDDEN_CHUNKS = 1


def contract_last(left, right):
    return lax.dot_general(
        left, right, (((1,), (1,)), ((), ())), preferred_element_type=jnp.float32
    )


def swiglu_back(hidden_grad, gate_saved, up_saved):
    gate_float = gate_saved.astype(jnp.float32)
    up_float = up_saved.astype(jnp.float32)
    sigmoid_gate = jax.nn.sigmoid(gate_float)
    up_grad = (hidden_grad * gate_float * sigmoid_gate).astype(jnp.bfloat16)
    gate_grad = (
        hidden_grad * up_float * sigmoid_gate * (1.0 + gate_float * (1.0 - sigmoid_gate))
    ).astype(jnp.bfloat16)
    return (gate_grad, up_grad)


def swap(value, axis, size, bit):
    return lax.ppermute(value, axis, [(i, i ^ bit) for i in range(size)])


def turn(value, axis, size, distance):
    return lax.ppermute(value, axis, [(i, (i + distance) % size) for i in range(size)])


def halve(blocks, rows, bits):
    state = dict(enumerate(blocks))
    for bit in bits:
        sent = [k for k in sorted(state) if k & bit]
        got = swap(
            jnp.stack([state[k] for k in sent]).astype(jnp.bfloat16), "row", rows, 2 * bit
        )
        for j, k in enumerate(sent):
            state[k ^ bit] = state[k ^ bit] + got[j].astype(jnp.float32)
            del state[k]
    return state[0]


def double(block, rows, bits):
    parts = [(block[None], [0])]
    for bit in bits:
        whole = parts[0][0] if len(parts) == 1 else jnp.concatenate([p for p, _ in parts])
        order = [k for _, ks in parts for k in ks]
        parts.append((swap(whole, "row", rows, 2 * bit), [k ^ bit for k in order]))
    placed = {k: p[j] for p, ks in parts for j, k in enumerate(ks)}
    return jnp.concatenate([placed[k] for k in sorted(placed)])


def per_device(rows, cols, out_grad, gate_saved, up_saved, gate_weight, up_weight, down_weight):
    me, plane = lax.axis_index("row"), lax.axis_index("col")
    share, hidden = gate_saved.shape
    width = out_grad.shape[1]
    per_plane = rows // cols
    step = share // TOKEN_CHUNKS
    depth = hidden // HIDDEN_CHUNKS
    half = rows // 2
    bits = [1 << i for i in range(half.bit_length() - 1)]
    order = [s for s in range(rows) if s & 1] + [s for s in range(rows) if not s & 1]
    back = [s for s in range(rows) if not s & 1] + [s for s in range(rows) if s & 1]

    results = []
    for t in range(TOKEN_CHUNKS):
        own = out_grad.reshape(per_plane, TOKEN_CHUNKS, step, width)[:, t]
        pieces = jnp.concatenate([own] + [turn(own, "col", cols, d) for d in range(1, cols)])
        picked = []
        for s in order:
            block = me ^ s
            far = lax.rem(plane - block // per_plane + cols, cols)
            picked.append(
                lax.dynamic_index_in_dim(
                    pieces, far * per_plane + lax.rem(block, per_plane), 0, keepdims=False
                )
            )
        tokens = jnp.concatenate(picked)
        total = None
        for h in range(HIDDEN_CHUNKS):
            span = slice(h * depth, (h + 1) * depth)
            partial = contract_last(tokens, down_weight[span]).astype(jnp.bfloat16)
            partial = partial.reshape(rows, step, depth)
            got = swap(partial[:half], "row", rows, 1)
            pair = partial[half:].astype(jnp.float32) + got.astype(jnp.float32)
            mid = depth // 2
            left = halve(list(pair[:, :, :mid]), rows, bits)
            right = halve(list(pair[:, :, mid:]), rows, bits[::-1])
            hidden_grad = jnp.concatenate([left, right], axis=1)
            mine = slice(t * step, (t + 1) * step)
            gate_grad, up_grad = swiglu_back(
                hidden_grad, gate_saved[mine, span], up_saved[mine, span]
            )
            gates = double(gate_grad, rows, bits)
            ups = double(up_grad, rows, bits[::-1])
            gates = jnp.concatenate([gates, swap(gates, "row", rows, 1)])
            ups = jnp.concatenate([ups, swap(ups, "row", rows, 1)])
            product = contract_last(gates, gate_weight[:, span]) + contract_last(
                ups, up_weight[:, span]
            )
            total = product if total is None else total + product
        total = total.reshape(rows, step, width)

        def owned_by(to):
            picked = []
            for sub in range(per_plane):
                s = me ^ (to * per_plane + sub)
                place = lax.rem(s, 2) * half + s // 2
                picked.append(lax.dynamic_index_in_dim(total, place, 0, keepdims=False))
            return jnp.stack(picked)

        result = owned_by(plane)
        for d in range(1, cols):
            sent = owned_by(lax.rem(plane + d, cols)).astype(jnp.bfloat16)
            result = result + turn(sent, "col", cols, d).astype(jnp.float32)
        results.append(result.astype(jnp.bfloat16))
    return jnp.stack(results, axis=1).reshape(out_grad.shape)


def solution(mesh):
    rows, cols = mesh.shape["row"], mesh.shape["col"]
    placed = (
        P("col", "row"),
        P("row", "col"),
        P("row", "col"),
        P("row", "col"),
        P("row", "col"),
        P("col", "row"),
    )

    def body(*arrays):
        return per_device(rows, cols, *arrays)

    return jax.shard_map(
        body, mesh=mesh, in_specs=placed, out_specs=P("col", "row"), check_vma=False
    )
```

time: 384 us -> 297 us (0.77)
  waiting for transfers between devices: 300 us -> 119 us
  starting transfers between devices: 0.16 us -> 45.1 us
  local copies, waits for them, and re-layouts: 0.01 us -> 35.2 us
  matrix products: 64.2 us -> 86.7 us
  between operations: 13.1 us -> 0.41 us
  other arithmetic: 5.56 us -> 10.5 us
    reduce_scatter x2 -> x0, waiting for transfers between devices: 174 us -> none  [the longest x1 96.8 us: per_device(): lax.psum_scatter(partial_hidden, 'row', scatter_dimension=0, tiled=True)]
    all_gather x3 -> x0, waiting for transfers between devices: 125 us -> none  [the longest x2 75.2 us: per_device(): block_pair = lax.all_gather((gate_grad, up_grad), 'row', axis=0, tiled=True)]
    ppermute x0 -> x34, waiting for transfers between devices: none -> 119 us  [the longest x22 71.1 us: swap(): return lax.ppermute(value, axis, [(i, i ^ bit) for i in range(size)])]
    ppermute x0 -> x34, starting transfers between devices: none -> 45.1 us  [the longest x12 28.2 us: turn(): lax.ppermute(value, axis, [(i, (i + distance) % size) for i in range(size)])]
    dot_general x3 -> x6, matrix products: 64.2 us -> 86.7 us  [contract_last(): lax.dot_general(left, right, (((1,), (1,)), ((), ())), preferred_element_...]
    unnamed x4 -> x29, local copies, waits for them, and re-layouts: 0.01 us -> 14.4 us
    concatenate x0 -> x6, local copies, waits for them, and re-layouts: none -> 10.3 us  [the longest x2 5.55 us: per_device(): gates = jnp.concatenate([gates, swap(gates, 'row', rows, 1)])]
    slice x0 -> x2, local copies, waits for them, and re-layouts: none -> 5.59 us  [per_device(): got = swap(partial[:half], 'row', rows, 1)]
  transfers between devices with their start and end apart: 5 -> 34, of which waited for: 5 -> 18; matrix products, arithmetic and copies ran while one was open for 6% -> 37% of each run, Pallas kernels for 0% -> 0%
where the time goes in v1:
time: 297 us
  waiting for transfers between devices  119 us (40%)
  matrix products  86.7 us (29%)
  starting transfers between devices  45.1 us (15%)
  local copies, waits for them, and re-layouts  35.2 us (12%)
  other arithmetic  10.5 us (4%)
    dot_general x6, matrix products, contract_last(): lax.dot_general(left, right, (((1,), (1,)), ((), ())), preferred_element_...  86.7 us
    ppermute x22, waiting for transfers between devices, swap(): return lax.ppermute(value, axis, [(i, i ^ bit) for i in range(size)])  71.1 us
    ppermute x12, waiting for transfers between devices, turn(): lax.ppermute(value, axis, [(i, (i + distance) % size) for i in range(size)])  48.1 us
    ppermute x12, starting transfers between devices, turn(): lax.ppermute(value, axis, [(i, (i + distance) % size) for i in range(size)])  28.2 us
    ppermute x22, starting transfers between devices, swap(): return lax.ppermute(value, axis, [(i, i ^ bit) for i in range(size)])  16.9 us
    unnamed x29, local copies, waits for them, and re-layouts  14.4 us
  transfers between devices with their start and end apart: 34, of which 18 were waited for; matrix products, arithmetic and copies ran while one was open for 37% of the time, Pallas kernels for 0%

profile of v1, /device:TPU:0, one launch (start us, length us, event | category | flops | bytes accessed | tf_op | source)
XLA Modules:
  0.0 297.1 jit_solution(9786320336118413839)
XLA Ops:
  1.1 5.1 %collective-permute-start.19 = (bf16[2,32,2048]{2,1,0:T(8,128)(2,1)S(1)}, bf16[2,32,2048]{2,1,0:T(8,128)(2,1)S(1)}, u32[]{:S(2)}, u32[]{:S(2)}) collective-permute-start(bf16[2,32,2048]{2,1,0:T(8,128)(2,1)S(1)} %get-tuple-element.64), channel_id=1, source_target_pairs={{0,3},{1,0},{2,1},{3,2},{4,7},{5,4},{6,5},{7,6},{8,11},{9,8},{10,9... | collective-permute-start | bytes 786440 | tf_op jit(solution)/shard_map/ppermute | solution.py:32
  7.2 2.8 collective-permute-start.2
  12.9 10.6 %collective-permute-start = (bf16[2,32,2048]{2,1,0:T(8,128)(2,1)S(1)}, bf16[2,32,2048]{2,1,0:T(8,128)(2,1)S(1)}, u32[]{:S(2)}, u32[]{:S(2)}) collective-permute-start(bf16[2,32,2048]{2,1,0:T(8,128)(2,1)S(1)} %get-tuple-element.63), channel_id=1, source_target_pairs={{0,1},{1,2},{2,3},{3,0},{4,5},{5,6},{6,7},{7,4},{8,9},{9,10},{10,1... | collective-permute-start | bytes 786440 | tf_op jit(solution)/shard_map/ppermute | solution.py:32
  23.5 7.3 %collective-permute-done.18 = bf16[2,32,2048]{2,1,0:T(8,128)(2,1)S(1)} collective-permute-done((bf16[2,32,2048]{2,1,0:T(8,128)(2,1)S(1)}, bf16[2,32,2048]{2,1,0:T(8,128)(2,1)S(1)}, u32[]{:S(2)}, u32[]{:S(2)}) %collective-permute-start.18) | collective-permute-done | bytes 262176 | tf_op jit(solution)/shard_map/ppermute | solution.py:32
  30.9 20.0 %collective-permute-done.1 = bf16[2,32,2048]{2,1,0:T(8,128)(2,1)S(1)} collective-permute-done((bf16[2,32,2048]{2,1,0:T(8,128)(2,1)S(1)}, bf16[2,32,2048]{2,1,0:T(8,128)(2,1)S(1)}, u32[]{:S(2)}, u32[]{:S(2)}) %collective-permute-start.1) | collective-permute-done | bytes 262176 | tf_op jit(solution)/shard_map/ppermute | solution.py:32
  51.9 13.7 %convolution_convert_fusion.1 = bf16[256,6656]{1,0:T(8,128)(2,1)} fusion(bf16[256,2048]{1,0:T(8,128)(2,1)S(1)} %bitcast_dynamic-update-slice_fusion.8, bf16[6656,2048]{1,0:T(8,128)(2,1)} %param.11), kind=kOutput, calls=%fused_computation.1 | convolution fusion | flops 6981025792 | bytes 31719424 | tf_op jit(solution)/shard_map/dot_general | solution.py:11
  65.6 3.4 %fusion.42 = (bf16[128,6656]{1,0:T(8,128)(2,1)}, bf16[128,6656]{1,0:T(8,128)(2,1)S(1)}) fusion(bf16[256,6656]{1,0:T(8,128)(2,1)} %convolution_convert_fusion.1), kind=kLoop, calls=%fused_computation.143 | loop fusion | bytes 6815744 | tf_op jit(solution)/shard_map/slice | solution.py:89
  73.7 14.0 %convolution_convert_fusion = bf16[256,6656]{1,0:T(8,128)(2,1)} fusion(bf16[256,2048]{1,0:T(8,128)(2,1)} %bitcast_dynamic-update-slice_fusion, bf16[6656,2048]{1,0:T(8,128)(2,1)} %param.11), kind=kOutput, calls=%fused_computation | convolution fusion | flops 6981025792 | bytes 31719424 | tf_op jit(solution)/shard_map/dot_general | solution.py:11
  98.6 8.5 %collective-permute-done.4 = bf16[2,32,3328]{2,1,0:T(8,128)(2,1)S(1)} collective-permute-done((bf16[2,32,3328]{2,1,0:T(8,128)(2,1)S(1)}, bf16[2,32,3328]{2,1,0:T(8,128)(2,1)S(1)}, u32[]{:S(2)}, u32[]{:S(2)}) %collective-permute-start.4) | collective-permute-done | bytes 426016 | tf_op jit(solution)/shard_map/ppermute | solution.py:28
  110.8 5.4 %collective-permute-done.21 = bf16[2,32,3328]{2,1,0:T(8,128)(2,1)S(1)} collective-permute-done((bf16[2,32,3328]{2,1,0:T(8,128)(2,1)S(1)}, bf16[2,32,3328]{2,1,0:T(8,128)(2,1)S(1)}, u32[]{:S(2)}, u32[]{:S(2)}) %collective-permute-start.21) | collective-permute-done | bytes 426016 | tf_op jit(solution)/shard_map/ppermute | solution.py:28
  122.4 3.6 %collective-permute-done.22 = bf16[1,32,3328]{2,1,0:T(8,128)(2,1)S(1)} collective-permute-done((bf16[1,32,3328]{2,1,0:T(8,128)(2,1)S(1)}, bf16[1,32,3328]{2,1,0:T(8,128)(2,1)S(1)}, u32[]{:S(2)}, u32[]{:S(2)}) %collective-permute-start.22) | collective-permute-done | bytes 213024 | tf_op jit(solution)/shard_map/ppermute | solution.py:28
  132.1 8.7 %collective-permute-done.28 = bf16[1,32,6656]{2,1,0:T(8,128)(2,1)S(1)} collective-permute-done((bf16[1,32,6656]{2,1,0:T(8,128)(2,1)S(1)}, bf16[1,32,6656]{2,1,0:T(8,128)(2,1)S(1)}, u32[]{:S(2)}, u32[]{:S(2)}) %collective-permute-start.28) | collective-permute-done | bytes 426016 | tf_op jit(solution)/shard_map/ppermute | solution.py:28
  143.2 6.8 %collective-permute-done.11 = bf16[1,32,6656]{2,1,0:T(8,128)(2,1)S(1)} collective-permute-done((bf16[1,32,6656]{2,1,0:T(8,128)(2,1)S(1)}, bf16[1,32,6656]{2,1,0:T(8,128)(2,1)S(1)}, u32[]{:S(2)}, u32[]{:S(2)}) %collective-permute-start.11) | collective-permute-done | bytes 426016 | tf_op jit(solution)/shard_map/ppermute | solution.py:28
  154.0 15.8 %collective-permute-done.29 = bf16[2,32,6656]{2,1,0:T(8,128)(2,1)S(1)} collective-permute-done((bf16[2,32,6656]{2,1,0:T(8,128)(2,1)S(1)}, bf16[2,32,6656]{2,1,0:T(8,128)(2,1)S(1)}, u32[]{:S(2)}, u32[]{:S(2)}) %collective-permute-start.29) | collective-permute-done | bytes 852000 | tf_op jit(solution)/shard_map/ppermute | solution.py:28
  171.9 14.1 %collective-permute-done.12 = bf16[2,32,6656]{2,1,0:T(8,128)(2,1)S(1)} collective-permute-done((bf16[2,32,6656]{2,1,0:T(8,128)(2,1)S(1)}, bf16[2,32,6656]{2,1,0:T(8,128)(2,1)S(1)}, u32[]{:S(2)}, u32[]{:S(2)}) %collective-permute-start.12) | collective-permute-done | bytes 852000 | tf_op jit(solution)/shard_map/ppermute | solution.py:28
  197.4 14.5 %fusion.47 = f32[256,2048]{1,0:T(8,128)} fusion(bf16[256,6656]{1,0:T(8,128)(2,1)} %constant_dynamic-update-slice_fusion.15, bf16[2048,6656]{1,0:T(8,128)(2,1)} %param.10), kind=kOutput, calls=%fused_computation.148 | convolution fusion | flops 6979321856 | bytes 32768000 | tf_op jit(solution)/shard_map/dot_general | solution.py:11
  211.9 2.8 constant_dynamic-update-slice_fusion.10
  214.7 15.7 %convolution_add_fusion = f32[256,2048]{1,0:T(8,128)} fusion(f32[256,2048]{1,0:T(8,128)} %fusion.47, bf16[256,6656]{1,0:T(8,128)(2,1)} %constant_dynamic-update-slice_fusion.10, bf16[2048,6656]{1,0:T(8,128)(2,1)} %param.9), kind=kOutput, calls=%fused_computation.4 | convolution fusion | flops 6979846144 | bytes 34865152 | tf_op jit(solution)/shard_map/dot_general | solution.py:11
  231.9 2.9 collective-permute-start.32
  240.3 14.5 %fusion.46 = f32[256,2048]{1,0:T(8,128)} fusion(bf16[256,6656]{1,0:T(8,128)(2,1)} %constant_dynamic-update-slice_fusion.5, bf16[2048,6656]{1,0:T(8,128)(2,1)} %param.10), kind=kOutput, calls=%fused_computation.147 | convolution fusion | flops 6979321856 | bytes 32768000 | tf_op jit(solution)/shard_map/dot_general | solution.py:11
  254.8 2.8 constant_dynamic-update-slice_fusion
  257.6 14.3 %convolution_add_fusion.1 = f32[256,2048]{1,0:T(8,128)S(1)} fusion(f32[256,2048]{1,0:T(8,128)} %fusion.46, bf16[256,6656]{1,0:T(8,128)(2,1)} %constant_dynamic-update-slice_fusion, bf16[2048,6656]{1,0:T(8,128)(2,1)} %param.9), kind=kOutput, calls=%fused_computation.5 | convolution fusion | flops 6979846144 | bytes 34865152 | tf_op jit(solution)/shard_map/dot_general | solution.py:11
  277.1 3.7 %collective-permute-done.16 = bf16[2,32,2048]{2,1,0:T(8,128)(2,1)S(1)} collective-permute-done((bf16[2,32,2048]{2,1,0:T(8,128)(2,1)S(1)}, bf16[2,32,2048]{2,1,0:T(8,128)(2,1)S(1)}, u32[]{:S(2)}, u32[]{:S(2)}) %collective-permute-start.16) | collective-permute-done | bytes 262176 | tf_op jit(solution)/shard_map/ppermute | solution.py:32
  280.8 15.3 %collective-permute-done.15 = bf16[2,32,2048]{2,1,0:T(8,128)(2,1)S(1)} collective-permute-done((bf16[2,32,2048]{2,1,0:T(8,128)(2,1)S(1)}, bf16[2,32,2048]{2,1,0:T(8,128)(2,1)S(1)}, u32[]{:S(2)}, u32[]{:S(2)}) %collective-permute-start.15) | collective-permute-done | bytes 262176 | tf_op jit(solution)/shard_map/ppermute | solution.py:32
  (129 shorter events, 70.6 us)
Async XLA Ops:
  6.2 24.6 %collective-permute-start.18 = (bf16[2,32,2048]{2,1,0:T(8,128)(2,1)S(1)}, bf16[2,32,2048]{2,1,0:T(8,128)(2,1)S(1)}, u32[]{:S(2)}, u32[]{:S(2)}) collective-permute-start(bf16[2,32,2048]{2,1,0:T(8,128)(2,1)S(1)} %get-tuple-element.64), channel_id=1, source_target_pairs={{0,2},{1,3},{2,0},{3,1},{4,6},{5,7},{6,4},{7,5},{8,10},{9,11},{10,... | collective-permute-start | bytes 786440 | tf_op jit(solution)/shard_map/ppermute | solution.py:32
  6.2 24.6 %collective-permute-start.17 = (bf16[2,32,2048]{2,1,0:T(8,128)(2,1)S(1)}, bf16[2,32,2048]{2,1,0:T(8,128)(2,1)S(1)}, u32[]{:S(2)}, u32[]{:S(2)}) collective-permute-start(bf16[2,32,2048]{2,1,0:T(8,128)(2,1)S(1)} %get-tuple-element.64), channel_id=1, source_target_pairs={{0,1},{1,2},{2,3},{3,0},{4,5},{5,6},{6,7},{7,4},{8,9},{9,10},{10,1... | collective-permute-start | bytes 786440 | tf_op jit(solution)/shard_map/ppermute | solution.py:32
  7.2 23.7 %collective-permute-start.2 = (bf16[2,32,2048]{2,1,0:T(8,128)(2,1)S(1)}, bf16[2,32,2048]{2,1,0:T(8,128)(2,1)S(1)}, u32[]{:S(2)}, u32[]{:S(2)}) collective-permute-start(bf16[2,32,2048]{2,1,0:T(8,128)(2,1)S(1)} %get-tuple-element.63), channel_id=1, source_target_pairs={{0,3},{1,0},{2,1},{3,2},{4,7},{5,4},{6,5},{7,6},{8,11},{9,8},{10,9... | collective-permute-start | bytes 786440 | tf_op jit(solution)/shard_map/ppermute | solution.py:32
  10.0 41.0 %collective-permute-start.1 = (bf16[2,32,2048]{2,1,0:T(8,128)(2,1)S(1)}, bf16[2,32,2048]{2,1,0:T(8,128)(2,1)S(1)}, u32[]{:S(2)}, u32[]{:S(2)}) collective-permute-start(bf16[2,32,2048]{2,1,0:T(8,128)(2,1)S(1)} %get-tuple-element.63), channel_id=1, source_target_pairs={{0,2},{1,3},{2,0},{3,1},{4,6},{5,7},{6,4},{7,5},{8,10},{9,11},{10,... | collective-permute-start | bytes 786440 | tf_op jit(solution)/shard_map/ppermute | solution.py:32
  12.9 38.0 %collective-permute-start = (bf16[2,32,2048]{2,1,0:T(8,128)(2,1)S(1)}, bf16[2,32,2048]{2,1,0:T(8,128)(2,1)S(1)}, u32[]{:S(2)}, u32[]{:S(2)}) collective-permute-start(bf16[2,32,2048]{2,1,0:T(8,128)(2,1)S(1)} %get-tuple-element.63), channel_id=1, source_target_pairs={{0,1},{1,2},{2,3},{3,0},{4,5},{5,6},{6,7},{7,4},{8,9},{9,10},{10,1... | collective-permute-start | bytes 786440 | tf_op jit(solution)/shard_map/ppermute | solution.py:32
  69.1 21.5 %collective-permute-start.3 = (bf16[4,32,6656]{2,1,0:T(8,128)(2,1)}, bf16[4,32,6656]{2,1,0:T(8,128)(2,1)}, u32[]{:S(2)}, u32[]{:S(2)}) collective-permute-start(bf16[4,32,6656]{2,1,0:T(8,128)(2,1)} %bitcast.11), channel_id=1, source_target_pairs={{0,4},{4,0},{8,12},{12,8},{16,20},{20,16},{24,28},{28,24},{1,5},{5... | collective-permute-start | bytes 5111816 | tf_op jit(solution)/shard_map/ppermute | solution.py:28
  97.5 18.7 %collective-permute-start.21 = (bf16[2,32,3328]{2,1,0:T(8,128)(2,1)S(1)}, bf16[2,32,3328]{2,1,0:T(8,128)(2,1)S(1)}, u32[]{:S(2)}, u32[]{:S(2)}) collective-permute-start(bf16[2,32,3328]{2,1,0:T(8,128)(2,1)S(1)} %pad_maximum_fusion.14), channel_id=1, source_target_pairs={{0,8},{4,12},{8,0},{12,4},{16,24},{20,28},{24,16},{28,20},{1,9},{5... | collective-permute-start | bytes 1277960 | tf_op jit(solution)/shard_map/ppermute | solution.py:28
  98.1 19.6 %collective-permute-start.23 = (bf16[2,32,3328]{2,1,0:T(8,128)(2,1)S(1)}, bf16[2,32,3328]{2,1,0:T(8,128)(2,1)S(1)}, u32[]{:S(2)}, u32[]{:S(2)}) collective-permute-start(bf16[2,32,3328]{2,1,0:T(8,128)(2,1)S(1)} %stack.89), channel_id=1, source_target_pairs={{0,16},{4,20},{8,24},{12,28},{16,0},{20,4},{24,8},{28,12},{1,17},{... | collective-permute-start | bytes 1277960 | tf_op jit(solution)/shard_map/ppermute | solution.py:28
  108.7 13.6 %collective-permute-start.5 = (bf16[1,32,3328]{2,1,0:T(8,128)(2,1)S(1)}, bf16[1,32,3328]{2,1,0:T(8,128)(2,1)S(1)}, u32[]{:S(2)}, u32[]{:S(2)}) collective-permute-start(bf16[1,32,3328]{2,1,0:T(8,128)(2,1)S(1)} %get-tuple-element.15), channel_id=1, source_target_pairs={{0,16},{4,20},{8,24},{12,28},{16,0},{20,4},{24,8},{28,12},{1,17},{... | collective-permute-start | bytes 638984 | tf_op jit(solution)/shard_map/ppermute | solution.py:28
  130.2 19.8 %collective-permute-start.11 = (bf16[1,32,6656]{2,1,0:T(8,128)(2,1)S(1)}, bf16[1,32,6656]{2,1,0:T(8,128)(2,1)S(1)}, u32[]{:S(2)}, u32[]{:S(2)}) collective-permute-start(bf16[1,32,6656]{2,1,0:T(8,128)(2,1)S(1)} %bitcast.122), channel_id=1, source_target_pairs={{0,16},{4,20},{8,24},{12,28},{16,0},{20,4},{24,8},{28,12},{1,17},{... | collective-permute-start | bytes 1277960 | tf_op jit(solution)/shard_map/ppermute | solution.py:28
  130.7 20.8 %collective-permute-start.8 = (bf16[1,32,6656]{2,1,0:T(8,128)(2,1)S(1)}, bf16[1,32,6656]{2,1,0:T(8,128)(2,1)S(1)}, u32[]{:S(2)}, u32[]{:S(2)}) collective-permute-start(bf16[1,32,6656]{2,1,0:T(8,128)(2,1)S(1)} %bitcast.120), channel_id=1, source_target_pairs={{0,8},{4,12},{8,0},{12,4},{16,24},{20,28},{24,16},{28,20},{1,9},{5... | collective-permute-start | bytes 1277960 | tf_op jit(solution)/shard_map/ppermute | solution.py:28
  140.9 28.8 %collective-permute-start.29 = (bf16[2,32,6656]{2,1,0:T(8,128)(2,1)S(1)}, bf16[2,32,6656]{2,1,0:T(8,128)(2,1)S(1)}, u32[]{:S(2)}, u32[]{:S(2)}) collective-permute-start(bf16[2,32,6656]{2,1,0:T(8,128)(2,1)S(1)} %pad_maximum_fusion.11), channel_id=1, source_target_pairs={{0,8},{4,12},{8,0},{12,4},{16,24},{20,28},{24,16},{28,20},{1,9},{5... | collective-permute-start | bytes 2555912 | tf_op jit(solution)/shard_map/ppermute | solution.py:28
  142.5 27.6 %collective-permute-start.26 = (bf16[2,32,6656]{2,1,0:T(8,128)(2,1)S(1)}, bf16[2,32,6656]{2,1,0:T(8,128)(2,1)S(1)}, u32[]{:S(2)}, u32[]{:S(2)}) collective-permute-start(bf16[2,32,6656]{2,1,0:T(8,128)(2,1)S(1)} %pad_maximum_fusion.10), channel_id=1, source_target_pairs={{0,16},{4,20},{8,24},{12,28},{16,0},{20,4},{24,8},{28,12},{1,17},{... | collective-permute-start | bytes 2555912 | tf_op jit(solution)/shard_map/ppermute | solution.py:28
  150.1 35.9 %collective-permute-start.12 = (bf16[2,32,6656]{2,1,0:T(8,128)(2,1)S(1)}, bf16[2,32,6656]{2,1,0:T(8,128)(2,1)S(1)}, u32[]{:S(2)}, u32[]{:S(2)}) collective-permute-start(bf16[2,32,6656]{2,1,0:T(8,128)(2,1)S(1)} %pad_maximum_fusion.8), channel_id=1, source_target_pairs={{0,8},{4,12},{8,0},{12,4},{16,24},{20,28},{24,16},{28,20},{1,9},{5... | collective-permute-start | bytes 2555912 | tf_op jit(solution)/shard_map/ppermute | solution.py:28
  151.6 34.6 %collective-permute-start.9 = (bf16[2,32,6656]{2,1,0:T(8,128)(2,1)S(1)}, bf16[2,32,6656]{2,1,0:T(8,128)(2,1)S(1)}, u32[]{:S(2)}, u32[]{:S(2)}) collective-permute-start(bf16[2,32,6656]{2,1,0:T(8,128)(2,1)S(1)} %pad_maximum_fusion.7), channel_id=1, source_target_pairs={{0,16},{4,20},{8,24},{12,28},{16,0},{20,4},{24,8},{28,12},{1,17},{... | collective-permute-start | bytes 2555912 | tf_op jit(solution)/shard_map/ppermute | solution.py:28
  169.9 26.1 %collective-permute-start.30 = (bf16[128,6656]{1,0:T(8,128)(2,1)S(1)}, bf16[128,6656]{1,0:T(8,128)(2,1)S(1)}, u32[]{:S(2)}, u32[]{:S(2)}) collective-permute-start(bf16[128,6656]{1,0:T(8,128)(2,1)S(1)} %pad_maximum_fusion.3), channel_id=1, source_target_pairs={{0,4},{4,0},{8,12},{12,8},{16,20},{20,16},{24,28},{28,24},{1,5},{5... | collective-permute-start | bytes 5111816 | tf_op jit(solution)/shard_map/ppermute | solution.py:28
  171.4 40.5 %collective-permute-start.27 = (bf16[128,6656]{1,0:T(8,128)(2,1)}, bf16[128,6656]{1,0:T(8,128)(2,1)}, u32[]{:S(2)}, u32[]{:S(2)}) collective-permute-start(bf16[128,6656]{1,0:T(8,128)(2,1)} %pad_maximum_fusion.2), channel_id=1, source_target_pairs={{0,4},{4,0},{8,12},{12,8},{16,20},{20,16},{24,28},{28,24},{1,5},{5... | collective-permute-start | bytes 5111816 | tf_op jit(solution)/shard_map/ppermute | solution.py:28
  186.1 51.5 %collective-permute-start.13 = (bf16[128,6656]{1,0:T(8,128)(2,1)S(1)}, bf16[128,6656]{1,0:T(8,128)(2,1)}, u32[]{:S(2)}, u32[]{:S(2)}) collective-permute-start(bf16[128,6656]{1,0:T(8,128)(2,1)S(1)} %pad_maximum_fusion.1), channel_id=1, source_target_pairs={{0,4},{4,0},{8,12},{12,8},{16,20},{20,16},{24,28},{28,24},{1,5},{5... | collective-permute-start | bytes 5111816 | tf_op jit(solution)/shard_map/ppermute | solution.py:28
  187.6 67.3 %collective-permute-start.10 = (bf16[128,6656]{1,0:T(8,128)(2,1)}, bf16[128,6656]{1,0:T(8,128)(2,1)}, u32[]{:S(2)}, u32[]{:S(2)}) collective-permute-start(bf16[128,6656]{1,0:T(8,128)(2,1)} %pad_maximum_fusion), channel_id=1, source_target_pairs={{0,4},{4,0},{8,12},{12,8},{16,20},{20,16},{24,28},{28,24},{1,5},{5... | collective-permute-start | bytes 5111816 | tf_op jit(solution)/shard_map/ppermute | solution.py:28
  231.8 43.4 %collective-permute-start.33 = (bf16[2,32,2048]{2,1,0:T(8,128)(2,1)S(1)}, bf16[2,32,2048]{2,1,0:T(8,128)(2,1)}, u32[]{:S(2)}, u32[]{:S(2)}) collective-permute-start(bf16[2,32,2048]{2,1,0:T(8,128)(2,1)S(1)} %pad_maximum_fusion.20), channel_id=1, source_target_pairs={{0,3},{1,0},{2,1},{3,2},{4,7},{5,4},{6,5},{7,6},{8,11},{9,8},{10,9... | collective-permute-start | bytes 786440 | tf_op jit(solution)/shard_map/ppermute | solution.py:32
  231.9 43.9 %collective-permute-start.32 = (bf16[2,32,2048]{2,1,0:T(8,128)(2,1)S(1)}, bf16[2,32,2048]{2,1,0:T(8,128)(2,1)}, u32[]{:S(2)}, u32[]{:S(2)}) collective-permute-start(bf16[2,32,2048]{2,1,0:T(8,128)(2,1)S(1)} %pad_maximum_fusion.19), channel_id=1, source_target_pairs={{0,2},{1,3},{2,0},{3,1},{4,6},{5,7},{6,4},{7,5},{8,10},{9,11},{10,... | collective-permute-start | bytes 786440 | tf_op jit(solution)/shard_map/ppermute | solution.py:32
  235.6 40.3 %collective-permute-start.31 = (bf16[2,32,2048]{2,1,0:T(8,128)(2,1)}, bf16[2,32,2048]{2,1,0:T(8,128)(2,1)}, u32[]{:S(2)}, u32[]{:S(2)}) collective-permute-start(bf16[2,32,2048]{2,1,0:T(8,128)(2,1)} %pad_maximum_fusion.18), channel_id=1, source_target_pairs={{0,1},{1,2},{2,3},{3,0},{4,5},{5,6},{6,7},{7,4},{8,9},{9,10},{10,1... | collective-permute-start | bytes 786440 | tf_op jit(solution)/shard_map/ppermute | solution.py:32
  274.0 22.1 %collective-permute-start.15 = (bf16[2,32,2048]{2,1,0:T(8,128)(2,1)S(1)}, bf16[2,32,2048]{2,1,0:T(8,128)(2,1)S(1)}, u32[]{:S(2)}, u32[]{:S(2)}) collective-permute-start(bf16[2,32,2048]{2,1,0:T(8,128)(2,1)S(1)} %pad_maximum_fusion.16), channel_id=1, source_target_pairs={{0,2},{1,3},{2,0},{3,1},{4,6},{5,7},{6,4},{7,5},{8,10},{9,11},{10,... | collective-permute-start | bytes 786440 | tf_op jit(solution)/shard_map/ppermute | solution.py:32
  275.2 20.9 %collective-permute-start.14 = (bf16[2,32,2048]{2,1,0:T(8,128)(2,1)S(1)}, bf16[2,32,2048]{2,1,0:T(8,128)(2,1)S(1)}, u32[]{:S(2)}, u32[]{:S(2)}) collective-permute-start(bf16[2,32,2048]{2,1,0:T(8,128)(2,1)S(1)} %pad_maximum_fusion.15), channel_id=1, source_target_pairs={{0,1},{1,2},{2,3},{3,0},{4,5},{5,6},{6,7},{7,4},{8,9},{9,10},{10,1... | collective-permute-start | bytes 786440 | tf_op jit(solution)/shard_map/ppermute | solution.py:32
  (12 other events, 118.8 us)

commit v2 on v0

v2 whole, which is shorter than its diff:
```python
import functools

import jax
import jax.numpy as jnp
from jax import lax
from jax.experimental import pallas as pl
from jax.experimental.pallas import tpu as pltpu
from jax.sharding import PartitionSpec as P

TOKEN_CHUNKS = 2
SLOTS = 4
HINT = 1 << 10
MIB = 1 << 20


def contract_last(left, right):
    return lax.dot_general(
        left, right, (((1,), (1,)), ((), ())), preferred_element_type=jnp.float32
    )


def swiglu_back(hidden_grad, gate_saved, up_saved):
    gate_float = gate_saved.astype(jnp.float32)
    up_float = up_saved.astype(jnp.float32)
    sigmoid_gate = jax.nn.sigmoid(gate_float)
    up_grad = (hidden_grad * gate_float * sigmoid_gate).astype(jnp.bfloat16)
    gate_grad = (
        hidden_grad * up_float * sigmoid_gate * (1.0 + gate_float * (1.0 - sigmoid_gate))
    ).astype(jnp.bfloat16)
    return (gate_grad, up_grad)


def swap(value, size):
    return lax.ppermute(value, "row", [(i, i ^ 1) for i in range(size)])


def exchange(value, size, j):
    top = (size // 2).bit_length() - 2
    return lax.ppermute(
        value, "row", [(i, i ^ (2 << (top - j if i & 1 else j))) for i in range(size)]
    )


def turn(value, size, distance):
    return lax.ppermute(value, "col", [(i, (i + distance) % size) for i in range(size)])


def after(value, *earlier):
    return lax.optimization_barrier((value, *earlier))[0]


def flipped(chip, core, k, chips):
    other = 0
    count = chips.bit_length() - 1
    for i in range(count):
        flip = ((k >> i) & 1) + core * (((k >> (count - 1 - i)) & 1) - ((k >> i) & 1))
        other = other + ((chip // (1 << i)) % 2 + flip) % 2 * (1 << i)
    return other


def difference(chip, other, core, chips):
    k = 0
    count = chips.bit_length() - 1
    for i in range(count):
        differs = ((chip // (1 << i)) % 2 + (other // (1 << i)) % 2) % 2
        k = k + differs * ((1 << i) + core * ((1 << (count - 1 - i)) - (1 << i)))
    return k


def block_of(extent, most):
    return max(d for d in range(128, most + 1, 128) if extent % d == 0)


def hidden_kernel(rows, cols, starts, block, count, *refs):
    pieces, weight, refs = refs[:count], refs[count], refs[count + 1 :]
    outs, (tokens, buffer, sems) = refs[:-3], refs[-3:]
    me, plane = lax.axis_index("row"), lax.axis_index("col")
    per_plane, half = rows // cols, rows // 2
    step = outs[0].shape[1]
    steps = outs[0].shape[2] // block

    def fetch(start, i):
        slot = lax.rem(i, SLOTS)
        return pltpu.make_async_copy(
            weight.at[pl.ds(start + i * block, block)], buffer.at[slot], sems.at[slot]
        )

    for i in range(min(SLOTS, steps)):
        fetch(starts[0], i).start()

    def place(piece, owner_plane):
        for sub in range(per_plane):
            owner = owner_plane * per_plane + sub
            k = difference(me // 2, owner // 2, owner % 2, half)
            same = 1 - (owner % 2 + me % 2) % 2
            to = pl.multiple_of((same * half + k) * step, step)
            tokens[pl.ds(to, step), :] = piece[sub * step : (sub + 1) * step, :]

    place(pieces[0], plane)
    for d in range(1, cols):
        if count == cols:
            place(pieces[d], (plane + cols - d) % cols)
        else:
            pl.when(plane >= d)(functools.partial(place, pieces[d], plane - d))
            pl.when(plane + d < cols)(functools.partial(place, pieces[cols - 1 + d], plane + d))

    for n, start in enumerate(starts):
        send, keep = outs[2 * n : 2 * n + 2]
        if n:
            for i in range(min(SLOTS, steps)):
                fetch(start, i).start()

        def body(i, carry):
            fetch(start, i).wait()
            result = contract_last(tokens[...], buffer[lax.rem(i, SLOTS)])
            columns = pl.ds(pl.multiple_of(i * block, 128), block)
            for k in range(half):
                send[k, :, columns] = result[k * step : (k + 1) * step].astype(send.dtype)
                keep[k, :, columns] = result[(half + k) * step : (half + k + 1) * step]

            @pl.when(i + SLOTS < steps)
            def _():
                fetch(start, i + SLOTS).start()

            return carry

        lax.fori_loop(0, steps, body, 0)


def hidden_partial(rows, cols, pieces, weight, starts, size):
    count, width = pieces[0].shape
    step = count * cols // rows
    half = rows // 2
    block = block_of(size, 256)
    whole = pl.BlockSpec(memory_space=pltpu.VMEM)
    return pl.pallas_call(
        functools.partial(hidden_kernel, rows, cols, starts, block, len(pieces)),
        out_shape=(
            jax.ShapeDtypeStruct((half, step, size), jnp.bfloat16),
            jax.ShapeDtypeStruct((half, step, size), jnp.float32),
        )
        * len(starts),
        in_specs=[whole] * len(pieces) + [pl.BlockSpec(memory_space=pl.ANY)],
        out_specs=(whole,) * (2 * len(starts)),
        scratch_shapes=[
            pltpu.VMEM((rows * step, width), jnp.bfloat16),
            pltpu.VMEM((SLOTS, block, width), jnp.bfloat16),
            pltpu.SemaphoreType.DMA((SLOTS,)),
        ],
        compiler_params=pltpu.CompilerParams(vmem_limit_bytes=40 * MIB),
        cost_estimate=pl.CostEstimate(flops=HINT, bytes_accessed=HINT, transcendentals=0),
    )(*pieces, weight)


def input_kernel(rows, cols, start, block, *refs):
    pieces, gate_weight, up_weight = refs[:rows], refs[rows], refs[rows + 1]
    outs, (left, right, buffer, sems) = refs[rows + 2 : -4], refs[-4:]
    me, plane = lax.axis_index("row"), lax.axis_index("col")
    per_plane, half = rows // cols, rows // 2
    step, depth = pieces[0].shape[1:]
    steps = outs[0].shape[1] // block
    count = per_plane * step

    def fetch(which, i):
        slot = lax.rem(2 * i + which, SLOTS)
        return pltpu.make_async_copy(
            (gate_weight, up_weight)[which].at[pl.ds(start + i * block, block)],
            buffer.at[slot],
            sems.at[slot],
        )

    for i in range(min(SLOTS, 2 * steps)):
        fetch(i % 2, i // 2).start()
    for j, piece in enumerate(pieces):
        core = (me + j // half) % 2
        owner = 2 * flipped(me // 2, core, j % half, half) + core
        distance = (owner // per_plane + cols - plane) % cols
        place = pl.multiple_of((distance * per_plane + owner % per_plane) * step, step)
        left[pl.ds(place, step), :] = piece[0]
        right[pl.ds(place, step), :] = piece[1]

    def multiply(which, held, i):
        fetch(which, i).wait()
        product = contract_last(held[...], buffer[lax.rem(2 * i + which, SLOTS)])

        @pl.when(2 * i + which + SLOTS < 2 * steps)
        def _():
            fetch(which, i + SLOTS // 2).start()

        return product

    def body(i, carry):
        result = multiply(0, left, i) + multiply(1, right, i)
        columns = pl.ds(pl.multiple_of(i * block, 128), block)
        outs[0][:, columns] = result[:count]
        for d in range(1, cols):
            outs[d][:, columns] = result[d * count : (d + 1) * count].astype(jnp.bfloat16)
        return carry

    lax.fori_loop(0, steps, body, 0)


def input_partial(rows, cols, pieces, gate_weight, up_weight, start, size):
    _, step, depth = pieces[0].shape
    count = step * rows // cols
    block = block_of(size, 256)
    whole, anywhere = pl.BlockSpec(memory_space=pltpu.VMEM), pl.BlockSpec(memory_space=pl.ANY)
    return pl.pallas_call(
        functools.partial(input_kernel, rows, cols, start, block),
        out_shape=(jax.ShapeDtypeStruct((count, size), jnp.float32),)
        + (jax.ShapeDtypeStruct((count, size), jnp.bfloat16),) * (cols - 1),
        in_specs=[whole] * rows + [anywhere] * 2,
        out_specs=(whole,) * cols,
        scratch_shapes=[
            pltpu.VMEM((rows * step, depth), jnp.bfloat16),
            pltpu.VMEM((rows * step, depth), jnp.bfloat16),
            pltpu.VMEM((SLOTS, block, depth), jnp.bfloat16),
            pltpu.SemaphoreType.DMA((SLOTS,)),
        ],
        compiler_params=pltpu.CompilerParams(vmem_limit_bytes=40 * MIB),
        cost_estimate=pl.CostEstimate(flops=HINT, bytes_accessed=HINT, transcendentals=0),
    )(*pieces, gate_weight, up_weight)


class Chain:
    def __init__(self):
        self.last = []

    def begin(self, value):
        return after(value, *self.last) if self.last else value

    def end(self, *values):
        self.last = list(values)


class Halving:
    def __init__(self, chain, rows, send, keep):
        self.chain, self.rows, self.keep = chain, rows, keep
        self.got, self.step = swap(send, rows), 0

    def pair(self):
        got = self.chain.begin(self.got)
        pair = self.keep + got.astype(jnp.float32)
        self.state = {k: pair[k] for k in range(pair.shape[0])}
        self.send()

    def send(self):
        self.sent = [k for k in sorted(self.state) if (k >> self.step) & 1]
        value = jnp.stack([self.state[k] for k in self.sent]).astype(jnp.bfloat16)
        self.chain.end(value)
        self.got = exchange(value, self.rows, self.step)

    def add(self):
        got = self.chain.begin(self.got)
        for j, k in enumerate(self.sent):
            to = k ^ (1 << self.step)
            self.state[to] = self.state[to] + got[j].astype(jnp.float32)
            del self.state[k]
        self.step += 1


def per_device(rows, cols, out_grad, gate_saved, up_saved, gate_weight, up_weight, down_weight):
    share, hidden = gate_saved.shape
    width = out_grad.shape[1]
    per_plane = rows // cols
    step = share // TOKEN_CHUNKS
    mid = hidden // 2
    half = rows // 2
    bits = range(half.bit_length() - 1)
    chain = Chain()

    def tokens(t):
        own = out_grad.reshape(per_plane, TOKEN_CHUNKS, step, width)[:, t]
        return own.reshape(per_plane * step, width)

    def multiply(pieces, parts):
        pieces = [chain.begin(pieces[0])] + pieces[1:]
        outs = hidden_partial(rows, cols, pieces, down_weight, [i * mid for i in parts], mid)
        chain.end(outs[1])
        return [
            Halving(chain, rows, *outs[2 * n : 2 * n + 2]) for n in range(len(parts))
        ]

    def next_sums(sides):
        for side in sides:
            side.add()
            side.send()

    def activate(t, sides):
        for side in sides:
            side.add()
        hidden_grad = jnp.concatenate([side.state[0] for side in sides], axis=1)
        mine = slice(t * step, (t + 1) * step)
        both = jnp.stack(swiglu_back(hidden_grad, gate_saved[mine], up_saved[mine]))
        chain.end(both)
        return [both]

    def spread(pieces):
        j = len(pieces).bit_length() - 1
        return pieces + [exchange(piece, rows, j) for piece in pieces]

    def cross(pieces):
        return pieces + [swap(piece, rows) for piece in pieces]

    def share_of(pieces, start, size):
        pieces = [chain.begin(pieces[0])] + pieces[1:]
        outs = input_partial(rows, cols, pieces, gate_weight, up_weight, start, size)
        chain.end(outs[0])
        return outs

    def start_sums(own, *sends):
        return [own] + [turn(send, cols, d) for d, send in enumerate(sends, 1)]

    def finish_sums(own, *others):
        own = chain.begin(own)
        for other in others:
            own = own + other.astype(jnp.float32)
        own = own.astype(jnp.bfloat16)
        chain.end(own)
        return own

    own, later = tokens(0), tokens(1)
    near = [own] + [turn(own, cols, d) for d in range(1, cols)]
    later = after(later, near[1])
    far = [later] + [turn(later, cols, d) for d in range(1, cols)]

    first = multiply(near, [0]) + multiply(near, [1])
    for side in first:
        side.pair()
    for _ in bits[1:]:
        next_sums(first)
    second = multiply(far, [0])
    first = activate(0, first)
    for _ in bits:
        first = spread(first)
    second += multiply(far, [1])
    for side in second:
        side.pair()
    for _ in bits[1:]:
        next_sums(second)
    chain.last += first[1:]
    second = activate(1, second)
    for _ in bits[1:]:
        second = spread(second)
    first = cross(first)
    sums = [share_of(first, 0, width // 2)]
    second = [chain.begin(piece) if j else piece for j, piece in enumerate(second)]
    second = spread(second)
    sums.append(share_of(first, width // 2, width // 2))
    sums = start_sums(*[jnp.concatenate(some, axis=1) for some in zip(*sums)])
    second = cross(second)
    results = [start_sums(*share_of(second, 0, width // 2))]
    first = finish_sums(*sums)
    results.append(start_sums(*share_of(second, width // 2, width // 2)))
    second = jnp.concatenate([finish_sums(*some) for some in results], axis=1)
    results = [value.reshape(per_plane, step, width) for value in (first, second)]
    return jnp.stack(results, axis=1).reshape(out_grad.shape)


def solution(mesh):
    rows, cols = mesh.shape["row"], mesh.shape["col"]
    placed = (
        P("col", "row"),
        P("row", "col"),
        P("row", "col"),
        P("row", "col"),
        P("row", "col"),
        P("col", "row"),
    )
    return jax.shard_map(
        functools.partial(per_device, rows, cols),
        mesh=mesh,
        in_specs=placed,
        out_specs=P("col", "row"),
        check_vma=False,
    )
```

time: 384 us -> 218 us (0.57)
  waiting for transfers between devices: 300 us -> 90 us
  Pallas kernels: 0 us -> 79.6 us
  matrix products: 64.2 us -> 0 us
  starting transfers between devices: 0.16 us -> 41.9 us
  between operations: 13.1 us -> 0.43 us
    reduce_scatter x2 -> x0, waiting for transfers between devices: 174 us -> none  [the longest x1 96.8 us: per_device(): lax.psum_scatter(partial_hidden, 'row', scatter_dimension=0, tiled=True)]
    all_gather x3 -> x0, waiting for transfers between devices: 125 us -> none  [the longest x2 75.2 us: per_device(): block_pair = lax.all_gather((gate_grad, up_grad), 'row', axis=0, tiled=True)]
    ppermute x0 -> x41, waiting for transfers between devices: none -> 90 us  [the longest x14 52.3 us: exchange(): lax.ppermute(value, 'row', [(i, i ^ 2 << (top - j if i & 1 else j)) for i...]
    pallas_call x0 -> x8, Pallas kernels: none -> 79.6 us  [the longest x4 49.2 us: input_partial(): pl.pallas_call(functools.partial(input_kernel, rows, cols, start, block),...]
    dot_general x3 -> x0, matrix products: 64.2 us -> none  [contract_last(): lax.dot_general(left, right, (((1,), (1,)), ((), ())), preferred_element_...]
    ppermute x0 -> x41, starting transfers between devices: none -> 41.9 us  [the longest x15 28.3 us: turn(): lax.ppermute(value, 'col', [(i, (i + distance) % size) for i in range(siz...]
    convert_element_type x2 -> x7, other arithmetic: 5.56 us -> 0.4 us  [the longest x3 0.24 us: finish_sums(): own = own.astype(jnp.bfloat16)]
  transfers between devices with their start and end apart: 5 -> 41, of which waited for: 5 -> 17; matrix products, arithmetic and copies ran while one was open for 6% -> 1% of each run, Pallas kernels for 0% -> 33%
where the time goes in v2:
time: 218 us
  waiting for transfers between devices  90 us (41%)
  Pallas kernels  79.6 us (37%)
  starting transfers between devices  41.9 us (19%)
  local copies, waits for them, and re-layouts  3.2 us (1%)
  other arithmetic  2.79 us (1%)
    ppermute x14, waiting for transfers between devices, exchange(): lax.ppermute(value, 'row', [(i, i ^ 2 << (top - j if i & 1 else j)) for i...  52.3 us
    pallas_call x4, Pallas kernels, input_partial(): pl.pallas_call(functools.partial(input_kernel, rows, cols, start, block),...  49.2 us
    ppermute x15, waiting for transfers between devices, turn(): lax.ppermute(value, 'col', [(i, (i + distance) % size) for i in range(siz...  34.9 us
    pallas_call x4, Pallas kernels, hidden_partial(): pl.pallas_call(functools.partial(hidden_kernel, rows, cols, starts, block...  30.4 us
    ppermute x15, starting transfers between devices, turn(): lax.ppermute(value, 'col', [(i, (i + distance) % size) for i in range(siz...  28.3 us
    ppermute x14, starting transfers between devices, exchange(): lax.ppermute(value, 'row', [(i, i ^ 2 << (top - j if i & 1 else j)) for i...  11.5 us
  transfers between devices with their start and end apart: 41, of which 17 were waited for; matrix products, arithmetic and copies ran while one was open for 1% of the time, Pallas kernels for 33%

profile of v2, /device:TPU:0, one launch (start us, length us, event | category | flops | bytes accessed | tf_op | source)
XLA Modules:
  0.0 217.9 jit_solution(3867921941772623460)
XLA Ops:
  1.1 3.1 %collective-permute-start = (bf16[64,2048]{1,0:T(8,128)(2,1)S(1)}, bf16[64,2048]{1,0:T(8,128)(2,1)S(1)}, u32[]{:S(2)}, u32[]{:S(2)}) collective-permute-start(bf16[64,2048]{1,0:T(8,128)(2,1)S(1)} %bitcast.31), channel_id=1, source_target_pairs={{0,1},{1,2},{2,3},{3,0},{4,5},{5,6},{6,7},{7,4},{8,9},{9,10},{10,1... | collective-permute-start | bytes 786440 | tf_op jit(solution)/shard_map/ppermute | solution.py:45
  4.2 2.6 %collective-permute-start.1 = (bf16[64,2048]{1,0:T(8,128)(2,1)S(1)}, bf16[64,2048]{1,0:T(8,128)(2,1)S(1)}, u32[]{:S(2)}, u32[]{:S(2)}) collective-permute-start(bf16[64,2048]{1,0:T(8,128)(2,1)S(1)} %bitcast.32), channel_id=1, source_target_pairs={{0,2},{1,3},{2,0},{3,1},{4,6},{5,7},{6,4},{7,5},{8,10},{9,11},{10,... | collective-permute-start | bytes 786440 | tf_op jit(solution)/shard_map/ppermute | solution.py:45
  8.1 5.4 %collective-permute-done.refs_1_ = bf16[64,2048]{1,0:T(8,128)(2,1)S(1)} collective-permute-done((bf16[64,2048]{1,0:T(8,128)(2,1)S(1)}, bf16[64,2048]{1,0:T(8,128)(2,1)S(1)}, u32[]{:S(2)}, u32[]{:S(2)}) %collective-permute-start) | collective-permute-done | bytes 262176 | tf_op jit(solution)/shard_map/ppermute | solution.py:45
  13.5 10.4 %collective-permute-done.1.refs_2_ = bf16[64,2048]{1,0:T(8,128)(2,1)S(1)} collective-permute-done((bf16[64,2048]{1,0:T(8,128)(2,1)S(1)}, bf16[64,2048]{1,0:T(8,128)(2,1)S(1)}, u32[]{:S(2)}, u32[]{:S(2)}) %collective-permute-start.1) | collective-permute-done | bytes 262176 | tf_op jit(solution)/shard_map/ppermute | solution.py:45
  23.9 7.6 %shard_map.64 = (bf16[4,32,3328]{2,1,0:T(8,128)(2,1)S(1)}, f32[4,32,3328]{2,1,0:T(8,128)S(1)}) custom-call(bf16[64,2048]{1,0:T(8,128)(2,1)S(1)} %bitcast.34, bf16[64,2048]{1,0:T(8,128)(2,1)S(1)} %collective-permute-done.refs_1_, bf16[64,2048]{1,0:T(8,128)(2,1)S(1)} %collective-permute-done.1.refs_2_, bf16[64,2048]{1,0:T(8,128)(2,1)S(1)} %collective-permute-done.2.refs_3_, ...), custom_call_target="tpu_custom_call" | custom-call | flops 1024 | bytes 1024 | tf_op jit(solution)/shard_map/pallas_call | solution.py:136
  31.5 6.1 %collective-permute-start.8 = (bf16[64,2048]{1,0:T(8,128)(2,1)S(1)}, bf16[64,2048]{1,0:T(8,128)(2,1)S(1)}, u32[]{:S(2)}, u32[]{:S(2)}) collective-permute-start(bf16[64,2048]{1,0:T(8,128)(2,1)S(1)} %bitcast.26), channel_id=1, source_target_pairs={{0,1},{1,2},{2,3},{3,0},{4,5},{5,6},{6,7},{7,4},{8,9},{9,10},{10,1... | collective-permute-start | bytes 786440 | tf_op jit(solution)/shard_map/ppermute | solution.py:45
  40.1 7.6 %shard_map.65 = (bf16[4,32,3328]{2,1,0:T(8,128)(2,1)S(1)}, f32[4,32,3328]{2,1,0:T(8,128)S(1)}) custom-call(bf16[64,2048]{1,0:T(8,128)(2,1)S(1)} %bitcast.35, bf16[64,2048]{1,0:T(8,128)(2,1)S(1)} %collective-permute-done.refs_1_, bf16[64,2048]{1,0:T(8,128)(2,1)S(1)} %collective-permute-done.1.refs_2_, bf16[64,2048]{1,0:T(8,128)(2,1)S(1)} %collective-permute-done.2.refs_3_, ...), custom_call_target="tpu_custom_call" | custom-call | flops 1024 | bytes 1024 | tf_op jit(solution)/shard_map/pallas_call | solution.py:136
  52.0 4.3 %collective-permute-done.4 = bf16[2,32,3328]{2,1,0:T(8,128)(2,1)S(1)} collective-permute-done((bf16[2,32,3328]{2,1,0:T(8,128)(2,1)S(1)}, bf16[2,32,3328]{2,1,0:T(8,128)(2,1)S(1)}, u32[]{:S(2)}, u32[]{:S(2)}) %collective-permute-start.4) | collective-permute-done | bytes 426016 | tf_op jit(solution)/shard_map/ppermute | solution.py:39
  56.4 4.5 %collective-permute-done.7 = bf16[2,32,3328]{2,1,0:T(8,128)(2,1)S(1)} collective-permute-done((bf16[2,32,3328]{2,1,0:T(8,128)(2,1)S(1)}, bf16[2,32,3328]{2,1,0:T(8,128)(2,1)S(1)}, u32[]{:S(2)}, u32[]{:S(2)}) %collective-permute-start.7) | collective-permute-done | bytes 426016 | tf_op jit(solution)/shard_map/ppermute | solution.py:39
  63.0 7.6 %shard_map.66 = (bf16[4,32,3328]{2,1,0:T(8,128)(2,1)S(1)}, f32[4,32,3328]{2,1,0:T(8,128)S(1)}) custom-call(bf16[64,2048]{1,0:T(8,128)(2,1)S(1)} %bitcast.29, bf16[64,2048]{1,0:T(8,128)(2,1)S(1)} %collective-permute-done.8.refs_1_, bf16[64,2048]{1,0:T(8,128)(2,1)S(1)} %collective-permute-done.9.refs_2_, bf16[64,2048]{1,0:T(8,128)(2,1)S(1)} %collective-permute-done.10.refs_3_, ...), custom_call_target="tpu_custom_call" | custom-call | flops 1024 | bytes 1024 | tf_op jit(solution)/shard_map/pallas_call | solution.py:136
  75.6 7.6 %shard_map.67 = (bf16[4,32,3328]{2,1,0:T(8,128)(2,1)S(1)}, f32[4,32,3328]{2,1,0:T(8,128)S(1)}) custom-call(bf16[64,2048]{1,0:T(8,128)(2,1)S(1)} %bitcast.30, bf16[64,2048]{1,0:T(8,128)(2,1)S(1)} %collective-permute-done.8.refs_1_, bf16[64,2048]{1,0:T(8,128)(2,1)S(1)} %collective-permute-done.9.refs_2_, bf16[64,2048]{1,0:T(8,128)(2,1)S(1)} %collective-permute-done.10.refs_3_, ...), custom_call_target="tpu_custom_call" | custom-call | flops 1024 | bytes 1024 | tf_op jit(solution)/shard_map/pallas_call | solution.py:136
  86.6 7.8 %collective-permute-done.17.refs_1_ = bf16[2,32,6656]{2,1,0:T(8,128)(2,1)S(1)} collective-permute-done((bf16[2,32,6656]{2,1,0:T(8,128)(2,1)S(1)}, bf16[2,32,6656]{2,1,0:T(8,128)(2,1)S(1)}, u32[]{:S(2)}, u32[]{:S(2)}) %collective-permute-start.17) | collective-permute-done | bytes 852000 | tf_op jit(solution)/shard_map/ppermute | solution.py:39
  94.6 8.9 %collective-permute-done.13 = bf16[2,32,3328]{2,1,0:T(8,128)(2,1)S(1)} collective-permute-done((bf16[2,32,3328]{2,1,0:T(8,128)(2,1)S(1)}, bf16[2,32,3328]{2,1,0:T(8,128)(2,1)S(1)}, u32[]{:S(2)}, u32[]{:S(2)}) %collective-permute-start.13) | collective-permute-done | bytes 426016 | tf_op jit(solution)/shard_map/ppermute | solution.py:39
  103.5 9.1 %collective-permute-done.16 = bf16[2,32,3328]{2,1,0:T(8,128)(2,1)S(1)} collective-permute-done((bf16[2,32,3328]{2,1,0:T(8,128)(2,1)S(1)}, bf16[2,32,3328]{2,1,0:T(8,128)(2,1)S(1)}, u32[]{:S(2)}, u32[]{:S(2)}) %collective-permute-start.16) | collective-permute-done | bytes 426016 | tf_op jit(solution)/shard_map/ppermute | solution.py:39
  113.4 5.2 %collective-permute-done.20 = bf16[1,32,3328]{2,1,0:T(8,128)(2,1)S(1)} collective-permute-done((bf16[1,32,3328]{2,1,0:T(8,128)(2,1)S(1)}, bf16[1,32,3328]{2,1,0:T(8,128)(2,1)S(1)}, u32[]{:S(2)}, u32[]{:S(2)}) %collective-permute-start.20) | collective-permute-done | bytes 213024 | tf_op jit(solution)/shard_map/ppermute | solution.py:39
  118.8 5.6 %collective-permute-done.15 = bf16[1,32,3328]{2,1,0:T(8,128)(2,1)S(1)} collective-permute-done((bf16[1,32,3328]{2,1,0:T(8,128)(2,1)S(1)}, bf16[1,32,3328]{2,1,0:T(8,128)(2,1)S(1)}, u32[]{:S(2)}, u32[]{:S(2)}) %collective-permute-start.15) | collective-permute-done | bytes 213024 | tf_op jit(solution)/shard_map/ppermute | solution.py:39
  127.4 12.3 %shard_map.68 = (f32[64,1024]{1,0:T(8,128)S(1)}, bf16[64,1024]{1,0:T(8,128)(2,1)S(1)}, bf16[64,1024]{1,0:T(8,128)(2,1)S(1)}, bf16[64,1024]{1,0:T(8,128)(2,1)S(1)}) custom-call(bf16[2,32,6656]{2,1,0:T(8,128)(2,1)S(1)} %pad_maximum_fusion.1.refs_0_, bf16[2,32,6656]{2,1,0:T(8,128)(2,1)S(1)} %collective-permute-done.17.refs_1_, ...), custom_call_target="tpu_custom_call" | custom-call | flops 1024 | bytes 1024 | tf_op jit(solution)/shard_map/pallas_call | solution.py:208
  139.7 6.9 %collective-permute-done.25.refs_1_ = bf16[2,32,6656]{2,1,0:T(8,128)(2,1)S(1)} collective-permute-done((bf16[2,32,6656]{2,1,0:T(8,128)(2,1)S(1)}, bf16[2,32,6656]{2,1,0:T(8,128)(2,1)S(1)}, u32[]{:S(2)}, u32[]{:S(2)}) %collective-permute-start.25) | collective-permute-done | bytes 852000 | tf_op jit(solution)/shard_map/ppermute | solution.py:39
  147.1 12.3 %shard_map.69 = (f32[64,1024]{1,0:T(8,128)S(1)}, bf16[64,1024]{1,0:T(8,128)(2,1)S(1)}, bf16[64,1024]{1,0:T(8,128)(2,1)S(1)}, bf16[64,1024]{1,0:T(8,128)(2,1)S(1)}) custom-call(bf16[2,32,6656]{2,1,0:T(8,128)(2,1)S(1)} %pad_maximum_fusion.1.refs_0_, bf16[2,32,6656]{2,1,0:T(8,128)(2,1)S(1)} %collective-permute-done.17.refs_1_, ...), custom_call_target="tpu_custom_call" | custom-call | flops 1024 | bytes 1024 | tf_op jit(solution)/shard_map/pallas_call | solution.py:208
  163.1 12.3 %shard_map.70 = (f32[64,1024]{1,0:T(8,128)S(1)}, bf16[64,1024]{1,0:T(8,128)(2,1)S(1)}, bf16[64,1024]{1,0:T(8,128)(2,1)S(1)}, bf16[64,1024]{1,0:T(8,128)(2,1)S(1)}) custom-call(bf16[2,32,6656]{2,1,0:T(8,128)(2,1)S(1)} %pad_maximum_fusion.3.refs_0_, bf16[2,32,6656]{2,1,0:T(8,128)(2,1)S(1)} %collective-permute-done.25.refs_1_, ...), custom_call_target="tpu_custom_call" | custom-call | flops 1024 | bytes 1024 | tf_op jit(solution)/shard_map/pallas_call | solution.py:208
  175.4 3.7 %collective-permute-start.37 = (bf16[64,1024]{1,0:T(8,128)(2,1)S(1)}, bf16[64,1024]{1,0:T(8,128)(2,1)S(1)}, u32[]{:S(2)}, u32[]{:S(2)}) collective-permute-start(bf16[64,1024]{1,0:T(8,128)(2,1)S(1)} %get-tuple-element.96), channel_id=1, source_target_pairs={{0,3},{1,0},{2,1},{3,2},{4,7},{5,4},{6,5},{7,6},{8,11},{9,8},{10,9... | collective-permute-start | bytes 393224 | tf_op jit(solution)/shard_map/ppermute | solution.py:45
  181.6 10.7 %collective-permute-done.33 = bf16[64,2048]{1,0:T(8,128)(2,1)S(1)} collective-permute-done((bf16[64,2048]{1,0:T(8,128)(2,1)S(1)}, bf16[64,2048]{1,0:T(8,128)(2,1)S(1)}, u32[]{:S(2)}, u32[]{:S(2)}) %collective-permute-start.33) | collective-permute-done | bytes 262176 | tf_op jit(solution)/shard_map/ppermute | solution.py:45
  192.4 12.3 %shard_map.71 = (f32[64,1024]{1,0:T(8,128)S(1)}, bf16[64,1024]{1,0:T(8,128)(2,1)S(1)}, bf16[64,1024]{1,0:T(8,128)(2,1)S(1)}, bf16[64,1024]{1,0:T(8,128)(2,1)S(1)}) custom-call(bf16[2,32,6656]{2,1,0:T(8,128)(2,1)S(1)} %pad_maximum_fusion.3.refs_0_, bf16[2,32,6656]{2,1,0:T(8,128)(2,1)S(1)} %collective-permute-done.25.refs_1_, ...), custom_call_target="tpu_custom_call" | custom-call | flops 1024 | bytes 1024 | tf_op jit(solution)/shard_map/pallas_call | solution.py:208
  210.1 6.9 %collective-permute-done.39 = bf16[64,1024]{1,0:T(8,128)(2,1)S(1)} collective-permute-done((bf16[64,1024]{1,0:T(8,128)(2,1)S(1)}, bf16[64,1024]{1,0:T(8,128)(2,1)S(1)}, u32[]{:S(2)}, u32[]{:S(2)}) %collective-permute-start.39) | collective-permute-done | bytes 131104 | tf_op jit(solution)/shard_map/ppermute | solution.py:45
  (104 shorter events, 36.8 us)
Async XLA Ops:
  4.2 19.7 %collective-permute-start.1 = (bf16[64,2048]{1,0:T(8,128)(2,1)S(1)}, bf16[64,2048]{1,0:T(8,128)(2,1)S(1)}, u32[]{:S(2)}, u32[]{:S(2)}) collective-permute-start(bf16[64,2048]{1,0:T(8,128)(2,1)S(1)} %bitcast.32), channel_id=1, source_target_pairs={{0,2},{1,3},{2,0},{3,1},{4,6},{5,7},{6,4},{7,5},{8,10},{9,11},{10,... | collective-permute-start | bytes 786440 | tf_op jit(solution)/shard_map/ppermute | solution.py:45
  6.7 17.1 %collective-permute-start.2 = (bf16[64,2048]{1,0:T(8,128)(2,1)S(1)}, bf16[64,2048]{1,0:T(8,128)(2,1)S(1)}, u32[]{:S(2)}, u32[]{:S(2)}) collective-permute-start(bf16[64,2048]{1,0:T(8,128)(2,1)S(1)} %bitcast.33), channel_id=1, source_target_pairs={{0,3},{1,0},{2,1},{3,2},{4,7},{5,4},{6,5},{7,6},{8,11},{9,8},{10,9... | collective-permute-start | bytes 786440 | tf_op jit(solution)/shard_map/ppermute | solution.py:45
  31.5 16.4 %collective-permute-start.3 = (bf16[4,32,3328]{2,1,0:T(8,128)(2,1)S(1)}, bf16[4,32,3328]{2,1,0:T(8,128)(2,1)S(1)}, u32[]{:S(2)}, u32[]{:S(2)}) collective-permute-start(bf16[4,32,3328]{2,1,0:T(8,128)(2,1)S(1)} %get-tuple-element.54), channel_id=1, source_target_pairs={{0,4},{4,0},{8,12},{12,8},{16,20},{20,16},{24,28},{28,24},{1,5},{5... | collective-permute-start | bytes 2555912 | tf_op jit(solution)/shard_map/ppermute | solution.py:34
  31.5 31.5 %collective-permute-start.8 = (bf16[64,2048]{1,0:T(8,128)(2,1)S(1)}, bf16[64,2048]{1,0:T(8,128)(2,1)S(1)}, u32[]{:S(2)}, u32[]{:S(2)}) collective-permute-start(bf16[64,2048]{1,0:T(8,128)(2,1)S(1)} %bitcast.26), channel_id=1, source_target_pairs={{0,1},{1,2},{2,3},{3,0},{4,5},{5,6},{6,7},{7,4},{8,9},{9,10},{10,1... | collective-permute-start | bytes 786440 | tf_op jit(solution)/shard_map/ppermute | solution.py:45
  37.7 25.3 %collective-permute-start.9 = (bf16[64,2048]{1,0:T(8,128)(2,1)S(1)}, bf16[64,2048]{1,0:T(8,128)(2,1)S(1)}, u32[]{:S(2)}, u32[]{:S(2)}) collective-permute-start(bf16[64,2048]{1,0:T(8,128)(2,1)S(1)} %bitcast.27), channel_id=1, source_target_pairs={{0,2},{1,3},{2,0},{3,1},{4,6},{5,7},{6,4},{7,5},{8,10},{9,11},{10,... | collective-permute-start | bytes 786440 | tf_op jit(solution)/shard_map/ppermute | solution.py:45
  39.3 23.7 %collective-permute-start.10 = (bf16[64,2048]{1,0:T(8,128)(2,1)S(1)}, bf16[64,2048]{1,0:T(8,128)(2,1)S(1)}, u32[]{:S(2)}, u32[]{:S(2)}) collective-permute-start(bf16[64,2048]{1,0:T(8,128)(2,1)S(1)} %bitcast.28), channel_id=1, source_target_pairs={{0,3},{1,0},{2,1},{3,2},{4,7},{5,4},{6,5},{7,6},{8,11},{9,8},{10,9... | collective-permute-start | bytes 786440 | tf_op jit(solution)/shard_map/ppermute | solution.py:45
  72.6 21.8 %collective-permute-start.17 = (bf16[2,32,6656]{2,1,0:T(8,128)(2,1)S(1)}, bf16[2,32,6656]{2,1,0:T(8,128)(2,1)S(1)}, u32[]{:S(2)}, u32[]{:S(2)}) collective-permute-start(bf16[2,32,6656]{2,1,0:T(8,128)(2,1)S(1)} %pad_maximum_fusion.1.refs_0_), channel_id=1, source_target_pairs={{0,8},{4,20},{8,0},{12,28},{16,24},{20,4},{24,16},{28,12},{1,9},{5... | collective-permute-start | bytes 2555912 | tf_op jit(solution)/shard_map/ppermute | solution.py:39
  74.1 39.3 %collective-permute-start.18 = (bf16[2,32,6656]{2,1,0:T(8,128)(2,1)S(1)}, bf16[2,32,6656]{2,1,0:T(8,128)(2,1)S(1)}, u32[]{:S(2)}, u32[]{:S(2)}) collective-permute-start(bf16[2,32,6656]{2,1,0:T(8,128)(2,1)S(1)} %pad_maximum_fusion.1.refs_0_), channel_id=1, source_target_pairs={{0,16},{4,12},{8,24},{12,4},{16,0},{20,28},{24,8},{28,20},{1,17},{... | collective-permute-start | bytes 2555912 | tf_op jit(solution)/shard_map/ppermute | solution.py:39
  83.6 19.9 %collective-permute-start.13 = (bf16[2,32,3328]{2,1,0:T(8,128)(2,1)S(1)}, bf16[2,32,3328]{2,1,0:T(8,128)(2,1)S(1)}, u32[]{:S(2)}, u32[]{:S(2)}) collective-permute-start(bf16[2,32,3328]{2,1,0:T(8,128)(2,1)S(1)} %pad_maximum_fusion.8), channel_id=1, source_target_pairs={{0,8},{4,20},{8,0},{12,28},{16,24},{20,4},{24,16},{28,12},{1,9},{5... | collective-permute-start | bytes 1277960 | tf_op jit(solution)/shard_map/ppermute | solution.py:39
  86.0 26.6 %collective-permute-start.16 = (bf16[2,32,3328]{2,1,0:T(8,128)(2,1)S(1)}, bf16[2,32,3328]{2,1,0:T(8,128)(2,1)S(1)}, u32[]{:S(2)}, u32[]{:S(2)}) collective-permute-start(bf16[2,32,3328]{2,1,0:T(8,128)(2,1)S(1)} %pad_maximum_fusion.9), channel_id=1, source_target_pairs={{0,8},{4,20},{8,0},{12,28},{16,24},{20,4},{24,16},{28,12},{1,9},{5... | collective-permute-start | bytes 1277960 | tf_op jit(solution)/shard_map/ppermute | solution.py:39
  94.4 24.4 %collective-permute-start.19 = (bf16[2,32,6656]{2,1,0:T(8,128)(2,1)S(1)}, bf16[2,32,6656]{2,1,0:T(8,128)(2,1)S(1)}, u32[]{:S(2)}, u32[]{:S(2)}) collective-permute-start(bf16[2,32,6656]{2,1,0:T(8,128)(2,1)S(1)} %collective-permute-done.17.refs_1_), channel_id=1, source_target_pairs={{0,16},{4,12},{8,24},{12,4},{16,0},{20,28},{24,8},{28,20},{1,17},{... | collective-permute-start | bytes 2555912 | tf_op jit(solution)/shard_map/ppermute | solution.py:39
  112.9 13.8 %collective-permute-start.21 = (bf16[2,32,6656]{2,1,0:T(8,128)(2,1)S(1)}, bf16[2,32,6656]{2,1,0:T(8,128)(2,1)S(1)}, u32[]{:S(2)}, u32[]{:S(2)}) collective-permute-start(bf16[2,32,6656]{2,1,0:T(8,128)(2,1)S(1)} %pad_maximum_fusion.1.refs_0_), channel_id=1, source_target_pairs={{0,4},{4,0},{8,12},{12,8},{16,20},{20,16},{24,28},{28,24},{1,5},{5... | collective-permute-start | bytes 2555912 | tf_op jit(solution)/shard_map/ppermute | solution.py:34
  112.9 13.8 %collective-permute-start.22 = (bf16[2,32,6656]{2,1,0:T(8,128)(2,1)S(1)}, bf16[2,32,6656]{2,1,0:T(8,128)(2,1)S(1)}, u32[]{:S(2)}, u32[]{:S(2)}) collective-permute-start(bf16[2,32,6656]{2,1,0:T(8,128)(2,1)S(1)} %collective-permute-done.17.refs_1_), channel_id=1, source_target_pairs={{0,4},{4,0},{8,12},{12,8},{16,20},{20,16},{24,28},{28,24},{1,5},{5... | collective-permute-start | bytes 2555912 | tf_op jit(solution)/shard_map/ppermute | solution.py:34
  113.4 13.3 %collective-permute-start.23 = (bf16[2,32,6656]{2,1,0:T(8,128)(2,1)S(1)}, bf16[2,32,6656]{2,1,0:T(8,128)(2,1)S(1)}, u32[]{:S(2)}, u32[]{:S(2)}) collective-permute-start(bf16[2,32,6656]{2,1,0:T(8,128)(2,1)S(1)} %collective-permute-done.18.refs_2_), channel_id=1, source_target_pairs={{0,4},{4,0},{8,12},{12,8},{16,20},{20,16},{24,28},{28,24},{1,5},{5... | collective-permute-start | bytes 2555912 | tf_op jit(solution)/shard_map/ppermute | solution.py:34
  125.1 21.5 %collective-permute-start.25 = (bf16[2,32,6656]{2,1,0:T(8,128)(2,1)S(1)}, bf16[2,32,6656]{2,1,0:T(8,128)(2,1)S(1)}, u32[]{:S(2)}, u32[]{:S(2)}) collective-permute-start(bf16[2,32,6656]{2,1,0:T(8,128)(2,1)S(1)} %pad_maximum_fusion.3.refs_0_), channel_id=1, source_target_pairs={{0,8},{4,20},{8,0},{12,28},{16,24},{20,4},{24,16},{28,12},{1,9},{5... | collective-permute-start | bytes 2555912 | tf_op jit(solution)/shard_map/ppermute | solution.py:39
  126.6 32.8 %collective-permute-start.26 = (bf16[2,32,6656]{2,1,0:T(8,128)(2,1)S(1)}, bf16[2,32,6656]{2,1,0:T(8,128)(2,1)S(1)}, u32[]{:S(2)}, u32[]{:S(2)}) collective-permute-start(bf16[2,32,6656]{2,1,0:T(8,128)(2,1)S(1)} %pad_maximum_fusion.3.refs_0_), channel_id=1, source_target_pairs={{0,16},{4,12},{8,24},{12,4},{16,0},{20,28},{24,8},{28,20},{1,17},{... | collective-permute-start | bytes 2555912 | tf_op jit(solution)/shard_map/ppermute | solution.py:39
  146.6 15.5 %collective-permute-start.28 = (bf16[2,32,6656]{2,1,0:T(8,128)(2,1)S(1)}, bf16[2,32,6656]{2,1,0:T(8,128)(2,1)S(1)}, u32[]{:S(2)}, u32[]{:S(2)}) collective-permute-start(bf16[2,32,6656]{2,1,0:T(8,128)(2,1)S(1)} %pad_maximum_fusion.3.refs_0_), channel_id=1, source_target_pairs={{0,4},{4,0},{8,12},{12,8},{16,20},{20,16},{24,28},{28,24},{1,5},{5... | collective-permute-start | bytes 2555912 | tf_op jit(solution)/shard_map/ppermute | solution.py:34
  146.8 16.0 %collective-permute-start.29 = (bf16[2,32,6656]{2,1,0:T(8,128)(2,1)S(1)}, bf16[2,32,6656]{2,1,0:T(8,128)(2,1)S(1)}, u32[]{:S(2)}, u32[]{:S(2)}) collective-permute-start(bf16[2,32,6656]{2,1,0:T(8,128)(2,1)S(1)} %collective-permute-done.25.refs_1_), channel_id=1, source_target_pairs={{0,4},{4,0},{8,12},{12,8},{16,20},{20,16},{24,28},{28,24},{1,5},{5... | collective-permute-start | bytes 2555912 | tf_op jit(solution)/shard_map/ppermute | solution.py:34
  160.0 19.5 %collective-permute-start.34 = (bf16[64,2048]{1,0:T(8,128)(2,1)S(1)}, bf16[64,2048]{1,0:T(8,128)(2,1)S(1)}, u32[]{:S(2)}, u32[]{:S(2)}) collective-permute-start(bf16[64,2048]{1,0:T(8,128)(2,1)S(1)} %pad_maximum_fusion.12), channel_id=1, source_target_pairs={{0,3},{1,0},{2,1},{3,2},{4,7},{5,4},{6,5},{7,6},{8,11},{9,8},{10,9... | collective-permute-start | bytes 786440 | tf_op jit(solution)/shard_map/ppermute | solution.py:45
  162.1 30.2 %collective-permute-start.33 = (bf16[64,2048]{1,0:T(8,128)(2,1)S(1)}, bf16[64,2048]{1,0:T(8,128)(2,1)S(1)}, u32[]{:S(2)}, u32[]{:S(2)}) collective-permute-start(bf16[64,2048]{1,0:T(8,128)(2,1)S(1)} %pad_maximum_fusion.11), channel_id=1, source_target_pairs={{0,2},{1,3},{2,0},{3,1},{4,6},{5,7},{6,4},{7,5},{8,10},{9,11},{10,... | collective-permute-start | bytes 786440 | tf_op jit(solution)/shard_map/ppermute | solution.py:45
  162.8 29.5 %collective-permute-start.32 = (bf16[64,2048]{1,0:T(8,128)(2,1)S(1)}, bf16[64,2048]{1,0:T(8,128)(2,1)S(1)}, u32[]{:S(2)}, u32[]{:S(2)}) collective-permute-start(bf16[64,2048]{1,0:T(8,128)(2,1)S(1)} %pad_maximum_fusion.10), channel_id=1, source_target_pairs={{0,1},{1,2},{2,3},{3,0},{4,5},{5,6},{6,7},{7,4},{8,9},{9,10},{10,1... | collective-permute-start | bytes 786440 | tf_op jit(solution)/shard_map/ppermute | solution.py:45
  175.4 31.1 %collective-permute-start.37 = (bf16[64,1024]{1,0:T(8,128)(2,1)S(1)}, bf16[64,1024]{1,0:T(8,128)(2,1)S(1)}, u32[]{:S(2)}, u32[]{:S(2)}) collective-permute-start(bf16[64,1024]{1,0:T(8,128)(2,1)S(1)} %get-tuple-element.96), channel_id=1, source_target_pairs={{0,3},{1,0},{2,1},{3,2},{4,7},{5,4},{6,5},{7,6},{8,11},{9,8},{10,9... | collective-permute-start | bytes 393224 | tf_op jit(solution)/shard_map/ppermute | solution.py:45
  179.1 29.4 %collective-permute-start.36 = (bf16[64,1024]{1,0:T(8,128)(2,1)S(1)}, bf16[64,1024]{1,0:T(8,128)(2,1)S(1)}, u32[]{:S(2)}, u32[]{:S(2)}) collective-permute-start(bf16[64,1024]{1,0:T(8,128)(2,1)S(1)} %get-tuple-element.95), channel_id=1, source_target_pairs={{0,2},{1,3},{2,0},{3,1},{4,6},{5,7},{6,4},{7,5},{8,10},{9,11},{10,... | collective-permute-start | bytes 393224 | tf_op jit(solution)/shard_map/ppermute | solution.py:45
  179.5 28.9 %collective-permute-start.35 = (bf16[64,1024]{1,0:T(8,128)(2,1)S(1)}, bf16[64,1024]{1,0:T(8,128)(2,1)S(1)}, u32[]{:S(2)}, u32[]{:S(2)}) collective-permute-start(bf16[64,1024]{1,0:T(8,128)(2,1)S(1)} %get-tuple-element.94), channel_id=1, source_target_pairs={{0,1},{1,2},{2,3},{3,0},{4,5},{5,6},{6,7},{7,4},{8,9},{9,10},{10,1... | collective-permute-start | bytes 393224 | tf_op jit(solution)/shard_map/ppermute | solution.py:45
  (19 other events, 131.3 us)

commit v3 on v2

--- a/solution.py
+++ b/solution.py
@@ -147,17 +147,25 @@
             pltpu.VMEM((SLOTS, block, width), jnp.bfloat16),
             pltpu.SemaphoreType.DMA((SLOTS,)),
         ],
-        compiler_params=pltpu.CompilerParams(vmem_limit_bytes=40 * MIB),
+        compiler_params=pltpu.CompilerParams(vmem_limit_bytes=39 * MIB),
         cost_estimate=pl.CostEstimate(flops=HINT, bytes_accessed=HINT, transcendentals=0),
     )(*pieces, weight)
 
 
 def input_kernel(rows, cols, start, block, *refs):
-    pieces, gate_weight, up_weight = refs[:rows], refs[rows], refs[rows + 1]
-    outs, (left, right, buffer, sems) = refs[rows + 2 : -4], refs[-4:]
+    refs, (buffer, sems) = refs[:-2], refs[-2:]
+    given = len(refs) - 2 - cols
+    whole = given == 2
+    if whole:
+        (left, right), refs = refs[:2], refs[2:]
+    else:
+        given -= 2
+        pieces, refs, (left, right) = refs[:given], refs[given:-2], refs[-2:]
+    (gate_weight, up_weight), outs = refs[:2], refs[2:]
     me, plane = lax.axis_index("row"), lax.axis_index("col")
     per_plane, half = rows // cols, rows // 2
-    step, depth = pieces[0].shape[1:]
+    depth = left.shape[1]
+    step = left.shape[0] // rows
     steps = outs[0].shape[1] // block
     count = per_plane * step
 
@@ -171,13 +179,32 @@
 
     for i in range(min(SLOTS, 2 * steps)):
         fetch(i % 2, i // 2).start()
-    for j, piece in enumerate(pieces):
+    places = []
+    for j in range(rows):
         core = (me + j // half) % 2
         owner = 2 * flipped(me // 2, core, j % half, half) + core
         distance = (owner // per_plane + cols - plane) % cols
-        place = pl.multiple_of((distance * per_plane + owner % per_plane) * step, step)
-        left[pl.ds(place, step), :] = piece[0]
-        right[pl.ds(place, step), :] = piece[1]
+        places.append(pl.multiple_of((distance * per_plane + owner % per_plane) * step, step))
+    if not whole and given == rows:
+        for piece, place in zip(pieces, places):
+            left[pl.ds(place, step), :] = piece[0]
+            right[pl.ds(place, step), :] = piece[1]
+    elif not whole:
+        some = block_of(depth, 512)
+
+        def activate(i, carry):
+            columns = pl.ds(pl.multiple_of(i * some, 128), some)
+            for hidden_grad, saved, place in zip(pieces[:rows], pieces[rows:], places):
+                gate_grad, up_grad = swiglu_back(
+                    hidden_grad[:, columns].astype(jnp.float32),
+                    saved[0, :, columns],
+                    saved[1, :, columns],
+                )
+                left[pl.ds(place, step), columns] = gate_grad
+                right[pl.ds(place, step), columns] = up_grad
+            return carry
+
+        lax.fori_loop(0, depth // some, activate, 0)
 
     def multiply(which, held, i):
         fetch(which, i).wait()
@@ -200,26 +227,30 @@
     lax.fori_loop(0, steps, body, 0)
 
 
-def input_partial(rows, cols, pieces, gate_weight, up_weight, start, size):
-    _, step, depth = pieces[0].shape
+def input_partial(rows, cols, given, gate_weight, up_weight, start, size):
+    step, depth = given[0].shape[-2:]
+    if len(given) == 2:
+        step //= rows
     count = step * rows // cols
     block = block_of(size, 256)
     whole, anywhere = pl.BlockSpec(memory_space=pltpu.VMEM), pl.BlockSpec(memory_space=pl.ANY)
-    return pl.pallas_call(
+    outs = (jax.ShapeDtypeStruct((count, size), jnp.float32),)
+    outs += (jax.ShapeDtypeStruct((count, size), jnp.bfloat16),) * (cols - 1)
+    if len(given) > 2:
+        outs += (jax.ShapeDtypeStruct((rows * step, depth), jnp.bfloat16),) * 2
+    outs = pl.pallas_call(
         functools.partial(input_kernel, rows, cols, start, block),
-        out_shape=(jax.ShapeDtypeStruct((count, size), jnp.float32),)
-        + (jax.ShapeDtypeStruct((count, size), jnp.bfloat16),) * (cols - 1),
-        in_specs=[whole] * rows + [anywhere] * 2,
-        out_specs=(whole,) * cols,
+        out_shape=outs,
+        in_specs=[whole] * len(given) + [anywhere] * 2,
+        out_specs=(whole,) * len(outs),
         scratch_shapes=[
-            pltpu.VMEM((rows * step, depth), jnp.bfloat16),
-            pltpu.VMEM((rows * step, depth), jnp.bfloat16),
             pltpu.VMEM((SLOTS, block, depth), jnp.bfloat16),
             pltpu.SemaphoreType.DMA((SLOTS,)),
         ],
-        compiler_params=pltpu.CompilerParams(vmem_limit_bytes=40 * MIB),
+        compiler_params=pltpu.CompilerParams(vmem_limit_bytes=39 * MIB),
         cost_estimate=pl.CostEstimate(flops=HINT, bytes_accessed=HINT, transcendentals=0),
-    )(*pieces, gate_weight, up_weight)
+    )(*given, gate_weight, up_weight)
+    return outs[:cols], outs[cols:]
 
 
 class Chain:
@@ -286,14 +317,14 @@
             side.add()
             side.send()
 
-    def activate(t, sides):
+    def own_hidden(sides):
         for side in sides:
             side.add()
-        hidden_grad = jnp.concatenate([side.state[0] for side in sides], axis=1)
+        return jnp.concatenate([side.state[0] for side in sides], axis=1)
+
+    def saved(t):
         mine = slice(t * step, (t + 1) * step)
-        both = jnp.stack(swiglu_back(hidden_grad, gate_saved[mine], up_saved[mine]))
-        chain.end(both)
-        return [both]
+        return gate_saved[mine], up_saved[mine]
 
     def spread(pieces):
         j = len(pieces).bit_length() - 1
@@ -302,20 +333,19 @@
     def cross(pieces):
         return pieces + [swap(piece, rows) for piece in pieces]
 
-    def share_of(pieces, start, size):
-        pieces = [chain.begin(pieces[0])] + pieces[1:]
-        outs = input_partial(rows, cols, pieces, gate_weight, up_weight, start, size)
+    def share_of(given, start, size):
+        given = [chain.begin(given[0])] + list(given[1:])
+        outs, both = input_partial(rows, cols, given, gate_weight, up_weight, start, size)
         chain.end(outs[0])
-        return outs
+        return outs, both
 
     def start_sums(own, *sends):
         return [own] + [turn(send, cols, d) for d, send in enumerate(sends, 1)]
 
-    def finish_sums(own, *others):
+    def add_up(own, *others):
         own = chain.begin(own)
         for other in others:
             own = own + other.astype(jnp.float32)
-        own = own.astype(jnp.bfloat16)
         chain.end(own)
         return own
 
@@ -324,13 +354,23 @@
     later = after(later, near[1])
     far = [later] + [turn(later, cols, d) for d in range(1, cols)]
 
-    first = multiply(near, [0]) + multiply(near, [1])
+    known = [jnp.stack(saved(0))]
+    for _ in bits[1:]:
+        known = spread(known)
+    chain.end(*known[1:])
+    first = multiply(near, [0])
+    known = spread(known)
+    chain.last += known[1:]
+    first += multiply(near, [1])
+    known = cross(known)
     for side in first:
         side.pair()
+    chain.last += known[1:]
     for _ in bits[1:]:
         next_sums(first)
     second = multiply(far, [0])
-    first = activate(0, first)
+    first = [own_hidden(first).astype(jnp.bfloat16)]
+    chain.end(first[0])
     for _ in bits:
         first = spread(first)
     second += multiply(far, [1])
@@ -339,20 +379,24 @@
     for _ in bits[1:]:
         next_sums(second)
     chain.last += first[1:]
-    second = activate(1, second)
+    second = [jnp.stack(swiglu_back(own_hidden(second), *saved(1)))]
+    chain.end(second[0])
     for _ in bits[1:]:
         second = spread(second)
     first = cross(first)
-    sums = [share_of(first, 0, width // 2)]
+    sums, both = share_of(first + known, 0, width // 2)
     second = [chain.begin(piece) if j else piece for j, piece in enumerate(second)]
     second = spread(second)
-    sums.append(share_of(first, width // 2, width // 2))
-    sums = start_sums(*[jnp.concatenate(some, axis=1) for some in zip(*sums)])
+    rest, _ = share_of(both, width // 2, width // 2)
+    first = start_sums(*[jnp.concatenate(some, axis=1) for some in zip(sums, rest)])
     second = cross(second)
-    results = [start_sums(*share_of(second, 0, width // 2))]
-    first = finish_sums(*sums)
-    results.append(start_sums(*share_of(second, width // 2, width // 2)))
-    second = jnp.concatenate([finish_sums(*some) for some in results], axis=1)
+    sums, both = share_of(second, 0, width // 2)
+    second = [start_sums(*sums)]
+    first = [add_up(*first[:2])] + first[2:]
+    sums, _ = share_of(both, width // 2, width // 2)
+    first = add_up(*first).astype(jnp.bfloat16)
+    second.append(start_sums(*sums))
+    second = jnp.concatenate([add_up(*some).astype(jnp.bfloat16) for some in second], axis=1)
     results = [value.reshape(per_plane, step, width) for value in (first, second)]
     return jnp.stack(results, axis=1).reshape(out_grad.shape)
 

time: 218 us -> 210 us (0.963)
  waiting for transfers between devices: 90 us -> 70.4 us
  starting transfers between devices: 41.9 us -> 51.1 us
    ppermute x14 -> x17, waiting for transfers between devices: 52.3 us -> 38.9 us  [exchange(): lax.ppermute(value, 'row', [(i, i ^ 2 << (top - j if i & 1 else j)) for i...]
    ppermute x14 -> x17, starting transfers between devices: 11.5 us -> 21.6 us  [exchange(): lax.ppermute(value, 'row', [(i, i ^ 2 << (top - j if i & 1 else j)) for i...]
    ppermute x15, waiting for transfers between devices: 34.9 us -> 28.9 us  [turn(): lax.ppermute(value, 'col', [(i, (i + distance) % size) for i in range(siz...]
    ppermute x15, starting transfers between devices: 28.3 us -> 25.9 us  [turn(): lax.ppermute(value, 'col', [(i, (i + distance) % size) for i in range(siz...]
  transfers between devices with their start and end apart: 41 -> 48, of which waited for: 17 -> 19; matrix products, arithmetic and copies ran while one was open for 1% -> 1% of each run, Pallas kernels for 33% -> 38%
where the time goes in v3:
time: 210 us; the launch traced here: 209 us
  Pallas kernels  80.4 us (38%)
  waiting for transfers between devices  70.4 us (34%)
  starting transfers between devices  51.1 us (24%)
  local copies, waits for them, and re-layouts  4.21 us (2%)
  other arithmetic  2.38 us (1%)
    pallas_call x4, Pallas kernels, input_partial(): pl.pallas_call(functools.partial(input_kernel, rows, cols, start, block),...  50 us
    ppermute x17, waiting for transfers between devices, exchange(): lax.ppermute(value, 'row', [(i, i ^ 2 << (top - j if i & 1 else j)) for i...  38.9 us
    pallas_call x4, Pallas kernels, hidden_partial(): pl.pallas_call(functools.partial(hidden_kernel, rows, cols, starts, block...  30.4 us
    ppermute x15, waiting for transfers between devices, turn(): lax.ppermute(value, 'col', [(i, (i + distance) % size) for i in range(siz...  28.9 us
    ppermute x15, starting transfers between devices, turn(): lax.ppermute(value, 'col', [(i, (i + distance) % size) for i in range(siz...  25.9 us
    ppermute x17, starting transfers between devices, exchange(): lax.ppermute(value, 'row', [(i, i ^ 2 << (top - j if i & 1 else j)) for i...  21.6 us
  transfers between devices with their start and end apart: 48, of which 19 were waited for; matrix products, arithmetic and copies ran while one was open for 1% of the time, Pallas kernels for 38%

profile of v3, /device:TPU:0, one launch (start us, length us, event | category | flops | bytes accessed | tf_op | source)
XLA Modules:
  0.0 209.0 jit_solution(8849858809646308481)
XLA Ops:
  1.3 3.0 %collective-permute-start = (bf16[2,32,6656]{2,1,0:T(8,128)(2,1)S(1)}, bf16[2,32,6656]{2,1,0:T(8,128)(2,1)S(1)}, u32[]{:S(2)}, u32[]{:S(2)}) collective-permute-start(bf16[2,32,6656]{2,1,0:T(8,128)(2,1)S(1)} %pad_maximum_fusion.refs_8_), channel_id=1, source_target_pairs={{0,8},{4,20},{8,0},{12,28},{16,24},{20,4},{24,16},{28,12},{1,9},{5... | collective-permute-start | bytes 2555912 | tf_op jit(solution)/shard_map/ppermute | solution.py:39
  4.4 3.7 %collective-permute-start.3 = (bf16[64,2048]{1,0:T(8,128)(2,1)S(1)}, bf16[64,2048]{1,0:T(8,128)(2,1)S(1)}, u32[]{:S(2)}, u32[]{:S(2)}) collective-permute-start(bf16[64,2048]{1,0:T(8,128)(2,1)S(1)} %bitcast.31), channel_id=1, source_target_pairs={{0,3},{1,0},{2,1},{3,2},{4,7},{5,4},{6,5},{7,6},{8,11},{9,8},{10,9... | collective-permute-start | bytes 786440 | tf_op jit(solution)/shard_map/ppermute | solution.py:45
  10.6 9.0 %collective-permute-done.refs_9_ = bf16[2,32,6656]{2,1,0:T(8,128)(2,1)S(1)} collective-permute-done((bf16[2,32,6656]{2,1,0:T(8,128)(2,1)S(1)}, bf16[2,32,6656]{2,1,0:T(8,128)(2,1)S(1)}, u32[]{:S(2)}, u32[]{:S(2)}) %collective-permute-start) | collective-permute-done | bytes 852000 | tf_op jit(solution)/shard_map/ppermute | solution.py:39
  19.6 3.5 %collective-permute-start.6 = (bf16[2,32,6656]{2,1,0:T(8,128)(2,1)S(1)}, bf16[2,32,6656]{2,1,0:T(8,128)(2,1)S(1)}, u32[]{:S(2)}, u32[]{:S(2)}) collective-permute-start(bf16[2,32,6656]{2,1,0:T(8,128)(2,1)S(1)} %collective-permute-done.refs_9_), channel_id=1, source_target_pairs={{0,16},{4,12},{8,24},{12,4},{16,0},{20,28},{24,8},{28,20},{1,17},{... | collective-permute-start | bytes 2555912 | tf_op jit(solution)/shard_map/ppermute | solution.py:39
  23.2 7.0 %collective-permute-done.2.refs_2_ = bf16[64,2048]{1,0:T(8,128)(2,1)S(1)} collective-permute-done((bf16[64,2048]{1,0:T(8,128)(2,1)S(1)}, bf16[64,2048]{1,0:T(8,128)(2,1)S(1)}, u32[]{:S(2)}, u32[]{:S(2)}) %collective-permute-start.2) | collective-permute-done | bytes 262176 | tf_op jit(solution)/shard_map/ppermute | solution.py:45
  30.1 7.6 %shard_map.64 = (bf16[4,32,3328]{2,1,0:T(8,128)(2,1)S(1)}, f32[4,32,3328]{2,1,0:T(8,128)S(1)}) custom-call(bf16[64,2048]{1,0:T(8,128)(2,1)S(1)} %bitcast.34, bf16[64,2048]{1,0:T(8,128)(2,1)S(1)} %collective-permute-done.1.refs_1_, bf16[64,2048]{1,0:T(8,128)(2,1)S(1)} %collective-permute-done.2.refs_2_, bf16[64,2048]{1,0:T(8,128)(2,1)S(1)} %collective-permute-done.3.refs_3_, ...), custom_call_target="tpu_custom_call" | custom-call | flops 1024 | bytes 1024 | tf_op jit(solution)/shard_map/pallas_call | solution.py:136
  38.8 7.6 %shard_map.65 = (bf16[4,32,3328]{2,1,0:T(8,128)(2,1)S(1)}, f32[4,32,3328]{2,1,0:T(8,128)S(1)}) custom-call(bf16[64,2048]{1,0:T(8,128)(2,1)S(1)} %bitcast.35, bf16[64,2048]{1,0:T(8,128)(2,1)S(1)} %collective-permute-done.1.refs_1_, bf16[64,2048]{1,0:T(8,128)(2,1)S(1)} %collective-permute-done.2.refs_2_, bf16[64,2048]{1,0:T(8,128)(2,1)S(1)} %collective-permute-done.3.refs_3_, ...), custom_call_target="tpu_custom_call" | custom-call | flops 1024 | bytes 1024 | tf_op jit(solution)/shard_map/pallas_call | solution.py:136
  49.6 2.9 %collective-permute-start.16 = (bf16[64,2048]{1,0:T(8,128)(2,1)S(1)}, bf16[64,2048]{1,0:T(8,128)(2,1)S(1)}, u32[]{:S(2)}, u32[]{:S(2)}) collective-permute-start(bf16[64,2048]{1,0:T(8,128)(2,1)S(1)} %bitcast.27), channel_id=1, source_target_pairs={{0,2},{1,3},{2,0},{3,1},{4,6},{5,7},{6,4},{7,5},{8,10},{9,11},{10,... | collective-permute-start | bytes 786440 | tf_op jit(solution)/shard_map/ppermute | solution.py:45
  57.2 7.2 %collective-permute-done.14 = bf16[2,32,3328]{2,1,0:T(8,128)(2,1)S(1)} collective-permute-done((bf16[2,32,3328]{2,1,0:T(8,128)(2,1)S(1)}, bf16[2,32,3328]{2,1,0:T(8,128)(2,1)S(1)}, u32[]{:S(2)}, u32[]{:S(2)}) %collective-permute-start.14) | collective-permute-done | bytes 426016 | tf_op jit(solution)/shard_map/ppermute | solution.py:39
  66.0 10.0 %collective-permute-done.16.refs_2_ = bf16[64,2048]{1,0:T(8,128)(2,1)S(1)} collective-permute-done((bf16[64,2048]{1,0:T(8,128)(2,1)S(1)}, bf16[64,2048]{1,0:T(8,128)(2,1)S(1)}, u32[]{:S(2)}, u32[]{:S(2)}) %collective-permute-start.16) | collective-permute-done | bytes 262176 | tf_op jit(solution)/shard_map/ppermute | solution.py:45
  76.1 7.6 %shard_map.66 = (bf16[4,32,3328]{2,1,0:T(8,128)(2,1)S(1)}, f32[4,32,3328]{2,1,0:T(8,128)S(1)}) custom-call(bf16[64,2048]{1,0:T(8,128)(2,1)S(1)} %bitcast.29, bf16[64,2048]{1,0:T(8,128)(2,1)S(1)} %collective-permute-done.15.refs_1_, bf16[64,2048]{1,0:T(8,128)(2,1)S(1)} %collective-permute-done.16.refs_2_, ...), custom_call_target="tpu_custom_call" | custom-call | flops 1024 | bytes 1024 | tf_op jit(solution)/shard_map/pallas_call | solution.py:136
  86.0 7.6 %shard_map.67 = (bf16[4,32,3328]{2,1,0:T(8,128)(2,1)S(1)}, f32[4,32,3328]{2,1,0:T(8,128)S(1)}) custom-call(bf16[64,2048]{1,0:T(8,128)(2,1)S(1)} %bitcast.30, bf16[64,2048]{1,0:T(8,128)(2,1)S(1)} %collective-permute-done.15.refs_1_, bf16[64,2048]{1,0:T(8,128)(2,1)S(1)} %collective-permute-done.16.refs_2_, ...), custom_call_target="tpu_custom_call" | custom-call | flops 1024 | bytes 1024 | tf_op jit(solution)/shard_map/pallas_call | solution.py:136
  99.2 7.6 %collective-permute-done.20 = bf16[2,32,3328]{2,1,0:T(8,128)(2,1)S(1)} collective-permute-done((bf16[2,32,3328]{2,1,0:T(8,128)(2,1)S(1)}, bf16[2,32,3328]{2,1,0:T(8,128)(2,1)S(1)}, u32[]{:S(2)}, u32[]{:S(2)}) %collective-permute-start.20) | collective-permute-done | bytes 426016 | tf_op jit(solution)/shard_map/ppermute | solution.py:39
  107.6 4.8 %collective-permute-done.23 = bf16[2,32,3328]{2,1,0:T(8,128)(2,1)S(1)} collective-permute-done((bf16[2,32,3328]{2,1,0:T(8,128)(2,1)S(1)}, bf16[2,32,3328]{2,1,0:T(8,128)(2,1)S(1)}, u32[]{:S(2)}, u32[]{:S(2)}) %collective-permute-start.23) | collective-permute-done | bytes 426016 | tf_op jit(solution)/shard_map/ppermute | solution.py:39
  115.2 3.2 %collective-permute-done.27 = bf16[1,32,3328]{2,1,0:T(8,128)(2,1)S(1)} collective-permute-done((bf16[1,32,3328]{2,1,0:T(8,128)(2,1)S(1)}, bf16[1,32,3328]{2,1,0:T(8,128)(2,1)S(1)}, u32[]{:S(2)}, u32[]{:S(2)}) %collective-permute-start.27) | collective-permute-done | bytes 213024 | tf_op jit(solution)/shard_map/ppermute | solution.py:39
  125.1 13.4 %shard_map.68 = (f32[64,1024]{1,0:T(8,128)S(1)}, bf16[64,1024]{1,0:T(8,128)(2,1)S(1)}, bf16[64,1024]{1,0:T(8,128)(2,1)S(1)}, bf16[64,1024]{1,0:T(8,128)(2,1)S(1)...) custom-call(bf16[32,6656]{1,0:T(8,128)(2,1)S(1)} %pad_maximum_fusion.7.refs_0_, ...), custom_call_target="tpu_custom_call" | custom-call | flops 1024 | bytes 1024 | tf_op jit(solution)/shard_map/pallas_call | solution.py:241
  141.6 12.1 %shard_map.69 = (f32[64,1024]{1,0:T(8,128)S(1)}, bf16[64,1024]{1,0:T(8,128)(2,1)S(1)}, bf16[64,1024]{1,0:T(8,128)(2,1)S(1)}, bf16[64,1024]{1,0:T(8,128)(2,1)S(1)}) custom-call(bf16[256,6656]{1,0:T(8,128)(2,1)S(1)} %get-tuple-element.87.refs_0_, bf16[256,6656]{1,0:T(8,128)(2,1)S(1)} %copy-done, bf16[2048,6656]{1,0:T(8,128)(2,1)} %refs_2_.3, ...), custom_call_target="tpu_custom_call" | custom-call | flops 1024 | bytes 1024 | tf_op jit(solution)/shard_map/pallas_call | solution.py:241
  155.0 4.1 %collective-permute-start.41 = (bf16[64,2048]{1,0:T(8,128)(2,1)S(1)}, bf16[64,2048]{1,0:T(8,128)(2,1)S(1)}, u32[]{:S(2)}, u32[]{:S(2)}) collective-permute-start(bf16[64,2048]{1,0:T(8,128)(2,1)S(1)} %pad_maximum_fusion.12), channel_id=1, source_target_pairs={{0,3},{1,0},{2,1},{3,2},{4,7},{5,4},{6,5},{7,6},{8,11},{9,8},{10,9... | collective-permute-start | bytes 786440 | tf_op jit(solution)/shard_map/ppermute | solution.py:45
  159.1 12.3 %shard_map.70 = (f32[64,1024]{1,0:T(8,128)S(1)}, bf16[64,1024]{1,0:T(8,128)(2,1)S(1)}, bf16[64,1024]{1,0:T(8,128)(2,1)S(1)}, bf16[64,1024]{1,0:T(8,128)(2,1)S(1)...) custom-call(bf16[2,32,6656]{2,1,0:T(8,128)(2,1)S(1)} %pad_maximum_fusion.2.refs_0_, ...), custom_call_target="tpu_custom_call" | custom-call | flops 1024 | bytes 1024 | tf_op jit(solution)/shard_map/pallas_call | solution.py:241
  171.5 12.2 %shard_map.71 = (f32[64,1024]{1,0:T(8,128)S(1)}, bf16[64,1024]{1,0:T(8,128)(2,1)S(1)}, bf16[64,1024]{1,0:T(8,128)(2,1)S(1)}, bf16[64,1024]{1,0:T(8,128)(2,1)S(1)}) custom-call(bf16[256,6656]{1,0:T(8,128)(2,1)S(1)} %get-tuple-element.97.refs_0_, bf16[256,6656]{1,0:T(8,128)(2,1)S(1)} %get-tuple-element.98.refs_1_, bf16[2048,6656]{1,0:T(8,128)(2,1)} %refs_2_.3, ...), custom_call_target="tpu_custom_call" | custom-call | flops 1024 | bytes 1024 | tf_op jit(solution)/shard_map/pallas_call | solution.py:241
  184.4 3.9 %collective-permute-start.43 = (bf16[64,1024]{1,0:T(8,128)(2,1)S(1)}, bf16[64,1024]{1,0:T(8,128)(2,1)S(1)}, u32[]{:S(2)}, u32[]{:S(2)}) collective-permute-start(bf16[64,1024]{1,0:T(8,128)(2,1)S(1)} %get-tuple-element.107), channel_id=1, source_target_pairs={{0,2},{1,3},{2,0},{3,1},{4,6},{5,7},{6,4},{7,5},{8,10},{9,11},{10,... | collective-permute-start | bytes 393224 | tf_op jit(solution)/shard_map/ppermute | solution.py:45
  192.0 4.2 %collective-permute-start.47 = (bf16[64,1024]{1,0:T(8,128)(2,1)S(1)}, bf16[64,1024]{1,0:T(8,128)(2,1)S(1)}, u32[]{:S(2)}, u32[]{:S(2)}) collective-permute-start(bf16[64,1024]{1,0:T(8,128)(2,1)S(1)} %get-tuple-element.112), channel_id=1, source_target_pairs={{0,3},{1,0},{2,1},{3,2},{4,7},{5,4},{6,5},{7,6},{8,11},{9,8},{10,9... | collective-permute-start | bytes 393224 | tf_op jit(solution)/shard_map/ppermute | solution.py:45
  196.2 4.6 %collective-permute-done.43 = bf16[64,1024]{1,0:T(8,128)(2,1)S(1)} collective-permute-done((bf16[64,1024]{1,0:T(8,128)(2,1)S(1)}, bf16[64,1024]{1,0:T(8,128)(2,1)S(1)}, u32[]{:S(2)}, u32[]{:S(2)}) %collective-permute-start.43) | collective-permute-done | bytes 131104 | tf_op jit(solution)/shard_map/ppermute | solution.py:45
  201.1 6.9 %collective-permute-done.46 = bf16[64,1024]{1,0:T(8,128)(2,1)S(1)} collective-permute-done((bf16[64,1024]{1,0:T(8,128)(2,1)S(1)}, bf16[64,1024]{1,0:T(8,128)(2,1)S(1)}, u32[]{:S(2)}, u32[]{:S(2)}) %collective-permute-start.46) | collective-permute-done | bytes 131104 | tf_op jit(solution)/shard_map/ppermute | solution.py:45
  (125 shorter events, 42.6 us)
Async XLA Ops:
  1.3 18.3 %collective-permute-start = (bf16[2,32,6656]{2,1,0:T(8,128)(2,1)S(1)}, bf16[2,32,6656]{2,1,0:T(8,128)(2,1)S(1)}, u32[]{:S(2)}, u32[]{:S(2)}) collective-permute-start(bf16[2,32,6656]{2,1,0:T(8,128)(2,1)S(1)} %pad_maximum_fusion.refs_8_), channel_id=1, source_target_pairs={{0,8},{4,20},{8,0},{12,28},{16,24},{20,4},{24,16},{28,12},{1,9},{5... | collective-permute-start | bytes 2555912 | tf_op jit(solution)/shard_map/ppermute | solution.py:39
  4.4 18.8 %collective-permute-start.3 = (bf16[64,2048]{1,0:T(8,128)(2,1)S(1)}, bf16[64,2048]{1,0:T(8,128)(2,1)S(1)}, u32[]{:S(2)}, u32[]{:S(2)}) collective-permute-start(bf16[64,2048]{1,0:T(8,128)(2,1)S(1)} %bitcast.31), channel_id=1, source_target_pairs={{0,3},{1,0},{2,1},{3,2},{4,7},{5,4},{6,5},{7,6},{8,11},{9,8},{10,9... | collective-permute-start | bytes 786440 | tf_op jit(solution)/shard_map/ppermute | solution.py:45
  8.1 22.1 %collective-permute-start.2 = (bf16[64,2048]{1,0:T(8,128)(2,1)S(1)}, bf16[64,2048]{1,0:T(8,128)(2,1)S(1)}, u32[]{:S(2)}, u32[]{:S(2)}) collective-permute-start(bf16[64,2048]{1,0:T(8,128)(2,1)S(1)} %bitcast.32), channel_id=1, source_target_pairs={{0,2},{1,3},{2,0},{3,1},{4,6},{5,7},{6,4},{7,5},{8,10},{9,11},{10,... | collective-permute-start | bytes 786440 | tf_op jit(solution)/shard_map/ppermute | solution.py:45
  8.1 22.1 %collective-permute-start.1 = (bf16[64,2048]{1,0:T(8,128)(2,1)S(1)}, bf16[64,2048]{1,0:T(8,128)(2,1)S(1)}, u32[]{:S(2)}, u32[]{:S(2)}) collective-permute-start(bf16[64,2048]{1,0:T(8,128)(2,1)S(1)} %bitcast.33), channel_id=1, source_target_pairs={{0,1},{1,2},{2,3},{3,0},{4,5},{5,6},{6,7},{7,4},{8,9},{9,10},{10,1... | collective-permute-start | bytes 786440 | tf_op jit(solution)/shard_map/ppermute | solution.py:45
  9.1 29.3 %collective-permute-start.5 = (bf16[2,32,6656]{2,1,0:T(8,128)(2,1)S(1)}, bf16[2,32,6656]{2,1,0:T(8,128)(2,1)S(1)}, u32[]{:S(2)}, u32[]{:S(2)}) collective-permute-start(bf16[2,32,6656]{2,1,0:T(8,128)(2,1)S(1)} %pad_maximum_fusion.refs_8_), channel_id=1, source_target_pairs={{0,16},{4,12},{8,24},{12,4},{16,0},{20,28},{24,8},{28,20},{1,17},{... | collective-permute-start | bytes 2555912 | tf_op jit(solution)/shard_map/ppermute | solution.py:39
  19.6 19.2 %collective-permute-start.6 = (bf16[2,32,6656]{2,1,0:T(8,128)(2,1)S(1)}, bf16[2,32,6656]{2,1,0:T(8,128)(2,1)S(1)}, u32[]{:S(2)}, u32[]{:S(2)}) collective-permute-start(bf16[2,32,6656]{2,1,0:T(8,128)(2,1)S(1)} %collective-permute-done.refs_9_), channel_id=1, source_target_pairs={{0,16},{4,12},{8,24},{12,4},{16,0},{20,28},{24,8},{28,20},{1,17},{... | collective-permute-start | bytes 2555912 | tf_op jit(solution)/shard_map/ppermute | solution.py:39
  38.3 14.2 %collective-permute-start.10 = (bf16[2,32,6656]{2,1,0:T(8,128)(2,1)S(1)}, bf16[2,32,6656]{2,1,0:T(8,128)(2,1)S(1)}, u32[]{:S(2)}, u32[]{:S(2)}) collective-permute-start(bf16[2,32,6656]{2,1,0:T(8,128)(2,1)S(1)} %collective-permute-done.refs_9_), channel_id=1, source_target_pairs={{0,4},{4,0},{8,12},{12,8},{16,20},{20,16},{24,28},{28,24},{1,5},{5... | collective-permute-start | bytes 2555912 | tf_op jit(solution)/shard_map/ppermute | solution.py:34
  49.5 16.5 %collective-permute-start.17 = (bf16[64,2048]{1,0:T(8,128)(2,1)S(1)}, bf16[64,2048]{1,0:T(8,128)(2,1)S(1)}, u32[]{:S(2)}, u32[]{:S(2)}) collective-permute-start(bf16[64,2048]{1,0:T(8,128)(2,1)S(1)} %bitcast.26), channel_id=1, source_target_pairs={{0,3},{1,0},{2,1},{3,2},{4,7},{5,4},{6,5},{7,6},{8,11},{9,8},{10,9... | collective-permute-start | bytes 786440 | tf_op jit(solution)/shard_map/ppermute | solution.py:45
  49.6 26.5 %collective-permute-start.16 = (bf16[64,2048]{1,0:T(8,128)(2,1)S(1)}, bf16[64,2048]{1,0:T(8,128)(2,1)S(1)}, u32[]{:S(2)}, u32[]{:S(2)}) collective-permute-start(bf16[64,2048]{1,0:T(8,128)(2,1)S(1)} %bitcast.27), channel_id=1, source_target_pairs={{0,2},{1,3},{2,0},{3,1},{4,6},{5,7},{6,4},{7,5},{8,10},{9,11},{10,... | collective-permute-start | bytes 786440 | tf_op jit(solution)/shard_map/ppermute | solution.py:45
  52.5 23.6 %collective-permute-start.15 = (bf16[64,2048]{1,0:T(8,128)(2,1)S(1)}, bf16[64,2048]{1,0:T(8,128)(2,1)S(1)}, u32[]{:S(2)}, u32[]{:S(2)}) collective-permute-start(bf16[64,2048]{1,0:T(8,128)(2,1)S(1)} %bitcast.28), channel_id=1, source_target_pairs={{0,1},{1,2},{2,3},{3,0},{4,5},{5,6},{6,7},{7,4},{8,9},{9,10},{10,1... | collective-permute-start | bytes 786440 | tf_op jit(solution)/shard_map/ppermute | solution.py:45
  56.6 27.1 %collective-permute-start.13 = (bf16[1,32,3328]{2,1,0:T(8,128)(2,1)S(1)}, bf16[1,32,3328]{2,1,0:T(8,128)(2,1)S(1)}, u32[]{:S(2)}, u32[]{:S(2)}) collective-permute-start(bf16[1,32,3328]{2,1,0:T(8,128)(2,1)S(1)} %fusion.17), channel_id=1, source_target_pairs={{0,16},{4,12},{8,24},{12,4},{16,0},{20,28},{24,8},{28,20},{1,17},{... | collective-permute-start | bytes 638984 | tf_op jit(solution)/shard_map/ppermute | solution.py:39
  64.5 19.4 %collective-permute-start.18 = (bf16[1,32,3328]{2,1,0:T(8,128)(2,1)S(1)}, bf16[1,32,3328]{2,1,0:T(8,128)(2,1)S(1)}, u32[]{:S(2)}, u32[]{:S(2)}) collective-permute-start(bf16[1,32,3328]{2,1,0:T(8,128)(2,1)S(1)} %fusion.16), channel_id=1, source_target_pairs={{0,16},{4,12},{8,24},{12,4},{16,0},{20,28},{24,8},{28,20},{1,17},{... | collective-permute-start | bytes 638984 | tf_op jit(solution)/shard_map/ppermute | solution.py:39
  85.5 27.1 %collective-permute-start.25 = (bf16[32,6656]{1,0:T(8,128)(2,1)S(1)}, bf16[32,6656]{1,0:T(8,128)(2,1)S(1)}, u32[]{:S(2)}, u32[]{:S(2)}) collective-permute-start(bf16[32,6656]{1,0:T(8,128)(2,1)S(1)} %pad_maximum_fusion.7.refs_0_), channel_id=1, source_target_pairs={{0,16},{4,12},{8,24},{12,4},{16,0},{20,28},{24,8},{28,20},{1,17},{... | collective-permute-start | bytes 1277960 | tf_op jit(solution)/shard_map/ppermute | solution.py:39
  96.5 16.2 %collective-permute-start.26 = (bf16[32,6656]{1,0:T(8,128)(2,1)S(1)}, bf16[32,6656]{1,0:T(8,128)(2,1)S(1)}, u32[]{:S(2)}, u32[]{:S(2)}) collective-permute-start(bf16[32,6656]{1,0:T(8,128)(2,1)S(1)} %collective-permute-done.24.refs_1_), channel_id=1, source_target_pairs={{0,16},{4,12},{8,24},{12,4},{16,0},{20,28},{24,8},{28,20},{1,17},{... | collective-permute-start | bytes 1277960 | tf_op jit(solution)/shard_map/ppermute | solution.py:39
  119.0 20.6 %collective-permute-start.32 = (bf16[2,32,6656]{2,1,0:T(8,128)(2,1)S(1)}, bf16[2,32,6656]{2,1,0:T(8,128)(2,1)S(1)}, u32[]{:S(2)}, u32[]{:S(2)}) collective-permute-start(bf16[2,32,6656]{2,1,0:T(8,128)(2,1)S(1)} %pad_maximum_fusion.2.refs_0_), channel_id=1, source_target_pairs={{0,8},{4,20},{8,0},{12,28},{16,24},{20,4},{24,16},{28,12},{1,9},{5... | collective-permute-start | bytes 2555912 | tf_op jit(solution)/shard_map/ppermute | solution.py:39
  123.3 31.0 %collective-permute-start.33 = (bf16[2,32,6656]{2,1,0:T(8,128)(2,1)S(1)}, bf16[2,32,6656]{2,1,0:T(8,128)(2,1)S(1)}, u32[]{:S(2)}, u32[]{:S(2)}) collective-permute-start(bf16[2,32,6656]{2,1,0:T(8,128)(2,1)S(1)} %pad_maximum_fusion.2.refs_0_), channel_id=1, source_target_pairs={{0,16},{4,12},{8,24},{12,4},{16,0},{20,28},{24,8},{28,20},{1,17},{... | collective-permute-start | bytes 2555912 | tf_op jit(solution)/shard_map/ppermute | solution.py:39
  139.6 14.8 %collective-permute-start.34 = (bf16[2,32,6656]{2,1,0:T(8,128)(2,1)S(1)}, bf16[2,32,6656]{2,1,0:T(8,128)(2,1)S(1)}, u32[]{:S(2)}, u32[]{:S(2)}) collective-permute-start(bf16[2,32,6656]{2,1,0:T(8,128)(2,1)S(1)} %collective-permute-done.32.refs_1_), channel_id=1, source_target_pairs={{0,16},{4,12},{8,24},{12,4},{16,0},{20,28},{24,8},{28,20},{1,17},{... | collective-permute-start | bytes 2555912 | tf_op jit(solution)/shard_map/ppermute | solution.py:39
  139.6 15.4 %collective-permute-start.35 = (bf16[2,32,6656]{2,1,0:T(8,128)(2,1)S(1)}, bf16[2,32,6656]{2,1,0:T(8,128)(2,1)S(1)}, u32[]{:S(2)}, u32[]{:S(2)}) collective-permute-start(bf16[2,32,6656]{2,1,0:T(8,128)(2,1)S(1)} %pad_maximum_fusion.2.refs_0_), channel_id=1, source_target_pairs={{0,4},{4,0},{8,12},{12,8},{16,20},{20,16},{24,28},{28,24},{1,5},{5... | collective-permute-start | bytes 2555912 | tf_op jit(solution)/shard_map/ppermute | solution.py:34
  154.8 16.6 %collective-permute-start.39 = (bf16[64,2048]{1,0:T(8,128)(2,1)S(1)}, bf16[64,2048]{1,0:T(8,128)(2,1)S(1)}, u32[]{:S(2)}, u32[]{:S(2)}) collective-permute-start(bf16[64,2048]{1,0:T(8,128)(2,1)S(1)} %pad_maximum_fusion.10), channel_id=1, source_target_pairs={{0,1},{1,2},{2,3},{3,0},{4,5},{5,6},{6,7},{7,4},{8,9},{9,10},{10,1... | collective-permute-start | bytes 786440 | tf_op jit(solution)/shard_map/ppermute | solution.py:45
  155.0 36.1 %collective-permute-start.41 = (bf16[64,2048]{1,0:T(8,128)(2,1)S(1)}, bf16[64,2048]{1,0:T(8,128)(2,1)S(1)}, u32[]{:S(2)}, u32[]{:S(2)}) collective-permute-start(bf16[64,2048]{1,0:T(8,128)(2,1)S(1)} %pad_maximum_fusion.12), channel_id=1, source_target_pairs={{0,3},{1,0},{2,1},{3,2},{4,7},{5,4},{6,5},{7,6},{8,11},{9,8},{10,9... | collective-permute-start | bytes 786440 | tf_op jit(solution)/shard_map/ppermute | solution.py:45
  159.1 32.0 %collective-permute-start.40 = (bf16[64,2048]{1,0:T(8,128)(2,1)S(1)}, bf16[64,2048]{1,0:T(8,128)(2,1)S(1)}, u32[]{:S(2)}, u32[]{:S(2)}) collective-permute-start(bf16[64,2048]{1,0:T(8,128)(2,1)S(1)} %pad_maximum_fusion.11), channel_id=1, source_target_pairs={{0,2},{1,3},{2,0},{3,1},{4,6},{5,7},{6,4},{7,5},{8,10},{9,11},{10,... | collective-permute-start | bytes 786440 | tf_op jit(solution)/shard_map/ppermute | solution.py:45
  184.4 16.4 %collective-permute-start.43 = (bf16[64,1024]{1,0:T(8,128)(2,1)S(1)}, bf16[64,1024]{1,0:T(8,128)(2,1)S(1)}, u32[]{:S(2)}, u32[]{:S(2)}) collective-permute-start(bf16[64,1024]{1,0:T(8,128)(2,1)S(1)} %get-tuple-element.107), channel_id=1, source_target_pairs={{0,2},{1,3},{2,0},{3,1},{4,6},{5,7},{6,4},{7,5},{8,10},{9,11},{10,... | collective-permute-start | bytes 393224 | tf_op jit(solution)/shard_map/ppermute | solution.py:45
  191.2 16.7 %collective-permute-start.46 = (bf16[64,1024]{1,0:T(8,128)(2,1)S(1)}, bf16[64,1024]{1,0:T(8,128)(2,1)S(1)}, u32[]{:S(2)}, u32[]{:S(2)}) collective-permute-start(bf16[64,1024]{1,0:T(8,128)(2,1)S(1)} %get-tuple-element.111), channel_id=1, source_target_pairs={{0,2},{1,3},{2,0},{3,1},{4,6},{5,7},{6,4},{7,5},{8,10},{9,11},{10,... | collective-permute-start | bytes 393224 | tf_op jit(solution)/shard_map/ppermute | solution.py:45
  192.0 16.0 %collective-permute-start.47 = (bf16[64,1024]{1,0:T(8,128)(2,1)S(1)}, bf16[64,1024]{1,0:T(8,128)(2,1)S(1)}, u32[]{:S(2)}, u32[]{:S(2)}) collective-permute-start(bf16[64,1024]{1,0:T(8,128)(2,1)S(1)} %get-tuple-element.112), channel_id=1, source_target_pairs={{0,3},{1,0},{2,1},{3,2},{4,7},{5,4},{6,5},{7,6},{8,11},{9,8},{10,9... | collective-permute-start | bytes 393224 | tf_op jit(solution)/shard_map/ppermute | solution.py:45
  (28 other events, 200.8 us)

commit v4 on v3

--- a/solution.py
+++ b/solution.py
@@ -247,7 +247,7 @@
             pltpu.VMEM((SLOTS, block, depth), jnp.bfloat16),
             pltpu.SemaphoreType.DMA((SLOTS,)),
         ],
-        compiler_params=pltpu.CompilerParams(vmem_limit_bytes=39 * MIB),
+        compiler_params=pltpu.CompilerParams(vmem_limit_bytes=30 * MIB),
         cost_estimate=pl.CostEstimate(flops=HINT, bytes_accessed=HINT, transcendentals=0),
     )(*given, gate_weight, up_weight)
     return outs[:cols], outs[cols:]
@@ -390,13 +390,9 @@
     rest, _ = share_of(both, width // 2, width // 2)
     first = start_sums(*[jnp.concatenate(some, axis=1) for some in zip(sums, rest)])
     second = cross(second)
-    sums, both = share_of(second, 0, width // 2)
-    second = [start_sums(*sums)]
-    first = [add_up(*first[:2])] + first[2:]
-    sums, _ = share_of(both, width // 2, width // 2)
+    sums, _ = share_of(second, 0, width)
     first = add_up(*first).astype(jnp.bfloat16)
-    second.append(start_sums(*sums))
-    second = jnp.concatenate([add_up(*some).astype(jnp.bfloat16) for some in second], axis=1)
+    second = add_up(*start_sums(*sums)).astype(jnp.bfloat16)
     results = [value.reshape(per_plane, step, width) for value in (first, second)]
     return jnp.stack(results, axis=1).reshape(out_grad.shape)
 

time: 210 us -> 206 us (0.981)
  starting transfers between devices: 51.1 us -> 41.7 us
  waiting for transfers between devices: 70.4 us -> 77.8 us
    ppermute x15 -> x12, starting transfers between devices: 25.9 us -> 16.9 us  [turn(): lax.ppermute(value, 'col', [(i, (i + distance) % size) for i in range(siz...]
    ppermute x15 -> x12, waiting for transfers between devices: 28.9 us -> 33.6 us  [turn(): lax.ppermute(value, 'col', [(i, (i + distance) % size) for i in range(siz...]
    pallas_call x4 -> x3, Pallas kernels: 50 us -> 48.8 us  [input_partial(): pl.pallas_call(functools.partial(input_kernel, rows, cols, start, block),...]
  transfers between devices with their start and end apart: 48 -> 45, of which waited for: 19 -> 19; matrix products, arithmetic and copies ran while one was open for 1% -> 1% of each run, Pallas kernels for 38% -> 39%
where the time goes in v4:
time: 206 us; the launch traced here: 204 us
  Pallas kernels  79.2 us (38%)
  waiting for transfers between devices  77.8 us (38%)
  starting transfers between devices  41.7 us (20%)
  other arithmetic  2.33 us (1%)
  local copies, waits for them, and re-layouts  2.25 us (1%)
    pallas_call x3, Pallas kernels, input_partial(): pl.pallas_call(functools.partial(input_kernel, rows, cols, start, block),...  48.8 us
    ppermute x17, waiting for transfers between devices, exchange(): lax.ppermute(value, 'row', [(i, i ^ 2 << (top - j if i & 1 else j)) for i...  40.9 us
    ppermute x12, waiting for transfers between devices, turn(): lax.ppermute(value, 'col', [(i, (i + distance) % size) for i in range(siz...  33.6 us
    pallas_call x4, Pallas kernels, hidden_partial(): pl.pallas_call(functools.partial(hidden_kernel, rows, cols, starts, block...  30.4 us
    ppermute x17, starting transfers between devices, exchange(): lax.ppermute(value, 'row', [(i, i ^ 2 << (top - j if i & 1 else j)) for i...  21.6 us
    ppermute x12, starting transfers between devices, turn(): lax.ppermute(value, 'col', [(i, (i + distance) % size) for i in range(siz...  16.9 us
  transfers between devices with their start and end apart: 45, of which 19 were waited for; matrix products, arithmetic and copies ran while one was open for 1% of the time, Pallas kernels for 39%

profile of v4, /device:TPU:0, one launch (start us, length us, event | category | flops | bytes accessed | tf_op | source)
XLA Modules:
  0.0 203.7 jit_solution(8771577988563330238)
XLA Ops:
  1.3 3.0 %collective-permute-start = (bf16[2,32,6656]{2,1,0:T(8,128)(2,1)S(1)}, bf16[2,32,6656]{2,1,0:T(8,128)(2,1)S(1)}, u32[]{:S(2)}, u32[]{:S(2)}) collective-permute-start(bf16[2,32,6656]{2,1,0:T(8,128)(2,1)S(1)} %pad_maximum_fusion.refs_8_), channel_id=1, source_target_pairs={{0,8},{4,20},{8,0},{12,28},{16,24},{20,4},{24,16},{28,12},{1,9},{5... | collective-permute-start | bytes 2555912 | tf_op jit(solution)/shard_map/ppermute | solution.py:39
  4.4 3.7 %collective-permute-start.3 = (bf16[64,2048]{1,0:T(8,128)(2,1)S(1)}, bf16[64,2048]{1,0:T(8,128)(2,1)S(1)}, u32[]{:S(2)}, u32[]{:S(2)}) collective-permute-start(bf16[64,2048]{1,0:T(8,128)(2,1)S(1)} %bitcast.31), channel_id=1, source_target_pairs={{0,3},{1,0},{2,1},{3,2},{4,7},{5,4},{6,5},{7,6},{8,11},{9,8},{10,9... | collective-permute-start | bytes 786440 | tf_op jit(solution)/shard_map/ppermute | solution.py:45
  10.6 9.0 %collective-permute-done.refs_9_ = bf16[2,32,6656]{2,1,0:T(8,128)(2,1)S(1)} collective-permute-done((bf16[2,32,6656]{2,1,0:T(8,128)(2,1)S(1)}, bf16[2,32,6656]{2,1,0:T(8,128)(2,1)S(1)}, u32[]{:S(2)}, u32[]{:S(2)}) %collective-permute-start) | collective-permute-done | bytes 852000 | tf_op jit(solution)/shard_map/ppermute | solution.py:39
  19.6 3.5 %collective-permute-start.6 = (bf16[2,32,6656]{2,1,0:T(8,128)(2,1)S(1)}, bf16[2,32,6656]{2,1,0:T(8,128)(2,1)S(1)}, u32[]{:S(2)}, u32[]{:S(2)}) collective-permute-start(bf16[2,32,6656]{2,1,0:T(8,128)(2,1)S(1)} %collective-permute-done.refs_9_), channel_id=1, source_target_pairs={{0,16},{4,12},{8,24},{12,4},{16,0},{20,28},{24,8},{28,20},{1,17},{... | collective-permute-start | bytes 2555912 | tf_op jit(solution)/shard_map/ppermute | solution.py:39
  23.2 7.0 %collective-permute-done.2.refs_2_ = bf16[64,2048]{1,0:T(8,128)(2,1)S(1)} collective-permute-done((bf16[64,2048]{1,0:T(8,128)(2,1)S(1)}, bf16[64,2048]{1,0:T(8,128)(2,1)S(1)}, u32[]{:S(2)}, u32[]{:S(2)}) %collective-permute-start.2) | collective-permute-done | bytes 262176 | tf_op jit(solution)/shard_map/ppermute | solution.py:45
  30.1 7.6 %shard_map.64 = (bf16[4,32,3328]{2,1,0:T(8,128)(2,1)S(1)}, f32[4,32,3328]{2,1,0:T(8,128)S(1)}) custom-call(bf16[64,2048]{1,0:T(8,128)(2,1)S(1)} %bitcast.34, bf16[64,2048]{1,0:T(8,128)(2,1)S(1)} %collective-permute-done.1.refs_1_, bf16[64,2048]{1,0:T(8,128)(2,1)S(1)} %collective-permute-done.2.refs_2_, bf16[64,2048]{1,0:T(8,128)(2,1)S(1)} %collective-permute-done.3.refs_3_, ...), custom_call_target="tpu_custom_call" | custom-call | flops 1024 | bytes 1024 | tf_op jit(solution)/shard_map/pallas_call | solution.py:136
  38.8 7.6 %shard_map.65 = (bf16[4,32,3328]{2,1,0:T(8,128)(2,1)S(1)}, f32[4,32,3328]{2,1,0:T(8,128)S(1)}) custom-call(bf16[64,2048]{1,0:T(8,128)(2,1)S(1)} %bitcast.35, bf16[64,2048]{1,0:T(8,128)(2,1)S(1)} %collective-permute-done.1.refs_1_, bf16[64,2048]{1,0:T(8,128)(2,1)S(1)} %collective-permute-done.2.refs_2_, bf16[64,2048]{1,0:T(8,128)(2,1)S(1)} %collective-permute-done.3.refs_3_, ...), custom_call_target="tpu_custom_call" | custom-call | flops 1024 | bytes 1024 | tf_op jit(solution)/shard_map/pallas_call | solution.py:136
  49.6 2.9 %collective-permute-start.16 = (bf16[64,2048]{1,0:T(8,128)(2,1)S(1)}, bf16[64,2048]{1,0:T(8,128)(2,1)S(1)}, u32[]{:S(2)}, u32[]{:S(2)}) collective-permute-start(bf16[64,2048]{1,0:T(8,128)(2,1)S(1)} %bitcast.27), channel_id=1, source_target_pairs={{0,2},{1,3},{2,0},{3,1},{4,6},{5,7},{6,4},{7,5},{8,10},{9,11},{10,... | collective-permute-start | bytes 786440 | tf_op jit(solution)/shard_map/ppermute | solution.py:45
  57.2 7.2 %collective-permute-done.14 = bf16[2,32,3328]{2,1,0:T(8,128)(2,1)S(1)} collective-permute-done((bf16[2,32,3328]{2,1,0:T(8,128)(2,1)S(1)}, bf16[2,32,3328]{2,1,0:T(8,128)(2,1)S(1)}, u32[]{:S(2)}, u32[]{:S(2)}) %collective-permute-start.14) | collective-permute-done | bytes 426016 | tf_op jit(solution)/shard_map/ppermute | solution.py:39
  66.0 10.0 %collective-permute-done.16.refs_2_ = bf16[64,2048]{1,0:T(8,128)(2,1)S(1)} collective-permute-done((bf16[64,2048]{1,0:T(8,128)(2,1)S(1)}, bf16[64,2048]{1,0:T(8,128)(2,1)S(1)}, u32[]{:S(2)}, u32[]{:S(2)}) %collective-permute-start.16) | collective-permute-done | bytes 262176 | tf_op jit(solution)/shard_map/ppermute | solution.py:45
  76.1 7.6 %shard_map.66 = (bf16[4,32,3328]{2,1,0:T(8,128)(2,1)S(1)}, f32[4,32,3328]{2,1,0:T(8,128)S(1)}) custom-call(bf16[64,2048]{1,0:T(8,128)(2,1)S(1)} %bitcast.29, bf16[64,2048]{1,0:T(8,128)(2,1)S(1)} %collective-permute-done.15.refs_1_, bf16[64,2048]{1,0:T(8,128)(2,1)S(1)} %collective-permute-done.16.refs_2_, ...), custom_call_target="tpu_custom_call" | custom-call | flops 1024 | bytes 1024 | tf_op jit(solution)/shard_map/pallas_call | solution.py:136
  86.0 7.6 %shard_map.67 = (bf16[4,32,3328]{2,1,0:T(8,128)(2,1)S(1)}, f32[4,32,3328]{2,1,0:T(8,128)S(1)}) custom-call(bf16[64,2048]{1,0:T(8,128)(2,1)S(1)} %bitcast.30, bf16[64,2048]{1,0:T(8,128)(2,1)S(1)} %collective-permute-done.15.refs_1_, bf16[64,2048]{1,0:T(8,128)(2,1)S(1)} %collective-permute-done.16.refs_2_, ...), custom_call_target="tpu_custom_call" | custom-call | flops 1024 | bytes 1024 | tf_op jit(solution)/shard_map/pallas_call | solution.py:136
  93.7 2.7 %collective-permute-done.24.refs_1_ = bf16[32,6656]{1,0:T(8,128)(2,1)S(1)} collective-permute-done((bf16[32,6656]{1,0:T(8,128)(2,1)S(1)}, bf16[32,6656]{1,0:T(8,128)(2,1)S(1)}, u32[]{:S(2)}, u32[]{:S(2)}) %collective-permute-start.24) | collective-permute-done | bytes 426016 | tf_op jit(solution)/shard_map/ppermute | solution.py:39
  99.2 7.6 %collective-permute-done.20 = bf16[2,32,3328]{2,1,0:T(8,128)(2,1)S(1)} collective-permute-done((bf16[2,32,3328]{2,1,0:T(8,128)(2,1)S(1)}, bf16[2,32,3328]{2,1,0:T(8,128)(2,1)S(1)}, u32[]{:S(2)}, u32[]{:S(2)}) %collective-permute-start.20) | collective-permute-done | bytes 426016 | tf_op jit(solution)/shard_map/ppermute | solution.py:39
  107.6 4.8 %collective-permute-done.23 = bf16[2,32,3328]{2,1,0:T(8,128)(2,1)S(1)} collective-permute-done((bf16[2,32,3328]{2,1,0:T(8,128)(2,1)S(1)}, bf16[2,32,3328]{2,1,0:T(8,128)(2,1)S(1)}, u32[]{:S(2)}, u32[]{:S(2)}) %collective-permute-start.23) | collective-permute-done | bytes 426016 | tf_op jit(solution)/shard_map/ppermute | solution.py:39
  112.6 2.5 %collective-permute-done.22 = bf16[1,32,3328]{2,1,0:T(8,128)(2,1)S(1)} collective-permute-done((bf16[1,32,3328]{2,1,0:T(8,128)(2,1)S(1)}, bf16[1,32,3328]{2,1,0:T(8,128)(2,1)S(1)}, u32[]{:S(2)}, u32[]{:S(2)}) %collective-permute-start.22) | collective-permute-done | bytes 213024 | tf_op jit(solution)/shard_map/ppermute | solution.py:39
  115.2 3.2 %collective-permute-done.27 = bf16[1,32,3328]{2,1,0:T(8,128)(2,1)S(1)} collective-permute-done((bf16[1,32,3328]{2,1,0:T(8,128)(2,1)S(1)}, bf16[1,32,3328]{2,1,0:T(8,128)(2,1)S(1)}, u32[]{:S(2)}, u32[]{:S(2)}) %collective-permute-start.27) | collective-permute-done | bytes 213024 | tf_op jit(solution)/shard_map/ppermute | solution.py:39
  119.0 2.5 %collective-permute-start.32 = (bf16[2,32,6656]{2,1,0:T(8,128)(2,1)S(1)}, bf16[2,32,6656]{2,1,0:T(8,128)(2,1)S(1)}, u32[]{:S(2)}, u32[]{:S(2)}) collective-permute-start(bf16[2,32,6656]{2,1,0:T(8,128)(2,1)S(1)} %pad_maximum_fusion.2.refs_0_), channel_id=1, source_target_pairs={{0,8},{4,20},{8,0},{12,28},{16,24},{20,4},{24,16},{28,12},{1,9},{5... | collective-permute-start | bytes 2555912 | tf_op jit(solution)/shard_map/ppermute | solution.py:39
  125.1 13.4 %shard_map.68 = (f32[64,1024]{1,0:T(8,128)S(1)}, bf16[64,1024]{1,0:T(8,128)(2,1)S(1)}, bf16[64,1024]{1,0:T(8,128)(2,1)S(1)}, bf16[64,1024]{1,0:T(8,128)(2,1)S(1)...) custom-call(bf16[32,6656]{1,0:T(8,128)(2,1)S(1)} %pad_maximum_fusion.7.refs_0_, ...), custom_call_target="tpu_custom_call" | custom-call | flops 1024 | bytes 1024 | tf_op jit(solution)/shard_map/pallas_call | solution.py:241
  141.6 12.1 %shard_map.69 = (f32[64,1024]{1,0:T(8,128)S(1)}, bf16[64,1024]{1,0:T(8,128)(2,1)S(1)}, bf16[64,1024]{1,0:T(8,128)(2,1)S(1)}, bf16[64,1024]{1,0:T(8,128)(2,1)S(1)}) custom-call(bf16[256,6656]{1,0:T(8,128)(2,1)S(1)} %get-tuple-element.78.refs_0_, bf16[256,6656]{1,0:T(8,128)(2,1)S(1)} %get-tuple-element.79.refs_1_, bf16[2048,6656]{1,0:T(8,128)(2,1)} %refs_8_.1, ...), custom_call_target="tpu_custom_call" | custom-call | flops 1024 | bytes 1024 | tf_op jit(solution)/shard_map/pallas_call | solution.py:241
  157.6 23.3 %shard_map.70 = (f32[64,2048]{1,0:T(8,128)S(1)}, bf16[64,2048]{1,0:T(8,128)(2,1)S(1)}, bf16[64,2048]{1,0:T(8,128)(2,1)S(1)}, bf16[64,2048]{1,0:T(8,128)(2,1)S(1)...) custom-call(bf16[2,32,6656]{2,1,0:T(8,128)(2,1)S(1)} %pad_maximum_fusion.2.refs_0_, ...), custom_call_target="tpu_custom_call" | custom-call | flops 1024 | bytes 1024 | tf_op jit(solution)/shard_map/pallas_call | solution.py:241
  183.1 2.8 %collective-permute-start.44 = (bf16[64,2048]{1,0:T(8,128)(2,1)S(1)}, bf16[64,2048]{1,0:T(8,128)(2,1)S(1)}, u32[]{:S(2)}, u32[]{:S(2)}) collective-permute-start(bf16[64,2048]{1,0:T(8,128)(2,1)S(1)} %get-tuple-element.94), channel_id=1, source_target_pairs={{0,3},{1,0},{2,1},{3,2},{4,7},{5,4},{6,5},{7,6},{8,11},{9,8},{10,9... | collective-permute-start | bytes 786440 | tf_op jit(solution)/shard_map/ppermute | solution.py:45
  186.1 5.9 %collective-permute-done.42 = bf16[64,2048]{1,0:T(8,128)(2,1)S(1)} collective-permute-done((bf16[64,2048]{1,0:T(8,128)(2,1)S(1)}, bf16[64,2048]{1,0:T(8,128)(2,1)S(1)}, u32[]{:S(2)}, u32[]{:S(2)}) %collective-permute-start.42) | collective-permute-done | bytes 262176 | tf_op jit(solution)/shard_map/ppermute | solution.py:45
  192.0 10.7 %collective-permute-done.43 = bf16[64,2048]{1,0:T(8,128)(2,1)S(1)} collective-permute-done((bf16[64,2048]{1,0:T(8,128)(2,1)S(1)}, bf16[64,2048]{1,0:T(8,128)(2,1)S(1)}, u32[]{:S(2)}, u32[]{:S(2)}) %collective-permute-start.43) | collective-permute-done | bytes 262176 | tf_op jit(solution)/shard_map/ppermute | solution.py:45
  (113 shorter events, 34.9 us)
Async XLA Ops:
  1.3 18.3 %collective-permute-start = (bf16[2,32,6656]{2,1,0:T(8,128)(2,1)S(1)}, bf16[2,32,6656]{2,1,0:T(8,128)(2,1)S(1)}, u32[]{:S(2)}, u32[]{:S(2)}) collective-permute-start(bf16[2,32,6656]{2,1,0:T(8,128)(2,1)S(1)} %pad_maximum_fusion.refs_8_), channel_id=1, source_target_pairs={{0,8},{4,20},{8,0},{12,28},{16,24},{20,4},{24,16},{28,12},{1,9},{5... | collective-permute-start | bytes 2555912 | tf_op jit(solution)/shard_map/ppermute | solution.py:39
  4.4 18.8 %collective-permute-start.3 = (bf16[64,2048]{1,0:T(8,128)(2,1)S(1)}, bf16[64,2048]{1,0:T(8,128)(2,1)S(1)}, u32[]{:S(2)}, u32[]{:S(2)}) collective-permute-start(bf16[64,2048]{1,0:T(8,128)(2,1)S(1)} %bitcast.31), channel_id=1, source_target_pairs={{0,3},{1,0},{2,1},{3,2},{4,7},{5,4},{6,5},{7,6},{8,11},{9,8},{10,9... | collective-permute-start | bytes 786440 | tf_op jit(solution)/shard_map/ppermute | solution.py:45
  8.1 22.1 %collective-permute-start.2 = (bf16[64,2048]{1,0:T(8,128)(2,1)S(1)}, bf16[64,2048]{1,0:T(8,128)(2,1)S(1)}, u32[]{:S(2)}, u32[]{:S(2)}) collective-permute-start(bf16[64,2048]{1,0:T(8,128)(2,1)S(1)} %bitcast.32), channel_id=1, source_target_pairs={{0,2},{1,3},{2,0},{3,1},{4,6},{5,7},{6,4},{7,5},{8,10},{9,11},{10,... | collective-permute-start | bytes 786440 | tf_op jit(solution)/shard_map/ppermute | solution.py:45
  8.1 22.1 %collective-permute-start.1 = (bf16[64,2048]{1,0:T(8,128)(2,1)S(1)}, bf16[64,2048]{1,0:T(8,128)(2,1)S(1)}, u32[]{:S(2)}, u32[]{:S(2)}) collective-permute-start(bf16[64,2048]{1,0:T(8,128)(2,1)S(1)} %bitcast.33), channel_id=1, source_target_pairs={{0,1},{1,2},{2,3},{3,0},{4,5},{5,6},{6,7},{7,4},{8,9},{9,10},{10,1... | collective-permute-start | bytes 786440 | tf_op jit(solution)/shard_map/ppermute | solution.py:45
  9.1 29.3 %collective-permute-start.5 = (bf16[2,32,6656]{2,1,0:T(8,128)(2,1)S(1)}, bf16[2,32,6656]{2,1,0:T(8,128)(2,1)S(1)}, u32[]{:S(2)}, u32[]{:S(2)}) collective-permute-start(bf16[2,32,6656]{2,1,0:T(8,128)(2,1)S(1)} %pad_maximum_fusion.refs_8_), channel_id=1, source_target_pairs={{0,16},{4,12},{8,24},{12,4},{16,0},{20,28},{24,8},{28,20},{1,17},{... | collective-permute-start | bytes 2555912 | tf_op jit(solution)/shard_map/ppermute | solution.py:39
  19.6 19.2 %collective-permute-start.6 = (bf16[2,32,6656]{2,1,0:T(8,128)(2,1)S(1)}, bf16[2,32,6656]{2,1,0:T(8,128)(2,1)S(1)}, u32[]{:S(2)}, u32[]{:S(2)}) collective-permute-start(bf16[2,32,6656]{2,1,0:T(8,128)(2,1)S(1)} %collective-permute-done.refs_9_), channel_id=1, source_target_pairs={{0,16},{4,12},{8,24},{12,4},{16,0},{20,28},{24,8},{28,20},{1,17},{... | collective-permute-start | bytes 2555912 | tf_op jit(solution)/shard_map/ppermute | solution.py:39
  38.3 14.2 %collective-permute-start.10 = (bf16[2,32,6656]{2,1,0:T(8,128)(2,1)S(1)}, bf16[2,32,6656]{2,1,0:T(8,128)(2,1)S(1)}, u32[]{:S(2)}, u32[]{:S(2)}) collective-permute-start(bf16[2,32,6656]{2,1,0:T(8,128)(2,1)S(1)} %collective-permute-done.refs_9_), channel_id=1, source_target_pairs={{0,4},{4,0},{8,12},{12,8},{16,20},{20,16},{24,28},{28,24},{1,5},{5... | collective-permute-start | bytes 2555912 | tf_op jit(solution)/shard_map/ppermute | solution.py:34
  49.5 16.5 %collective-permute-start.17 = (bf16[64,2048]{1,0:T(8,128)(2,1)S(1)}, bf16[64,2048]{1,0:T(8,128)(2,1)S(1)}, u32[]{:S(2)}, u32[]{:S(2)}) collective-permute-start(bf16[64,2048]{1,0:T(8,128)(2,1)S(1)} %bitcast.26), channel_id=1, source_target_pairs={{0,3},{1,0},{2,1},{3,2},{4,7},{5,4},{6,5},{7,6},{8,11},{9,8},{10,9... | collective-permute-start | bytes 786440 | tf_op jit(solution)/shard_map/ppermute | solution.py:45
  49.6 26.5 %collective-permute-start.16 = (bf16[64,2048]{1,0:T(8,128)(2,1)S(1)}, bf16[64,2048]{1,0:T(8,128)(2,1)S(1)}, u32[]{:S(2)}, u32[]{:S(2)}) collective-permute-start(bf16[64,2048]{1,0:T(8,128)(2,1)S(1)} %bitcast.27), channel_id=1, source_target_pairs={{0,2},{1,3},{2,0},{3,1},{4,6},{5,7},{6,4},{7,5},{8,10},{9,11},{10,... | collective-permute-start | bytes 786440 | tf_op jit(solution)/shard_map/ppermute | solution.py:45
  52.5 23.6 %collective-permute-start.15 = (bf16[64,2048]{1,0:T(8,128)(2,1)S(1)}, bf16[64,2048]{1,0:T(8,128)(2,1)S(1)}, u32[]{:S(2)}, u32[]{:S(2)}) collective-permute-start(bf16[64,2048]{1,0:T(8,128)(2,1)S(1)} %bitcast.28), channel_id=1, source_target_pairs={{0,1},{1,2},{2,3},{3,0},{4,5},{5,6},{6,7},{7,4},{8,9},{9,10},{10,1... | collective-permute-start | bytes 786440 | tf_op jit(solution)/shard_map/ppermute | solution.py:45
  56.6 27.1 %collective-permute-start.13 = (bf16[1,32,3328]{2,1,0:T(8,128)(2,1)S(1)}, bf16[1,32,3328]{2,1,0:T(8,128)(2,1)S(1)}, u32[]{:S(2)}, u32[]{:S(2)}) collective-permute-start(bf16[1,32,3328]{2,1,0:T(8,128)(2,1)S(1)} %fusion.17), channel_id=1, source_target_pairs={{0,16},{4,12},{8,24},{12,4},{16,0},{20,28},{24,8},{28,20},{1,17},{... | collective-permute-start | bytes 638984 | tf_op jit(solution)/shard_map/ppermute | solution.py:39
  64.5 19.4 %collective-permute-start.18 = (bf16[1,32,3328]{2,1,0:T(8,128)(2,1)S(1)}, bf16[1,32,3328]{2,1,0:T(8,128)(2,1)S(1)}, u32[]{:S(2)}, u32[]{:S(2)}) collective-permute-start(bf16[1,32,3328]{2,1,0:T(8,128)(2,1)S(1)} %fusion.16), channel_id=1, source_target_pairs={{0,16},{4,12},{8,24},{12,4},{16,0},{20,28},{24,8},{28,20},{1,17},{... | collective-permute-start | bytes 638984 | tf_op jit(solution)/shard_map/ppermute | solution.py:39
  85.5 27.1 %collective-permute-start.25 = (bf16[32,6656]{1,0:T(8,128)(2,1)S(1)}, bf16[32,6656]{1,0:T(8,128)(2,1)S(1)}, u32[]{:S(2)}, u32[]{:S(2)}) collective-permute-start(bf16[32,6656]{1,0:T(8,128)(2,1)S(1)} %pad_maximum_fusion.7.refs_0_), channel_id=1, source_target_pairs={{0,16},{4,12},{8,24},{12,4},{16,0},{20,28},{24,8},{28,20},{1,17},{... | collective-permute-start | bytes 1277960 | tf_op jit(solution)/shard_map/ppermute | solution.py:39
  96.5 16.2 %collective-permute-start.26 = (bf16[32,6656]{1,0:T(8,128)(2,1)S(1)}, bf16[32,6656]{1,0:T(8,128)(2,1)S(1)}, u32[]{:S(2)}, u32[]{:S(2)}) collective-permute-start(bf16[32,6656]{1,0:T(8,128)(2,1)S(1)} %collective-permute-done.24.refs_1_), channel_id=1, source_target_pairs={{0,16},{4,12},{8,24},{12,4},{16,0},{20,28},{24,8},{28,20},{1,17},{... | collective-permute-start | bytes 1277960 | tf_op jit(solution)/shard_map/ppermute | solution.py:39
  98.6 13.8 %collective-permute-start.23 = (bf16[2,32,3328]{2,1,0:T(8,128)(2,1)S(1)}, bf16[2,32,3328]{2,1,0:T(8,128)(2,1)S(1)}, u32[]{:S(2)}, u32[]{:S(2)}) collective-permute-start(bf16[2,32,3328]{2,1,0:T(8,128)(2,1)S(1)} %pad_maximum_fusion.9), channel_id=1, source_target_pairs={{0,8},{4,20},{8,0},{12,28},{16,24},{20,4},{24,16},{28,12},{1,9},{5... | collective-permute-start | bytes 1277960 | tf_op jit(solution)/shard_map/ppermute | solution.py:39
  119.0 20.6 %collective-permute-start.32 = (bf16[2,32,6656]{2,1,0:T(8,128)(2,1)S(1)}, bf16[2,32,6656]{2,1,0:T(8,128)(2,1)S(1)}, u32[]{:S(2)}, u32[]{:S(2)}) collective-permute-start(bf16[2,32,6656]{2,1,0:T(8,128)(2,1)S(1)} %pad_maximum_fusion.2.refs_0_), channel_id=1, source_target_pairs={{0,8},{4,20},{8,0},{12,28},{16,24},{20,4},{24,16},{28,12},{1,9},{5... | collective-permute-start | bytes 2555912 | tf_op jit(solution)/shard_map/ppermute | solution.py:39
  123.3 18.3 %collective-permute-start.33 = (bf16[2,32,6656]{2,1,0:T(8,128)(2,1)S(1)}, bf16[2,32,6656]{2,1,0:T(8,128)(2,1)S(1)}, u32[]{:S(2)}, u32[]{:S(2)}) collective-permute-start(bf16[2,32,6656]{2,1,0:T(8,128)(2,1)S(1)} %pad_maximum_fusion.2.refs_0_), channel_id=1, source_target_pairs={{0,16},{4,12},{8,24},{12,4},{16,0},{20,28},{24,8},{28,20},{1,17},{... | collective-permute-start | bytes 2555912 | tf_op jit(solution)/shard_map/ppermute | solution.py:39
  139.6 14.7 %collective-permute-start.34 = (bf16[2,32,6656]{2,1,0:T(8,128)(2,1)S(1)}, bf16[2,32,6656]{2,1,0:T(8,128)(2,1)S(1)}, u32[]{:S(2)}, u32[]{:S(2)}) collective-permute-start(bf16[2,32,6656]{2,1,0:T(8,128)(2,1)S(1)} %collective-permute-done.32.refs_1_), channel_id=1, source_target_pairs={{0,16},{4,12},{8,24},{12,4},{16,0},{20,28},{24,8},{28,20},{1,17},{... | collective-permute-start | bytes 2555912 | tf_op jit(solution)/shard_map/ppermute | solution.py:39
  139.6 15.0 %collective-permute-start.35 = (bf16[2,32,6656]{2,1,0:T(8,128)(2,1)S(1)}, bf16[2,32,6656]{2,1,0:T(8,128)(2,1)S(1)}, u32[]{:S(2)}, u32[]{:S(2)}) collective-permute-start(bf16[2,32,6656]{2,1,0:T(8,128)(2,1)S(1)} %pad_maximum_fusion.2.refs_0_), channel_id=1, source_target_pairs={{0,4},{4,0},{8,12},{12,8},{16,20},{20,16},{24,28},{28,24},{1,5},{5... | collective-permute-start | bytes 2555912 | tf_op jit(solution)/shard_map/ppermute | solution.py:34
  154.5 28.7 %collective-permute-start.41 = (bf16[64,2048]{1,0:T(8,128)(2,1)S(1)}, bf16[64,2048]{1,0:T(8,128)(2,1)S(1)}, u32[]{:S(2)}, u32[]{:S(2)}) collective-permute-start(bf16[64,2048]{1,0:T(8,128)(2,1)S(1)} %pad_maximum_fusion.12), channel_id=1, source_target_pairs={{0,3},{1,0},{2,1},{3,2},{4,7},{5,4},{6,5},{7,6},{8,11},{9,8},{10,9... | collective-permute-start | bytes 786440 | tf_op jit(solution)/shard_map/ppermute | solution.py:45
  154.6 31.4 %collective-permute-start.40 = (bf16[64,2048]{1,0:T(8,128)(2,1)S(1)}, bf16[64,2048]{1,0:T(8,128)(2,1)S(1)}, u32[]{:S(2)}, u32[]{:S(2)}) collective-permute-start(bf16[64,2048]{1,0:T(8,128)(2,1)S(1)} %pad_maximum_fusion.11), channel_id=1, source_target_pairs={{0,2},{1,3},{2,0},{3,1},{4,6},{5,7},{6,4},{7,5},{8,10},{9,11},{10,... | collective-permute-start | bytes 786440 | tf_op jit(solution)/shard_map/ppermute | solution.py:45
  154.8 31.2 %collective-permute-start.39 = (bf16[64,2048]{1,0:T(8,128)(2,1)S(1)}, bf16[64,2048]{1,0:T(8,128)(2,1)S(1)}, u32[]{:S(2)}, u32[]{:S(2)}) collective-permute-start(bf16[64,2048]{1,0:T(8,128)(2,1)S(1)} %pad_maximum_fusion.10), channel_id=1, source_target_pairs={{0,1},{1,2},{2,3},{3,0},{4,5},{5,6},{6,7},{7,4},{8,9},{9,10},{10,1... | collective-permute-start | bytes 786440 | tf_op jit(solution)/shard_map/ppermute | solution.py:45
  181.6 21.1 %collective-permute-start.43 = (bf16[64,2048]{1,0:T(8,128)(2,1)S(1)}, bf16[64,2048]{1,0:T(8,128)(2,1)S(1)}, u32[]{:S(2)}, u32[]{:S(2)}) collective-permute-start(bf16[64,2048]{1,0:T(8,128)(2,1)S(1)} %get-tuple-element.93), channel_id=1, source_target_pairs={{0,2},{1,3},{2,0},{3,1},{4,6},{5,7},{6,4},{7,5},{8,10},{9,11},{10,... | collective-permute-start | bytes 786440 | tf_op jit(solution)/shard_map/ppermute | solution.py:45
  183.1 19.6 %collective-permute-start.44 = (bf16[64,2048]{1,0:T(8,128)(2,1)S(1)}, bf16[64,2048]{1,0:T(8,128)(2,1)S(1)}, u32[]{:S(2)}, u32[]{:S(2)}) collective-permute-start(bf16[64,2048]{1,0:T(8,128)(2,1)S(1)} %get-tuple-element.94), channel_id=1, source_target_pairs={{0,3},{1,0},{2,1},{3,2},{4,7},{5,4},{6,5},{7,6},{8,11},{9,8},{10,9... | collective-permute-start | bytes 786440 | tf_op jit(solution)/shard_map/ppermute | solution.py:45
  (24 other events, 170.0 us)

commit v5 on v4

--- a/solution.py
+++ b/solution.py
@@ -147,7 +147,7 @@
             pltpu.VMEM((SLOTS, block, width), jnp.bfloat16),
             pltpu.SemaphoreType.DMA((SLOTS,)),
         ],
-        compiler_params=pltpu.CompilerParams(vmem_limit_bytes=39 * MIB),
+        compiler_params=pltpu.CompilerParams(vmem_limit_bytes=30 * MIB),
         cost_estimate=pl.CostEstimate(flops=HINT, bytes_accessed=HINT, transcendentals=0),
     )(*pieces, weight)
 
@@ -360,19 +360,21 @@
     chain.end(*known[1:])
     first = multiply(near, [0])
     known = spread(known)
+    first += multiply(near, [1])
     chain.last += known[1:]
-    first += multiply(near, [1])
     known = cross(known)
     for side in first:
         side.pair()
     chain.last += known[1:]
     for _ in bits[1:]:
         next_sums(first)
-    second = multiply(far, [0])
     first = [own_hidden(first).astype(jnp.bfloat16)]
     chain.end(first[0])
-    for _ in bits:
+    for _ in bits[1:]:
         first = spread(first)
+    second = multiply(far, [0])
+    chain.last += first[1:]
+    first = spread(first)
     second += multiply(far, [1])
     for side in second:
         side.pair()

time: 206 us -> 214 us (1.039)
  waiting for transfers between devices: 77.8 us -> 87.5 us
    ppermute x17, waiting for transfers between devices: 40.9 us -> 53.8 us  [exchange(): lax.ppermute(value, 'row', [(i, i ^ 2 << (top - j if i & 1 else j)) for i...]
    ppermute x12, waiting for transfers between devices: 33.6 us -> 28.3 us  [turn(): lax.ppermute(value, 'col', [(i, (i + distance) % size) for i in range(siz...]
  transfers between devices with their start and end apart: 45 -> 45, of which waited for: 19 -> 22; matrix products, arithmetic and copies ran while one was open for 1% -> 1% of each run, Pallas kernels for 39% -> 34%
where the time goes in v5:
time: 214 us; the launch traced here: 211 us
  waiting for transfers between devices  87.5 us (41%)
  Pallas kernels  79.2 us (37%)
  starting transfers between devices  39.6 us (19%)
  other arithmetic  2.33 us (1%)
  local copies, waits for them, and re-layouts  2.25 us (1%)
    ppermute x17, waiting for transfers between devices, exchange(): lax.ppermute(value, 'row', [(i, i ^ 2 << (top - j if i & 1 else j)) for i...  53.8 us
    pallas_call x3, Pallas kernels, input_partial(): pl.pallas_call(functools.partial(input_kernel, rows, cols, start, block),...  48.8 us
    pallas_call x4, Pallas kernels, hidden_partial(): pl.pallas_call(functools.partial(hidden_kernel, rows, cols, starts, block...  30.4 us
    ppermute x12, waiting for transfers between devices, turn(): lax.ppermute(value, 'col', [(i, (i + distance) % size) for i in range(siz...  28.3 us
    ppermute x17, starting transfers between devices, exchange(): lax.ppermute(value, 'row', [(i, i ^ 2 << (top - j if i & 1 else j)) for i...  20.6 us
    ppermute x12, starting transfers between devices, turn(): lax.ppermute(value, 'col', [(i, (i + distance) % size) for i in range(siz...  15.1 us
    ppermute x16, waiting for transfers between devices, swap(): return lax.ppermute(value, 'row', [(i, i ^ 1) for i in range(size)])  5.32 us
  transfers between devices with their start and end apart: 45, of which 22 were waited for; matrix products, arithmetic and copies ran while one was open for 1% of the time, Pallas kernels for 34%

profile of v5, /device:TPU:0, one launch (start us, length us, event | category | flops | bytes accessed | tf_op | source)
XLA Modules:
  0.0 211.3 jit_solution(12262270965105772148)
XLA Ops:
  1.3 3.0 %collective-permute-start = (bf16[2,32,6656]{2,1,0:T(8,128)(2,1)S(1)}, bf16[2,32,6656]{2,1,0:T(8,128)(2,1)S(1)}, u32[]{:S(2)}, u32[]{:S(2)}) collective-permute-start(bf16[2,32,6656]{2,1,0:T(8,128)(2,1)S(1)} %pad_maximum_fusion.refs_8_), channel_id=1, source_target_pairs={{0,8},{4,20},{8,0},{12,28},{16,24},{20,4},{24,16},{28,12},{1,9},{5... | collective-permute-start | bytes 2555912 | tf_op jit(solution)/shard_map/ppermute | solution.py:39
  4.4 3.7 %collective-permute-start.3 = (bf16[64,2048]{1,0:T(8,128)(2,1)S(1)}, bf16[64,2048]{1,0:T(8,128)(2,1)S(1)}, u32[]{:S(2)}, u32[]{:S(2)}) collective-permute-start(bf16[64,2048]{1,0:T(8,128)(2,1)S(1)} %bitcast.31), channel_id=1, source_target_pairs={{0,3},{1,0},{2,1},{3,2},{4,7},{5,4},{6,5},{7,6},{8,11},{9,8},{10,9... | collective-permute-start | bytes 786440 | tf_op jit(solution)/shard_map/ppermute | solution.py:45
  10.6 9.0 %collective-permute-done.refs_9_ = bf16[2,32,6656]{2,1,0:T(8,128)(2,1)S(1)} collective-permute-done((bf16[2,32,6656]{2,1,0:T(8,128)(2,1)S(1)}, bf16[2,32,6656]{2,1,0:T(8,128)(2,1)S(1)}, u32[]{:S(2)}, u32[]{:S(2)}) %collective-permute-start) | collective-permute-done | bytes 852000 | tf_op jit(solution)/shard_map/ppermute | solution.py:39
  19.6 3.5 %collective-permute-start.6 = (bf16[2,32,6656]{2,1,0:T(8,128)(2,1)S(1)}, bf16[2,32,6656]{2,1,0:T(8,128)(2,1)S(1)}, u32[]{:S(2)}, u32[]{:S(2)}) collective-permute-start(bf16[2,32,6656]{2,1,0:T(8,128)(2,1)S(1)} %collective-permute-done.refs_9_), channel_id=1, source_target_pairs={{0,16},{4,12},{8,24},{12,4},{16,0},{20,28},{24,8},{28,20},{1,17},{... | collective-permute-start | bytes 2555912 | tf_op jit(solution)/shard_map/ppermute | solution.py:39
  23.2 7.0 %collective-permute-done.2.refs_2_ = bf16[64,2048]{1,0:T(8,128)(2,1)S(1)} collective-permute-done((bf16[64,2048]{1,0:T(8,128)(2,1)S(1)}, bf16[64,2048]{1,0:T(8,128)(2,1)S(1)}, u32[]{:S(2)}, u32[]{:S(2)}) %collective-permute-start.2) | collective-permute-done | bytes 262176 | tf_op jit(solution)/shard_map/ppermute | solution.py:45
  30.1 7.6 %shard_map.64 = (bf16[4,32,3328]{2,1,0:T(8,128)(2,1)S(1)}, f32[4,32,3328]{2,1,0:T(8,128)S(1)}) custom-call(bf16[64,2048]{1,0:T(8,128)(2,1)S(1)} %bitcast.34, bf16[64,2048]{1,0:T(8,128)(2,1)S(1)} %collective-permute-done.1.refs_1_, bf16[64,2048]{1,0:T(8,128)(2,1)S(1)} %collective-permute-done.2.refs_2_, bf16[64,2048]{1,0:T(8,128)(2,1)S(1)} %collective-permute-done.3.refs_3_, ...), custom_call_target="tpu_custom_call" | custom-call | flops 1024 | bytes 1024 | tf_op jit(solution)/shard_map/pallas_call | solution.py:136
  38.3 7.6 %shard_map.65 = (bf16[4,32,3328]{2,1,0:T(8,128)(2,1)S(1)}, f32[4,32,3328]{2,1,0:T(8,128)S(1)}) custom-call(bf16[64,2048]{1,0:T(8,128)(2,1)S(1)} %bitcast.35, bf16[64,2048]{1,0:T(8,128)(2,1)S(1)} %collective-permute-done.1.refs_1_, bf16[64,2048]{1,0:T(8,128)(2,1)S(1)} %collective-permute-done.2.refs_2_, bf16[64,2048]{1,0:T(8,128)(2,1)S(1)} %collective-permute-done.3.refs_3_, ...), custom_call_target="tpu_custom_call" | custom-call | flops 1024 | bytes 1024 | tf_op jit(solution)/shard_map/pallas_call | solution.py:136
  50.8 2.8 %collective-permute-start.17 = (bf16[64,2048]{1,0:T(8,128)(2,1)S(1)}, bf16[64,2048]{1,0:T(8,128)(2,1)S(1)}, u32[]{:S(2)}, u32[]{:S(2)}) collective-permute-start(bf16[64,2048]{1,0:T(8,128)(2,1)S(1)} %bitcast.27), channel_id=1, source_target_pairs={{0,2},{1,3},{2,0},{3,1},{4,6},{5,7},{6,4},{7,5},{8,10},{9,11},{10,... | collective-permute-start | bytes 786440 | tf_op jit(solution)/shard_map/ppermute | solution.py:45
  57.2 7.2 %collective-permute-done.14 = bf16[2,32,3328]{2,1,0:T(8,128)(2,1)S(1)} collective-permute-done((bf16[2,32,3328]{2,1,0:T(8,128)(2,1)S(1)}, bf16[2,32,3328]{2,1,0:T(8,128)(2,1)S(1)}, u32[]{:S(2)}, u32[]{:S(2)}) %collective-permute-start.14) | collective-permute-done | bytes 426016 | tf_op jit(solution)/shard_map/ppermute | solution.py:39
  66.1 4.2 %collective-permute-done.15 = bf16[1,32,3328]{2,1,0:T(8,128)(2,1)S(1)} collective-permute-done((bf16[1,32,3328]{2,1,0:T(8,128)(2,1)S(1)}, bf16[1,32,3328]{2,1,0:T(8,128)(2,1)S(1)}, u32[]{:S(2)}, u32[]{:S(2)}) %collective-permute-start.15) | collective-permute-done | bytes 213024 | tf_op jit(solution)/shard_map/ppermute | solution.py:39
  70.5 5.0 %collective-permute-done.17.refs_2_ = bf16[64,2048]{1,0:T(8,128)(2,1)S(1)} collective-permute-done((bf16[64,2048]{1,0:T(8,128)(2,1)S(1)}, bf16[64,2048]{1,0:T(8,128)(2,1)S(1)}, u32[]{:S(2)}, u32[]{:S(2)}) %collective-permute-start.17) | collective-permute-done | bytes 262176 | tf_op jit(solution)/shard_map/ppermute | solution.py:45
  75.5 7.6 %shard_map.66 = (bf16[4,32,3328]{2,1,0:T(8,128)(2,1)S(1)}, f32[4,32,3328]{2,1,0:T(8,128)S(1)}) custom-call(bf16[64,2048]{1,0:T(8,128)(2,1)S(1)} %bitcast.29, bf16[64,2048]{1,0:T(8,128)(2,1)S(1)} %collective-permute-done.16.refs_1_, bf16[64,2048]{1,0:T(8,128)(2,1)S(1)} %collective-permute-done.17.refs_2_, ...), custom_call_target="tpu_custom_call" | custom-call | flops 1024 | bytes 1024 | tf_op jit(solution)/shard_map/pallas_call | solution.py:136
  85.1 10.5 %collective-permute-done.20.refs_1_ = bf16[32,6656]{1,0:T(8,128)(2,1)S(1)} collective-permute-done((bf16[32,6656]{1,0:T(8,128)(2,1)S(1)}, bf16[32,6656]{1,0:T(8,128)(2,1)S(1)}, u32[]{:S(2)}, u32[]{:S(2)}) %collective-permute-start.20) | collective-permute-done | bytes 426016 | tf_op jit(solution)/shard_map/ppermute | solution.py:39
  95.6 7.6 %shard_map.67 = (bf16[4,32,3328]{2,1,0:T(8,128)(2,1)S(1)}, f32[4,32,3328]{2,1,0:T(8,128)S(1)}) custom-call(bf16[64,2048]{1,0:T(8,128)(2,1)S(1)} %bitcast.30, bf16[64,2048]{1,0:T(8,128)(2,1)S(1)} %collective-permute-done.16.refs_1_, bf16[64,2048]{1,0:T(8,128)(2,1)S(1)} %collective-permute-done.17.refs_2_, ...), custom_call_target="tpu_custom_call" | custom-call | flops 1024 | bytes 1024 | tf_op jit(solution)/shard_map/pallas_call | solution.py:136
  107.4 8.1 %collective-permute-done.21 = bf16[2,32,3328]{2,1,0:T(8,128)(2,1)S(1)} collective-permute-done((bf16[2,32,3328]{2,1,0:T(8,128)(2,1)S(1)}, bf16[2,32,3328]{2,1,0:T(8,128)(2,1)S(1)}, u32[]{:S(2)}, u32[]{:S(2)}) %collective-permute-start.21) | collective-permute-done | bytes 426016 | tf_op jit(solution)/shard_map/ppermute | solution.py:39
  115.8 5.4 %collective-permute-done.24 = bf16[2,32,3328]{2,1,0:T(8,128)(2,1)S(1)} collective-permute-done((bf16[2,32,3328]{2,1,0:T(8,128)(2,1)S(1)}, bf16[2,32,3328]{2,1,0:T(8,128)(2,1)S(1)}, u32[]{:S(2)}, u32[]{:S(2)}) %collective-permute-start.24) | collective-permute-done | bytes 426016 | tf_op jit(solution)/shard_map/ppermute | solution.py:39
  123.0 4.2 %collective-permute-done.27 = bf16[1,32,3328]{2,1,0:T(8,128)(2,1)S(1)} collective-permute-done((bf16[1,32,3328]{2,1,0:T(8,128)(2,1)S(1)}, bf16[1,32,3328]{2,1,0:T(8,128)(2,1)S(1)}, u32[]{:S(2)}, u32[]{:S(2)}) %collective-permute-start.27) | collective-permute-done | bytes 213024 | tf_op jit(solution)/shard_map/ppermute | solution.py:39
  132.9 13.4 %shard_map.68 = (f32[64,1024]{1,0:T(8,128)S(1)}, bf16[64,1024]{1,0:T(8,128)(2,1)S(1)}, bf16[64,1024]{1,0:T(8,128)(2,1)S(1)}, bf16[64,1024]{1,0:T(8,128)(2,1)S(1)...) custom-call(bf16[32,6656]{1,0:T(8,128)(2,1)S(1)} %pad_maximum_fusion.7.refs_0_, ...), custom_call_target="tpu_custom_call" | custom-call | flops 1024 | bytes 1024 | tf_op jit(solution)/shard_map/pallas_call | solution.py:241
  149.5 12.1 %shard_map.69 = (f32[64,1024]{1,0:T(8,128)S(1)}, bf16[64,1024]{1,0:T(8,128)(2,1)S(1)}, bf16[64,1024]{1,0:T(8,128)(2,1)S(1)}, bf16[64,1024]{1,0:T(8,128)(2,1)S(1)}) custom-call(bf16[256,6656]{1,0:T(8,128)(2,1)S(1)} %get-tuple-element.78.refs_0_, bf16[256,6656]{1,0:T(8,128)(2,1)S(1)} %get-tuple-element.79.refs_1_, bf16[2048,6656]{1,0:T(8,128)(2,1)} %refs_8_.1, ...), custom_call_target="tpu_custom_call" | custom-call | flops 1024 | bytes 1024 | tf_op jit(solution)/shard_map/pallas_call | solution.py:241
  162.6 2.0 collective-permute-start.39
  165.3 23.3 %shard_map.70 = (f32[64,2048]{1,0:T(8,128)S(1)}, bf16[64,2048]{1,0:T(8,128)(2,1)S(1)}, bf16[64,2048]{1,0:T(8,128)(2,1)S(1)}, bf16[64,2048]{1,0:T(8,128)(2,1)S(1)...) custom-call(bf16[2,32,6656]{2,1,0:T(8,128)(2,1)S(1)} %pad_maximum_fusion.2.refs_0_, ...), custom_call_target="tpu_custom_call" | custom-call | flops 1024 | bytes 1024 | tf_op jit(solution)/shard_map/pallas_call | solution.py:241
  190.9 2.8 %collective-permute-start.44 = (bf16[64,2048]{1,0:T(8,128)(2,1)S(1)}, bf16[64,2048]{1,0:T(8,128)(2,1)S(1)}, u32[]{:S(2)}, u32[]{:S(2)}) collective-permute-start(bf16[64,2048]{1,0:T(8,128)(2,1)S(1)} %get-tuple-element.94), channel_id=1, source_target_pairs={{0,3},{1,0},{2,1},{3,2},{4,7},{5,4},{6,5},{7,6},{8,11},{9,8},{10,9... | collective-permute-start | bytes 786440 | tf_op jit(solution)/shard_map/ppermute | solution.py:45
  193.9 5.9 %collective-permute-done.42 = bf16[64,2048]{1,0:T(8,128)(2,1)S(1)} collective-permute-done((bf16[64,2048]{1,0:T(8,128)(2,1)S(1)}, bf16[64,2048]{1,0:T(8,128)(2,1)S(1)}, u32[]{:S(2)}, u32[]{:S(2)}) %collective-permute-start.42) | collective-permute-done | bytes 262176 | tf_op jit(solution)/shard_map/ppermute | solution.py:45
  199.8 10.5 %collective-permute-done.43 = bf16[64,2048]{1,0:T(8,128)(2,1)S(1)} collective-permute-done((bf16[64,2048]{1,0:T(8,128)(2,1)S(1)}, bf16[64,2048]{1,0:T(8,128)(2,1)S(1)}, u32[]{:S(2)}, u32[]{:S(2)}) %collective-permute-start.43) | collective-permute-done | bytes 262176 | tf_op jit(solution)/shard_map/ppermute | solution.py:45
  (113 shorter events, 36.8 us)
Async XLA Ops:
  1.3 18.3 %collective-permute-start = (bf16[2,32,6656]{2,1,0:T(8,128)(2,1)S(1)}, bf16[2,32,6656]{2,1,0:T(8,128)(2,1)S(1)}, u32[]{:S(2)}, u32[]{:S(2)}) collective-permute-start(bf16[2,32,6656]{2,1,0:T(8,128)(2,1)S(1)} %pad_maximum_fusion.refs_8_), channel_id=1, source_target_pairs={{0,8},{4,20},{8,0},{12,28},{16,24},{20,4},{24,16},{28,12},{1,9},{5... | collective-permute-start | bytes 2555912 | tf_op jit(solution)/shard_map/ppermute | solution.py:39
  4.4 18.8 %collective-permute-start.3 = (bf16[64,2048]{1,0:T(8,128)(2,1)S(1)}, bf16[64,2048]{1,0:T(8,128)(2,1)S(1)}, u32[]{:S(2)}, u32[]{:S(2)}) collective-permute-start(bf16[64,2048]{1,0:T(8,128)(2,1)S(1)} %bitcast.31), channel_id=1, source_target_pairs={{0,3},{1,0},{2,1},{3,2},{4,7},{5,4},{6,5},{7,6},{8,11},{9,8},{10,9... | collective-permute-start | bytes 786440 | tf_op jit(solution)/shard_map/ppermute | solution.py:45
  8.1 22.1 %collective-permute-start.2 = (bf16[64,2048]{1,0:T(8,128)(2,1)S(1)}, bf16[64,2048]{1,0:T(8,128)(2,1)S(1)}, u32[]{:S(2)}, u32[]{:S(2)}) collective-permute-start(bf16[64,2048]{1,0:T(8,128)(2,1)S(1)} %bitcast.32), channel_id=1, source_target_pairs={{0,2},{1,3},{2,0},{3,1},{4,6},{5,7},{6,4},{7,5},{8,10},{9,11},{10,... | collective-permute-start | bytes 786440 | tf_op jit(solution)/shard_map/ppermute | solution.py:45
  8.1 22.1 %collective-permute-start.1 = (bf16[64,2048]{1,0:T(8,128)(2,1)S(1)}, bf16[64,2048]{1,0:T(8,128)(2,1)S(1)}, u32[]{:S(2)}, u32[]{:S(2)}) collective-permute-start(bf16[64,2048]{1,0:T(8,128)(2,1)S(1)} %bitcast.33), channel_id=1, source_target_pairs={{0,1},{1,2},{2,3},{3,0},{4,5},{5,6},{6,7},{7,4},{8,9},{9,10},{10,1... | collective-permute-start | bytes 786440 | tf_op jit(solution)/shard_map/ppermute | solution.py:45
  9.1 37.0 %collective-permute-start.5 = (bf16[2,32,6656]{2,1,0:T(8,128)(2,1)S(1)}, bf16[2,32,6656]{2,1,0:T(8,128)(2,1)S(1)}, u32[]{:S(2)}, u32[]{:S(2)}) collective-permute-start(bf16[2,32,6656]{2,1,0:T(8,128)(2,1)S(1)} %pad_maximum_fusion.refs_8_), channel_id=1, source_target_pairs={{0,16},{4,12},{8,24},{12,4},{16,0},{20,28},{24,8},{28,20},{1,17},{... | collective-permute-start | bytes 2555912 | tf_op jit(solution)/shard_map/ppermute | solution.py:39
  19.6 26.9 %collective-permute-start.6 = (bf16[2,32,6656]{2,1,0:T(8,128)(2,1)S(1)}, bf16[2,32,6656]{2,1,0:T(8,128)(2,1)S(1)}, u32[]{:S(2)}, u32[]{:S(2)}) collective-permute-start(bf16[2,32,6656]{2,1,0:T(8,128)(2,1)S(1)} %collective-permute-done.refs_9_), channel_id=1, source_target_pairs={{0,16},{4,12},{8,24},{12,4},{16,0},{20,28},{24,8},{28,20},{1,17},{... | collective-permute-start | bytes 2555912 | tf_op jit(solution)/shard_map/ppermute | solution.py:39
  48.8 21.6 %collective-permute-start.18 = (bf16[64,2048]{1,0:T(8,128)(2,1)S(1)}, bf16[64,2048]{1,0:T(8,128)(2,1)S(1)}, u32[]{:S(2)}, u32[]{:S(2)}) collective-permute-start(bf16[64,2048]{1,0:T(8,128)(2,1)S(1)} %bitcast.26), channel_id=1, source_target_pairs={{0,3},{1,0},{2,1},{3,2},{4,7},{5,4},{6,5},{7,6},{8,11},{9,8},{10,9... | collective-permute-start | bytes 786440 | tf_op jit(solution)/shard_map/ppermute | solution.py:45
  50.8 24.7 %collective-permute-start.17 = (bf16[64,2048]{1,0:T(8,128)(2,1)S(1)}, bf16[64,2048]{1,0:T(8,128)(2,1)S(1)}, u32[]{:S(2)}, u32[]{:S(2)}) collective-permute-start(bf16[64,2048]{1,0:T(8,128)(2,1)S(1)} %bitcast.27), channel_id=1, source_target_pairs={{0,2},{1,3},{2,0},{3,1},{4,6},{5,7},{6,4},{7,5},{8,10},{9,11},{10,... | collective-permute-start | bytes 786440 | tf_op jit(solution)/shard_map/ppermute | solution.py:45
  53.6 21.9 %collective-permute-start.16 = (bf16[64,2048]{1,0:T(8,128)(2,1)S(1)}, bf16[64,2048]{1,0:T(8,128)(2,1)S(1)}, u32[]{:S(2)}, u32[]{:S(2)}) collective-permute-start(bf16[64,2048]{1,0:T(8,128)(2,1)S(1)} %bitcast.28), channel_id=1, source_target_pairs={{0,1},{1,2},{2,3},{3,0},{4,5},{5,6},{6,7},{7,4},{8,9},{9,10},{10,1... | collective-permute-start | bytes 786440 | tf_op jit(solution)/shard_map/ppermute | solution.py:45
  83.1 20.4 %collective-permute-start.19 = (bf16[4,32,3328]{2,1,0:T(8,128)(2,1)S(1)}, bf16[4,32,3328]{2,1,0:T(8,128)(2,1)S(1)}, u32[]{:S(2)}, u32[]{:S(2)}) collective-permute-start(bf16[4,32,3328]{2,1,0:T(8,128)(2,1)S(1)} %get-tuple-element.65), channel_id=1, source_target_pairs={{0,4},{4,0},{8,12},{12,8},{16,20},{20,16},{24,28},{28,24},{1,5},{5... | collective-permute-start | bytes 2555912 | tf_op jit(solution)/shard_map/ppermute | solution.py:34
  83.2 12.4 %collective-permute-start.20 = (bf16[32,6656]{1,0:T(8,128)(2,1)S(1)}, bf16[32,6656]{1,0:T(8,128)(2,1)S(1)}, u32[]{:S(2)}, u32[]{:S(2)}) collective-permute-start(bf16[32,6656]{1,0:T(8,128)(2,1)S(1)} %pad_maximum_fusion.7.refs_0_), channel_id=1, source_target_pairs={{0,8},{4,20},{8,0},{12,28},{16,24},{20,4},{24,16},{28,12},{1,9},{5... | collective-permute-start | bytes 1277960 | tf_op jit(solution)/shard_map/ppermute | solution.py:39
  84.6 36.8 %collective-permute-start.25 = (bf16[32,6656]{1,0:T(8,128)(2,1)S(1)}, bf16[32,6656]{1,0:T(8,128)(2,1)S(1)}, u32[]{:S(2)}, u32[]{:S(2)}) collective-permute-start(bf16[32,6656]{1,0:T(8,128)(2,1)S(1)} %pad_maximum_fusion.7.refs_0_), channel_id=1, source_target_pairs={{0,16},{4,12},{8,24},{12,4},{16,0},{20,28},{24,8},{28,20},{1,17},{... | collective-permute-start | bytes 1277960 | tf_op jit(solution)/shard_map/ppermute | solution.py:39
  103.3 18.2 %collective-permute-start.26 = (bf16[32,6656]{1,0:T(8,128)(2,1)S(1)}, bf16[32,6656]{1,0:T(8,128)(2,1)S(1)}, u32[]{:S(2)}, u32[]{:S(2)}) collective-permute-start(bf16[32,6656]{1,0:T(8,128)(2,1)S(1)} %collective-permute-done.20.refs_1_), channel_id=1, source_target_pairs={{0,16},{4,12},{8,24},{12,4},{16,0},{20,28},{24,8},{28,20},{1,17},{... | collective-permute-start | bytes 1277960 | tf_op jit(solution)/shard_map/ppermute | solution.py:39
  105.9 15.3 %collective-permute-start.24 = (bf16[2,32,3328]{2,1,0:T(8,128)(2,1)S(1)}, bf16[2,32,3328]{2,1,0:T(8,128)(2,1)S(1)}, u32[]{:S(2)}, u32[]{:S(2)}) collective-permute-start(bf16[2,32,3328]{2,1,0:T(8,128)(2,1)S(1)} %pad_maximum_fusion.9), channel_id=1, source_target_pairs={{0,8},{4,20},{8,0},{12,28},{16,24},{20,4},{24,16},{28,12},{1,9},{5... | collective-permute-start | bytes 1277960 | tf_op jit(solution)/shard_map/ppermute | solution.py:39
  127.8 19.5 %collective-permute-start.32 = (bf16[2,32,6656]{2,1,0:T(8,128)(2,1)S(1)}, bf16[2,32,6656]{2,1,0:T(8,128)(2,1)S(1)}, u32[]{:S(2)}, u32[]{:S(2)}) collective-permute-start(bf16[2,32,6656]{2,1,0:T(8,128)(2,1)S(1)} %pad_maximum_fusion.2.refs_0_), channel_id=1, source_target_pairs={{0,8},{4,20},{8,0},{12,28},{16,24},{20,4},{24,16},{28,12},{1,9},{5... | collective-permute-start | bytes 2555912 | tf_op jit(solution)/shard_map/ppermute | solution.py:39
  131.0 17.7 %collective-permute-start.33 = (bf16[2,32,6656]{2,1,0:T(8,128)(2,1)S(1)}, bf16[2,32,6656]{2,1,0:T(8,128)(2,1)S(1)}, u32[]{:S(2)}, u32[]{:S(2)}) collective-permute-start(bf16[2,32,6656]{2,1,0:T(8,128)(2,1)S(1)} %pad_maximum_fusion.2.refs_0_), channel_id=1, source_target_pairs={{0,16},{4,12},{8,24},{12,4},{16,0},{20,28},{24,8},{28,20},{1,17},{... | collective-permute-start | bytes 2555912 | tf_op jit(solution)/shard_map/ppermute | solution.py:39
  147.2 14.5 %collective-permute-start.34 = (bf16[2,32,6656]{2,1,0:T(8,128)(2,1)S(1)}, bf16[2,32,6656]{2,1,0:T(8,128)(2,1)S(1)}, u32[]{:S(2)}, u32[]{:S(2)}) collective-permute-start(bf16[2,32,6656]{2,1,0:T(8,128)(2,1)S(1)} %collective-permute-done.32.refs_1_), channel_id=1, source_target_pairs={{0,16},{4,12},{8,24},{12,4},{16,0},{20,28},{24,8},{28,20},{1,17},{... | collective-permute-start | bytes 2555912 | tf_op jit(solution)/shard_map/ppermute | solution.py:39
  147.3 15.0 %collective-permute-start.35 = (bf16[2,32,6656]{2,1,0:T(8,128)(2,1)S(1)}, bf16[2,32,6656]{2,1,0:T(8,128)(2,1)S(1)}, u32[]{:S(2)}, u32[]{:S(2)}) collective-permute-start(bf16[2,32,6656]{2,1,0:T(8,128)(2,1)S(1)} %pad_maximum_fusion.2.refs_0_), channel_id=1, source_target_pairs={{0,4},{4,0},{8,12},{12,8},{16,20},{20,16},{24,28},{28,24},{1,5},{5... | collective-permute-start | bytes 2555912 | tf_op jit(solution)/shard_map/ppermute | solution.py:34
  148.7 13.9 %collective-permute-start.37 = (bf16[2,32,6656]{2,1,0:T(8,128)(2,1)S(1)}, bf16[2,32,6656]{2,1,0:T(8,128)(2,1)S(1)}, u32[]{:S(2)}, u32[]{:S(2)}) collective-permute-start(bf16[2,32,6656]{2,1,0:T(8,128)(2,1)S(1)} %collective-permute-done.33.refs_2_), channel_id=1, source_target_pairs={{0,4},{4,0},{8,12},{12,8},{16,20},{20,16},{24,28},{28,24},{1,5},{5... | collective-permute-start | bytes 2555912 | tf_op jit(solution)/shard_map/ppermute | solution.py:34
  162.2 28.7 %collective-permute-start.41 = (bf16[64,2048]{1,0:T(8,128)(2,1)S(1)}, bf16[64,2048]{1,0:T(8,128)(2,1)S(1)}, u32[]{:S(2)}, u32[]{:S(2)}) collective-permute-start(bf16[64,2048]{1,0:T(8,128)(2,1)S(1)} %pad_maximum_fusion.12), channel_id=1, source_target_pairs={{0,3},{1,0},{2,1},{3,2},{4,7},{5,4},{6,5},{7,6},{8,11},{9,8},{10,9... | collective-permute-start | bytes 786440 | tf_op jit(solution)/shard_map/ppermute | solution.py:45
  162.4 31.4 %collective-permute-start.40 = (bf16[64,2048]{1,0:T(8,128)(2,1)S(1)}, bf16[64,2048]{1,0:T(8,128)(2,1)S(1)}, u32[]{:S(2)}, u32[]{:S(2)}) collective-permute-start(bf16[64,2048]{1,0:T(8,128)(2,1)S(1)} %pad_maximum_fusion.11), channel_id=1, source_target_pairs={{0,2},{1,3},{2,0},{3,1},{4,6},{5,7},{6,4},{7,5},{8,10},{9,11},{10,... | collective-permute-start | bytes 786440 | tf_op jit(solution)/shard_map/ppermute | solution.py:45
  162.6 31.1 %collective-permute-start.39 = (bf16[64,2048]{1,0:T(8,128)(2,1)S(1)}, bf16[64,2048]{1,0:T(8,128)(2,1)S(1)}, u32[]{:S(2)}, u32[]{:S(2)}) collective-permute-start(bf16[64,2048]{1,0:T(8,128)(2,1)S(1)} %pad_maximum_fusion.10), channel_id=1, source_target_pairs={{0,1},{1,2},{2,3},{3,0},{4,5},{5,6},{6,7},{7,4},{8,9},{9,10},{10,1... | collective-permute-start | bytes 786440 | tf_op jit(solution)/shard_map/ppermute | solution.py:45
  189.4 20.9 %collective-permute-start.43 = (bf16[64,2048]{1,0:T(8,128)(2,1)S(1)}, bf16[64,2048]{1,0:T(8,128)(2,1)S(1)}, u32[]{:S(2)}, u32[]{:S(2)}) collective-permute-start(bf16[64,2048]{1,0:T(8,128)(2,1)S(1)} %get-tuple-element.93), channel_id=1, source_target_pairs={{0,2},{1,3},{2,0},{3,1},{4,6},{5,7},{6,4},{7,5},{8,10},{9,11},{10,... | collective-permute-start | bytes 786440 | tf_op jit(solution)/shard_map/ppermute | solution.py:45
  190.9 19.4 %collective-permute-start.44 = (bf16[64,2048]{1,0:T(8,128)(2,1)S(1)}, bf16[64,2048]{1,0:T(8,128)(2,1)S(1)}, u32[]{:S(2)}, u32[]{:S(2)}) collective-permute-start(bf16[64,2048]{1,0:T(8,128)(2,1)S(1)} %get-tuple-element.94), channel_id=1, source_target_pairs={{0,3},{1,0},{2,1},{3,2},{4,7},{5,4},{6,5},{7,6},{8,11},{9,8},{10,9... | collective-permute-start | bytes 786440 | tf_op jit(solution)/shard_map/ppermute | solution.py:45
  (24 other events, 146.3 us)
